TPU v7x, 32 devices: a whole 2x2x4 slice. The times are simulated.
32 devices in a mesh: rows: 8 (over z, x), cols: 4 (over y, core).
Axes of the slice: x: 2, y: 2, z: 4, core: 2. Of those that a mesh axis runs over, the one named last changes fastest.
Arguments:
- warped: bfloat16 [64, 256, 2048], P(None, 'rows', 'cols'), may hold values from -6 to 6
- cotangent: bfloat16 [64, 256, 2048], P(None, 'rows', 'cols'), may hold values from -6 to 6
- w_first: bfloat16 [64, 64, 3, 3], replicated, may hold values from -0.25 to 0.25
- b_first: float32 [64], replicated, may hold values from -4 to 4
- w_second: bfloat16 [64, 64, 3, 3], replicated, may hold values from -0.25 to 0.25
- source_tile: int32 [16, 128], P('rows', 'cols'), may hold values from 0 to 31, as said below
- source_block: int32 [16, 128], P('rows', 'cols'), may hold values from 0 to 63
Outputs:
- frame_grad: float32 [64, 256, 2048], P(None, 'rows', 'cols')
- w_first_grad: float32 [64, 64, 3, 3], replicated
- b_first_grad: float32 [64], replicated
- w_second_grad: float32 [64, 64, 3, 3], replicated
- b_second_grad: float32 [64], replicated
Inputs may be any that keep to these rules, and one draw needn't show every extreme that they name: `source_tile`: among the blocks of one tile, at most 2 name the same source tile; in every draw one source tile is named exactly 2 times by the blocks of every tile.
All inputs are finite; a program needn't handle non-finite values.
Results may differ from a plain program's by a relative error of at most 0.005.
Values may be sent and summed in bfloat16 or wider, within the bound.
No kernel may reach another device: no remote copies, remote signals or barrier semaphores. Data moves between devices by JAX's collectives and lax.ppermute only.
A program may use at most 128 MiB of HBM per device.

v0:
```python
import math

import jax
import jax.numpy as jnp
from jax import lax
from jax.sharding import PartitionSpec as P

BLOCK = 16
CAP = 2


def padded(block, sides, width):
    for axis, dim in sides:
        count = lax.axis_size(axis)
        forward = [(i, i + 1) for i in range(count - 1)]
        backward = [(target, source) for source, target in forward]
        low = lax.ppermute(
            lax.slice_in_dim(block, block.shape[dim] - width, None, axis=dim), axis, forward
        )
        high = lax.ppermute(lax.slice_in_dim(block, 0, width, axis=dim), axis, backward)
        block = jnp.concatenate([low, block, high], axis=dim)
    return block


def conv_valid(source, kernel):
    result = lax.conv_general_dilated(
        source[None],
        kernel,
        (1, 1),
        "VALID",
        dimension_numbers=("NCHW", "OIHW", "NCHW"),
        preferred_element_type=jnp.float32,
    )
    return result[0]


def flipped(kernel):
    return jnp.transpose(kernel[:, :, ::-1, ::-1], (1, 0, 2, 3))


def silu_slope(value):
    sigma = jax.nn.sigmoid(value)
    return sigma * (1.0 + value * (1.0 - sigma))


def correlate(image, grads):
    height = grads.shape[1]
    breadth = grads.shape[2]
    columns = []
    for row_shift in range(3):
        for col_shift in range(3):
            window = image[:, row_shift : row_shift + height, col_shift : col_shift + breadth]
            columns.append(
                jnp.einsum("ohw,ihw->oi", grads, window, preferred_element_type=jnp.float32)
            )
    stacked = jnp.stack(columns, axis=-1)
    return stacked.reshape(grads.shape[0], image.shape[0], 3, 3)


def body(warped, cotangent, w_first, b_first, w_second, source_tile, source_block):
    channels, height, breadth = warped.shape
    row_count = lax.axis_size("rows")
    col_count = lax.axis_size("cols")
    devices = row_count * col_count
    factor = 1.0 / math.sqrt(height * row_count * breadth * col_count)
    rim_depth = 1
    stacked = jnp.stack([warped, cotangent])
    rimmed = padded(stacked, (("rows", 2), ("cols", 3)), rim_depth)
    act_wide = jax.nn.silu(rimmed[0].astype(jnp.float32)).astype(jnp.bfloat16)
    grad_rimmed = rimmed[1]
    bias_column = b_first[:, None, None]
    a_mid = (warped.astype(jnp.float32) + conv_valid(act_wide, w_first) + bias_column).astype(
        jnp.bfloat16
    )
    act_core = jax.nn.silu(a_mid.astype(jnp.float32)).astype(jnp.bfloat16)
    act_mid = padded(act_core, (("rows", 1), ("cols", 2)), 1)
    w_second_term = correlate(act_mid, cotangent)
    b_second_term = jnp.sum(cotangent.astype(jnp.float32), axis=(1, 2))
    back_second = conv_valid(grad_rimmed, flipped(w_second))
    g_mid = (
        cotangent.astype(jnp.float32) + silu_slope(a_mid.astype(jnp.float32)) * back_second
    ).astype(jnp.bfloat16)
    g_rimmed = padded(g_mid, (("rows", 1), ("cols", 2)), 1)
    back_first = conv_valid(g_rimmed, flipped(w_first))
    g_warped = (
        g_mid.astype(jnp.float32) + silu_slope(warped.astype(jnp.float32)) * back_first
    ).astype(jnp.bfloat16)
    block_rows = height // BLOCK
    block_cols = breadth // BLOCK
    count = block_rows * block_cols
    area = BLOCK * BLOCK
    pieces = (
        g_warped.reshape(channels, block_rows, BLOCK, block_cols, BLOCK)
        .transpose(1, 3, 0, 2, 4)
        .reshape(count, channels, area)
    )
    target = source_tile.reshape(count)
    matches = (target[:, None] == jnp.arange(devices, dtype=jnp.int32)[None, :]).astype(jnp.int32)
    ranking = jnp.sum(jnp.cumsum(matches, axis=0) * matches, axis=1) - 1
    places = target * CAP + ranking
    outgoing = jnp.zeros((devices * CAP, channels, area), jnp.bfloat16).at[places].set(pieces)
    labels = (
        jnp.full((devices * CAP,), -1.0, jnp.bfloat16)
        .at[places]
        .set(source_block.reshape(count).astype(jnp.bfloat16))
    )
    arrived, arrived_labels = (
        lax.all_to_all(
            outgoing.reshape(devices, CAP, channels, area),
            ("rows", "cols"),
            split_axis=0,
            concat_axis=0,
            tiled=True,
        ),
        lax.all_to_all(
            labels.reshape(devices, CAP), ("rows", "cols"), split_axis=0, concat_axis=0, tiled=True
        ),
    )
    w_first_term = correlate(act_wide, g_mid)
    b_first_term = jnp.sum(g_mid.astype(jnp.float32), axis=(1, 2))
    sums = lax.psum((w_first_term, b_first_term, w_second_term, b_second_term), ("rows", "cols"))
    owners = arrived_labels.reshape(devices * CAP).astype(jnp.int32)
    selector = (owners[None, :] == jnp.arange(count, dtype=jnp.int32)[:, None]).astype(jnp.bfloat16)
    gathered = jnp.dot(
        selector,
        arrived.reshape(devices * CAP, channels * area),
        preferred_element_type=jnp.float32,
    )
    frame_grad = (
        gathered.reshape(block_rows, block_cols, channels, BLOCK, BLOCK)
        .transpose(2, 0, 3, 1, 4)
        .reshape(channels, height, breadth)
    )
    return (frame_grad, sums[0] * factor, sums[1] * factor, sums[2] * factor, sums[3] * factor)


def solution(mesh):
    in_specs = (
        P(None, "rows", "cols"),
        P(None, "rows", "cols"),
        P(),
        P(),
        P(),
        P("rows", "cols"),
        P("rows", "cols"),
    )
    out_specs = (P(None, "rows", "cols"), P(), P(), P(), P())
    return jax.shard_map(body, mesh=mesh, in_specs=in_specs, out_specs=out_specs, check_vma=False)
```

profile of v0, /device:TPU:0, one launch (start us, length us, event | category | flops | bytes accessed | tf_op | source)
XLA Modules:
  0.0 537.1 jit_solution(11575672523195795367)
XLA Ops:
  7.2 4.6 copy_bitcast_fusion
  13.1 4.8 collective-permute-start
  21.7 7.6 %all-to-all-start = ((bf16[32,1,2]{2,1,0:T(2,128)(2,1)}), bf16[32,1,2]{2,1,0:T(2,128)(2,1)S(1)}, u32[]{:S(2)}, u32[]{:S(2)}) async-start(bf16[32,1,2]{2,1,0:T(2,128)(2,1)} %all_to_all.12), calls=%async_computation | async-start | bytes 32768 | tf_op jit(solution)/shard_map/all_to_all | solution.py:115
  29.8 2.8 pad_maximum_fusion.5
  36.8 3.9 collective-permute-start.2
  44.2 8.1 %pad_maximum_fusion = bf16[2,64,34,514]{3,1,2,0:T(8,128)(2,1)S(1)} fusion(bf16[2,64,34,1]{3,1,2,0:T(8,128)(2,1)} %copy.92, bf16[2,64,1,512]{3,1,2,0:T(8,128)(2,1)} %collective-permute-done.1, bf16[1,64,32,512]{3,1,2,0:T(8,128)(2,1)} %copy-done.2, bf16[1,64,32,512]{3,1,2,0:T(8,128)(2,1)S(1)} %get-tuple-element.42, ...), kind=kLoop, calls=%fused_computation.25 | loop fusion | flops 26843136 | bytes 8947712 | tf_op jit(solution)/shard_map/concatenate | solution.py:21
  52.3 3.2 fusion.8
  59.5 8.3 %reshape.120 = bf16[64,34,1,8,65]{4,3,0,1,2:T(8,128)(2,1)} reshape(bf16[64,34,1,520]{3,0,1,2:T(8,128)(2,1)} %pad.2) | data formatting | bytes 4526080 | tf_op jit(solution)/shard_map/conv_general_dilated | solution.py:26
  67.8 8.3 %copy.97 = bf16[64,34,1,8,65]{0,3,4,1,2:T(8,128)(2,1)} copy(bf16[64,34,1,8,65]{4,3,0,1,2:T(8,128)(2,1)} %reshape.120) | data formatting | bytes 4526080 | tf_op jit(solution)/shard_map/conv_general_dilated | solution.py:26
  77.0 5.4 %reshape.113 = bf16[64,34,1,8,65]{4,3,0,1,2:T(8,128)(2,1)} reshape(bf16[64,34,1,520]{3,0,1,2:T(8,128)(2,1)S(1)} %pad) | data formatting | bytes 4526080 | tf_op jit(solution)/shard_map/conv_general_dilated | solution.py:26
  82.4 8.4 %copy.94 = bf16[64,34,1,8,65]{0,3,4,1,2:T(8,128)(2,1)} copy(bf16[64,34,1,8,65]{4,3,0,1,2:T(8,128)(2,1)} %reshape.113) | data formatting | bytes 4526080 | tf_op jit(solution)/shard_map/conv_general_dilated | solution.py:26
  91.7 14.3 %broadcast_select_fusion.2 = f32[32,8,65,64]{3,1,2,0:T(8,128)} fusion(pred[8,65]{0,1:T(8,128)(4,1)S(1)} %copy-done.16, bf16[64,64,3,3]{1,0,3,2:T(8,128)(2,1)S(1)} %copy-done, bf16[64,34,1,7,2]{0,3,4,1,2:T(8,128)(2,1)S(1)} %slice.139, bf16[64,34,1,8,65]{0,3,4,1,2:T(8,128)(2,1)} %copy.94), kind=kOutput, calls=%fused_computation.50 | convolution fusion | flops 1234896896 | bytes 6658056 | tf_op jit(solution)/shard_map/conv_general_dilated | solution.py:26
  106.0 10.0 %copy.95 = f32[32,8,65,64]{2,1,3,0:T(8,128)} copy(f32[32,8,65,64]{3,1,2,0:T(8,128)} %broadcast_select_fusion.2) | data formatting | bytes 8519680 | tf_op jit(solution)/shard_map/conv_general_dilated | solution.py:26
  116.1 9.2 %reshape.117 = f32[32,1,520,64]{2,3,0,1:T(8,128)} reshape(f32[32,8,65,64]{2,1,3,0:T(8,128)} %copy.95) | data formatting | bytes 8519680 | tf_op jit(solution)/shard_map/conv_general_dilated | solution.py:26
  125.3 11.5 %broadcast_select_fusion.1 = f32[32,8,65,64]{3,1,2,0:T(8,128)} fusion(pred[8,65]{0,1:T(8,128)(4,1)S(1)} %copy-done.16, bf16[64,64,3,3]{1,0,3,2:T(8,128)(2,1)S(1)} %copy-done.14, bf16[64,34,1,7,2]{0,3,4,1,2:T(8,128)(2,1)S(1)} %slice.142, bf16[64,34,1,8,65]{0,3,4,1,2:T(8,128)(2,1)} %copy.97), kind=kOutput, calls=%fused_computation.49 | convolution fusion | flops 1234896896 | bytes 6658056 | tf_op jit(solution)/shard_map/conv_general_dilated | solution.py:26
  136.8 10.0 %copy.98 = f32[32,8,65,64]{2,1,3,0:T(8,128)} copy(f32[32,8,65,64]{3,1,2,0:T(8,128)} %broadcast_select_fusion.1) | data formatting | bytes 8519680 | tf_op jit(solution)/shard_map/conv_general_dilated | solution.py:26
  146.8 8.7 %reshape.124 = f32[32,1,520,64]{2,3,0,1:T(8,128)} reshape(f32[32,8,65,64]{2,1,3,0:T(8,128)} %copy.98) | data formatting | bytes 8519680 | tf_op jit(solution)/shard_map/conv_general_dilated | solution.py:26
  155.5 7.0 %convert_reduce_fusion = (f32[64]{0:T(128)S(1)}, bf16[64,32,512]{2,0,1:T(8,128)(2,1)S(1)}, bf16[64,32,512]{2,0,1:T(8,128)(2,1)S(1)}, f32[64]{0:T(128)S(1)}) fusion(f32[32,1,520,64]{2,3,0,1:T(8,128)} %reshape.124, bf16[64,32,512]{2,1,0:T(8,128)(2,1)} %param.8, f32[64]{0:T(128)S(1)} %copy-done.11, f32[32,1,520,64]{2,3,0,1:T(8,128)} %reshape.117, ...), kind=kLoop, calls=%fused_computation.26 | loop fusion | flops 19922816 | bytes 16777984 | tf_op jit(solution)/shard_map/reduce_sum | solution.py:120
  162.5 3.7 collective-permute-start.4
  179.9 43.0 %all-reduce = (f32[64]{0:T(128)S(1)}, f32[64]{0:T(128)}) all-reduce(f32[64]{0:T(128)S(1)} %get-tuple-element.24, f32[64]{0:T(128)S(1)} %get-tuple-element.37), channel_id=1, replica_groups=mesh['rows'=8,'cols'=4] {'rows','cols'}, use_global_device_ids=true, to_apply=%region_6.7 | all-reduce | flops 128 | bytes 1024 | tf_op jit(solution)/shard_map/psum | solution.py:121
  223.5 4.2 collective-permute-start.8
  233.1 3.6 collective-permute-start.6
  240.1 3.2 collective-permute-start.10
  246.7 3.8 maximum_bitcast_fusion
  252.4 8.3 %reshape.127 = bf16[64,34,1,8,65]{4,3,0,1,2:T(8,128)(2,1)} reshape(bf16[64,34,1,520]{3,0,1,2:T(8,128)(2,1)} %pad.4) | data formatting | bytes 4526080 | tf_op jit(solution)/shard_map/conv_general_dilated | solution.py:26
  260.7 8.4 %copy.104 = bf16[64,34,1,8,65]{0,3,4,1,2:T(8,128)(2,1)} copy(bf16[64,34,1,8,65]{4,3,0,1,2:T(8,128)(2,1)} %reshape.127) | data formatting | bytes 4526080 | tf_op jit(solution)/shard_map/conv_general_dilated | solution.py:26
  270.0 11.5 %broadcast_select_fusion = f32[32,8,65,64]{3,1,2,0:T(8,128)} fusion(pred[8,65]{0,1:T(8,128)(4,1)S(1)} %copy-done.17, bf16[64,64,3,3]{1,0,3,2:T(8,128)(2,1)S(1)} %copy-done, bf16[64,34,1,7,2]{0,3,4,1,2:T(8,128)(2,1)S(1)} %slice.146, bf16[64,34,1,8,65]{0,3,4,1,2:T(8,128)(2,1)} %copy.104), kind=kOutput, calls=%fused_computation.48 | convolution fusion | flops 1234896896 | bytes 6658056 | tf_op jit(solution)/shard_map/conv_general_dilated | solution.py:26
  281.4 10.0 %copy.105 = f32[32,8,65,64]{2,1,3,0:T(8,128)} copy(f32[32,8,65,64]{3,1,2,0:T(8,128)} %broadcast_select_fusion) | data formatting | bytes 8519680 | tf_op jit(solution)/shard_map/conv_general_dilated | solution.py:26
  291.5 8.7 %reshape.131 = f32[32,1,520,64]{2,3,0,1:T(8,128)} reshape(f32[32,8,65,64]{2,1,3,0:T(8,128)} %copy.105) | data formatting | bytes 8519680 | tf_op jit(solution)/shard_map/conv_general_dilated | solution.py:26
  300.2 5.2 fusion.35
  305.4 4.7 copy.106
  310.1 5.4 copy.107
  315.5 3.5 copy.108
  320.6 8.6 %scatter_fusion = bf16[64,64,256]{2,1,0:T(8,128)(2,1)} fusion(bf16[64,64,256]{2,1,0:T(8,128)(2,1)} %broadcast_in_dim.7, s32[64]{0:T(128)S(1)} %copy-done.13, bf16[64,64,256]{2,1,0:T(8,128)(2,1)S(1)} %copy.108), kind=kCustom, calls=%fused_computation.1 | custom fusion | bytes 6291712 | tf_op jit(solution)/shard_map/scatter | solution.py:101
  329.2 7.7 %all-to-all-start.1 = ((bf16[32,2,64,256]{3,2,1,0:T(8,128)(2,1)}), bf16[32,2,64,256]{3,2,1,0:T(8,128)(2,1)}, u32[]{:S(2)}, u32[]{:S(2)}) async-start(bf16[32,2,64,256]{3,2,1,0:T(8,128)(2,1)} %bitcast.21), calls=%async_computation.1 | async-start | bytes 4194304 | tf_op jit(solution)/shard_map/all_to_all | solution.py:108
  339.1 2.5 pad_maximum_fusion.1
  344.1 2.6 fusion.177
  346.6 2.7 fusion.141
  351.7 2.8 fusion.180
  354.5 2.7 fusion.153
  359.6 2.6 fusion.171
  362.2 2.7 fusion.165
  366.2 129.6 %all-reduce.4.cloned.1.call-done = (f32[64,64,3,3]{1,0,3,2:T(8,128)}, f32[64,64,3,3]{1,0,3,2:T(8,128)}) async-done(((f32[64,64,3,3]{1,0,3,2:T(8,128)}, f32[64,64,3,3]{1,0,3,2:T(8,128)}), (f32[64,64,3,3]{1,0,3,2:T(8,128)}, f32[64,64,3,3]{1,0,3,2:T(8,128)})) %all-reduce.4.cloned.1.call-update) | async-done | bytes 294928 | tf_op jit(solution)/shard_map/psum | solution.py:121
  499.2 2.9 copy.128
  502.1 3.5 copy.109
  505.6 6.3 %fusion.54 = f32[64,2,16,32,16]{0,3,4,2,1:T(8,128)S(1)} fusion(bf16[64,16,16,64]{3,2,1,0:T(8,128)(2,1)} %bitcast.214, s32[2,32]{1,0:T(2,128)S(1)} %copy-done.9, s32[64]{0:T(128)S(1)} %copy-done.8), kind=kOutput, calls=%fused_computation.74 | convolution fusion | flops 134221824 | bytes 6291968 | tf_op jit(solution)/shard_map/dot_general | solution.py:124
  512.0 10.8 %copy.111 = f32[64,2,16,32,16]{0,4,3,2,1:T(8,128)} copy(f32[64,2,16,32,16]{0,3,4,2,1:T(8,128)S(1)} %fusion.54) | data formatting | bytes 8388608 | tf_op jit(solution)/shard_map/transpose | solution.py:131
  522.8 7.3 %copy.126 = f32[64,32,512]{2,1,0:T(8,128)} copy(f32[64,32,512]{0,2,1:T(8,128)} %bitcast.213) | data formatting | bytes 8388608
  (118 shorter events, 63.9 us)
Async XLA Ops:
  7.2 84.6 %copy-start = (bf16[64,64,3,3]{1,0,3,2:T(8,128)(2,1)S(1)}, bf16[64,64,3,3]{1,0,3,2:T(8,128)(2,1)}, u32[]{:S(2)}) copy-start(bf16[64,64,3,3]{1,0,3,2:T(8,128)(2,1)} %param.9) | copy-start | bytes 221188
  11.8 1.3 copy-start.2
  11.8 7.5 %copy-start.10 = (s32[2,32]{1,0:T(2,128)S(1)}, s32[2,32]{1,0:T(2,128)}, u32[]{:S(2)}) copy-start(s32[2,32]{1,0:T(2,128)} %param.12) | copy-start | bytes 772
  11.8 8.0 %copy-start.15 = (s32[2,32]{1,0:T(2,128)S(1)}, s32[2,32]{1,0:T(2,128)}, u32[]{:S(2)}) copy-start(s32[2,32]{1,0:T(2,128)} %param.13) | copy-start | bytes 772
  13.1 16.7 %collective-permute-start = (bf16[2,64,1,512]{3,1,2,0:T(8,128)(2,1)S(1)}, bf16[2,64,1,512]{3,1,2,0:T(8,128)(2,1)S(1)}, u32[]{:S(2)}, u32[]{:S(2)}) collective-permute-start(bf16[2,64,1,512]{3,1,2,0:T(8,128)(2,1)S(1)} %get-tuple-element.29), channel_id=1, source_target_pairs={{0,4},{4,8},{8,12},{12,16},{16,20},{20,24},{24,28},{1,5},{5,9},{9,... | collective-permute-start | bytes 393224 | tf_op jit(solution)/shard_map/ppermute | solution.py:17
  18.0 11.8 %collective-permute-start.1 = (bf16[2,64,1,512]{3,1,2,0:T(8,128)(2,1)S(1)}, bf16[2,64,1,512]{3,1,2,0:T(8,128)(2,1)}, u32[]{:S(2)}, u32[]{:S(2)}) collective-permute-start(bf16[2,64,1,512]{3,1,2,0:T(8,128)(2,1)S(1)} %get-tuple-element.30), channel_id=1, source_target_pairs={{4,0},{8,4},{12,8},{16,12},{20,16},{24,20},{28,24},{5,1},{9,5},{13... | collective-permute-start | bytes 393224 | tf_op jit(solution)/shard_map/ppermute | solution.py:20
  19.9 10.0 %copy-start.12 = (s32[64]{0:T(128)}, s32[64]{0:T(128)S(1)}, u32[]{:S(2)}) copy-start(s32[64]{0:T(128)S(1)} %fusion.186) | copy-start | bytes 772
  21.7 19.0 %all-to-all-start = ((bf16[32,1,2]{2,1,0:T(2,128)(2,1)}), bf16[32,1,2]{2,1,0:T(2,128)(2,1)S(1)}, u32[]{:S(2)}, u32[]{:S(2)}) async-start(bf16[32,1,2]{2,1,0:T(2,128)(2,1)} %all_to_all.12), calls=%async_computation | async-start | bytes 32768 | tf_op jit(solution)/shard_map/all_to_all | solution.py:115
  35.5 7.2 %collective-permute-start.3 = (bf16[2,64,34,1]{1,0,3,2:T(2,128)(2,1)S(1)}, bf16[2,64,34,1]{1,0,3,2:T(2,128)(2,1)S(1)}, u32[]{:S(2)}, u32[]{:S(2)}) collective-permute-start(bf16[2,64,34,1]{1,0,3,2:T(2,128)(2,1)S(1)} %copy.90), channel_id=1, source_target_pairs={{1,0},{2,1},{3,2},{5,4},{6,5},{7,6},{9,8},{10,9},{11,10},{13,12},{... | collective-permute-start | bytes 26120 | tf_op jit(solution)/shard_map/ppermute | solution.py:20
  36.8 4.6 collective-permute-start.2
  82.4 9.3 %copy-start.16 = (pred[8,65]{0,1:T(8,128)(4,1)S(1)}, pred[8,65]{0,1:T(8,128)(4,1)}, u32[]{:S(2)}) copy-start(pred[8,65]{0,1:T(8,128)(4,1)} %constant.45) | copy-start | bytes 1564
  116.0 9.2 %copy-start.14 = (bf16[64,64,3,3]{1,0,3,2:T(8,128)(2,1)S(1)}, bf16[64,64,3,3]{1,0,3,2:T(8,128)(2,1)}, u32[]{:S(2)}) copy-start(bf16[64,64,3,3]{1,0,3,2:T(8,128)(2,1)} %param.11) | copy-start | bytes 221188
  146.8 8.7 %copy-start.11 = (f32[64]{0:T(128)S(1)}, f32[64]{0:T(128)}, u32[]{:S(2)}) copy-start(f32[64]{0:T(128)} %param.10) | copy-start | bytes 772
  155.5 12.2 %copy-start.6 = (bf16[64,34,514]{2,0,1:T(8,128)(2,1)S(1)}, bf16[64,34,514]{2,0,1:T(8,128)(2,1)}, u32[]{:S(2)}) copy-start(bf16[64,34,514]{2,0,1:T(8,128)(2,1)} %fusion.8) | copy-start | bytes 6710788
  162.5 66.4 %collective-permute-start.4 = (bf16[64,1,512]{2,0,1:T(8,128)(2,1)S(1)}, bf16[64,1,512]{2,0,1:T(8,128)(2,1)S(1)}, u32[]{:S(2)}, u32[]{:S(2)}) collective-permute-start(bf16[64,1,512]{2,0,1:T(8,128)(2,1)S(1)} %get-tuple-element.40), channel_id=1, source_target_pairs={{0,4},{4,8},{8,12},{12,16},{16,20},{20,24},{24,28},{1,5},{5,9},{9,... | collective-permute-start | bytes 196616 | tf_op jit(solution)/shard_map/ppermute | solution.py:17
  166.2 62.8 %collective-permute-start.5 = (bf16[64,1,512]{2,0,1:T(8,128)(2,1)S(1)}, bf16[64,1,512]{2,0,1:T(8,128)(2,1)}, u32[]{:S(2)}, u32[]{:S(2)}) collective-permute-start(bf16[64,1,512]{2,0,1:T(8,128)(2,1)S(1)} %get-tuple-element.41), channel_id=1, source_target_pairs={{4,0},{8,4},{12,8},{16,12},{20,16},{24,20},{28,24},{5,1},{9,5},{13... | collective-permute-start | bytes 196616 | tf_op jit(solution)/shard_map/ppermute | solution.py:20
  175.9 0.7 copy-start.7
  177.9 1.4 copy-start.3
  223.5 13.3 %collective-permute-start.8 = (bf16[64,1,512]{2,0,1:T(8,128)(2,1)}, bf16[64,1,512]{2,0,1:T(8,128)(2,1)S(1)}, u32[]{:S(2)}, u32[]{:S(2)}) collective-permute-start(bf16[64,1,512]{2,0,1:T(8,128)(2,1)} %get-tuple-element.38), channel_id=1, source_target_pairs={{0,4},{4,8},{8,12},{12,16},{16,20},{20,24},{24,28},{1,5},{5,9},{9,... | collective-permute-start | bytes 196616 | tf_op jit(solution)/shard_map/ppermute | solution.py:17
  227.7 9.1 %collective-permute-start.9 = (bf16[64,1,512]{2,0,1:T(8,128)(2,1)}, bf16[64,1,512]{2,0,1:T(8,128)(2,1)S(1)}, u32[]{:S(2)}, u32[]{:S(2)}) collective-permute-start(bf16[64,1,512]{2,0,1:T(8,128)(2,1)} %get-tuple-element.39), channel_id=1, source_target_pairs={{4,0},{8,4},{12,8},{16,12},{20,16},{24,20},{28,24},{5,1},{9,5},{13... | collective-permute-start | bytes 196616 | tf_op jit(solution)/shard_map/ppermute | solution.py:20
  231.8 13.8 %collective-permute-start.7 = (bf16[64,34,1]{0,1,2:T(8,128)(2,1)}, bf16[64,34,1]{0,1,2:T(8,128)(2,1)}, u32[]{:S(2)}, u32[]{:S(2)}) collective-permute-start(bf16[64,34,1]{0,1,2:T(8,128)(2,1)} %copy.100), channel_id=1, source_target_pairs={{1,0},{2,1},{3,2},{5,4},{6,5},{7,6},{9,8},{10,9},{11,10},{13,12},{... | collective-permute-start | bytes 13064 | tf_op jit(solution)/shard_map/ppermute | solution.py:20
  233.1 11.4 %collective-permute-start.6 = (bf16[64,34,1]{0,1,2:T(8,128)(2,1)}, bf16[64,34,1]{0,1,2:T(8,128)(2,1)}, u32[]{:S(2)}, u32[]{:S(2)}) collective-permute-start(bf16[64,34,1]{0,1,2:T(8,128)(2,1)} %copy.99), channel_id=1, source_target_pairs={{0,1},{1,2},{2,3},{4,5},{5,6},{6,7},{8,9},{9,10},{10,11},{12,13},{... | collective-permute-start | bytes 13064 | tf_op jit(solution)/shard_map/ppermute | solution.py:17
  240.1 98.0 %collective-permute-start.10 = (bf16[64,34,1]{0,1,2:T(8,128)(2,1)}, bf16[64,34,1]{0,1,2:T(8,128)(2,1)}, u32[]{:S(2)}, u32[]{:S(2)}) collective-permute-start(bf16[64,34,1]{0,1,2:T(8,128)(2,1)} %copy.112), channel_id=1, source_target_pairs={{0,1},{1,2},{2,3},{4,5},{5,6},{6,7},{8,9},{9,10},{10,11},{12,13},{... | collective-permute-start | bytes 13064 | tf_op jit(solution)/shard_map/ppermute | solution.py:17
  243.3 93.7 %collective-permute-start.11 = (bf16[64,34,1]{0,1,2:T(8,128)(2,1)}, bf16[64,34,1]{0,1,2:T(8,128)(2,1)}, u32[]{:S(2)}, u32[]{:S(2)}) collective-permute-start(bf16[64,34,1]{0,1,2:T(8,128)(2,1)} %copy.116), channel_id=1, source_target_pairs={{1,0},{2,1},{3,2},{5,4},{6,5},{7,6},{9,8},{10,9},{11,10},{13,12},{... | collective-permute-start | bytes 13064 | tf_op jit(solution)/shard_map/ppermute | solution.py:20
  260.7 9.3 %copy-start.17 = (pred[8,65]{0,1:T(8,128)(4,1)S(1)}, pred[8,65]{0,1:T(8,128)(4,1)}, u32[]{:S(2)}) copy-start(pred[8,65]{0,1:T(8,128)(4,1)} %constant.45) | copy-start | bytes 1564
  315.5 5.1 copy-start.13
  329.2 9.9 %copy-start.4 = (bf16[64,32,512]{2,0,1:T(8,128)(2,1)S(1)}, bf16[64,32,512]{2,0,1:T(8,128)(2,1)}, u32[]{:S(2)}) copy-start(bf16[64,32,512]{2,0,1:T(8,128)(2,1)} %copy-done.3) | copy-start | bytes 6291460
  329.2 170.0 %all-to-all-start.1 = ((bf16[32,2,64,256]{3,2,1,0:T(8,128)(2,1)}), bf16[32,2,64,256]{3,2,1,0:T(8,128)(2,1)}, u32[]{:S(2)}, u32[]{:S(2)}) async-start(bf16[32,2,64,256]{3,2,1,0:T(8,128)(2,1)} %bitcast.21), calls=%async_computation.1 | async-start | bytes 4194304 | tf_op jit(solution)/shard_map/all_to_all | solution.py:108
  336.9 158.9 %all-reduce.4.cloned.1.call-start = ((), (), s32[]{:S(2)}) async-start(), calls=%async_computation.2 | async-start | bytes 1179648 | tf_op jit(solution)/shard_map/psum | solution.py:121
  339.1 2.5 copy-start.5
  362.2 3.6 copy-start.18
  502.1 3.5 copy-start.8
  502.1 3.5 copy-start.9
  522.8 7.3 %copy-start.1 = (bf16[64,64,3,3]{1,0,3,2:T(8,128)(2,1)S(1)}, bf16[64,64,3,3]{1,0,3,2:T(8,128)(2,1)}, u32[]{:S(2)}) copy-start(bf16[64,64,3,3]{1,0,3,2:T(8,128)(2,1)} %param.9) | copy-start | bytes 221188
Sparse Core Ops, SparseCore 0:
  365.8 129.9 all-reduce.3
where the time goes:
time: 545 us; the launch traced here: 537 us
  local copies, waits for them, and re-layouts  185 us (34%)
  waiting for transfers between devices  130 us (24%)
  matrix products  74.8 us (14%)
  starting transfers between devices  46.6 us (9%)
  other arithmetic  43.3 us (8%)
  blocking collectives  43 us (8%)
  between operations  14.9 us (3%)
    psum x1, waiting for transfers between devices, body(): lax.psum((w_first_term, b_first_term, w_second_term, b_second_term), ('ro...  130 us
    conv_general_dilated x15, local copies, waits for them, and re-layouts, conv_valid(): lax.conv_general_dilated(source[None], kernel, (1, 1), 'VALID', dimension...  107 us
    psum x1, blocking collectives, body(): lax.psum((w_first_term, b_first_term, w_second_term, b_second_term), ('ro...  43 us
    conv_general_dilated x3, matrix products, conv_valid(): lax.conv_general_dilated(source[None], kernel, (1, 1), 'VALID', dimension...  37.2 us
    dot_general x18, matrix products, correlate(): jnp.einsum('ohw,ihw->oi', grads, window, preferred_element_type=jnp.float32)  31.3 us
    ppermute x6, starting transfers between devices, padded(): lax.ppermute(lax.slice_in_dim(block, block.shape[dim] - width, None, axis...  23.4 us
    unnamed x40, local copies, waits for them, and re-layouts  13.6 us
    concatenate x3, other arithmetic, padded(): block = jnp.concatenate([low, block, high], axis=dim)  12 us
  transfers between devices with their start and end apart: 15, of which 1 were waited for; matrix products, arithmetic and copies ran while one was open for 27% of the time, Pallas kernels for 0%

commit v1 on v0

v1 whole, which is shorter than its diff:
```python
import functools
import math

import jax
import jax.numpy as jnp
from jax import lax
from jax.experimental import pallas as pl
from jax.experimental.pallas import tpu as pltpu
from jax.sharding import PartitionSpec as P

BLOCK = 16
CAP = 2
AXES = ("rows", "cols")
BF16 = jnp.bfloat16
F32 = jnp.float32
NT = (((1,), (1,)), ((), ()))
TN = (((0,), (0,)), ((), ()))
VMEM_BYTES = 60 * 2**20


def params(**extra):
    return pltpu.CompilerParams(vmem_limit_bytes=VMEM_BYTES, **extra)


def sigmoid(value):
    return 1.0 / (1.0 + jnp.exp(-value))


def one_hot(shape, pairs):
    row = lax.broadcasted_iota(jnp.int32, shape, 0)
    col = lax.broadcasted_iota(jnp.int32, shape, 1)
    hit = jnp.zeros(shape, jnp.bool_)
    for at_row, at_col in pairs:
        hit = hit | ((row == at_row) & (col == at_col))
    return hit.astype(F32).astype(BF16)


def reorder_kernel(w_ref, c_ref, xw_ref, xc_ref):
    channels, rows, _ = w_ref.shape
    for source, target in ((w_ref, xw_ref), (c_ref, xc_ref)):
        value = source[...].astype(F32)
        swapped = jnp.swapaxes(value, 0, 1)
        target[...] = swapped.reshape(rows * channels, value.shape[2]).astype(BF16)


def reorder(warped, cotangent):
    channels, height, breadth = warped.shape
    step = 16
    lanes = 128
    spec_in = pl.BlockSpec((channels, step, lanes), lambda h, x: (0, h, x))
    spec_out = pl.BlockSpec((step * channels, lanes), lambda h, x: (h, x))
    shape = jax.ShapeDtypeStruct((height * channels, breadth), BF16)
    return pl.pallas_call(
        reorder_kernel,
        grid=(height // step, breadth // lanes),
        in_specs=[spec_in, spec_in],
        out_specs=[spec_out, spec_out],
        out_shape=[shape, shape],
        compiler_params=params(),
        name="reorder",
    )(warped, cotangent)


def edges_kernel(wl_ref, cl_ref, wr_ref, cr_ref, to_right_ref, to_left_ref):
    lanes = wl_ref.shape[1]
    last = lanes - 1
    shape = (16, lanes)

    def pick(ref, pairs):
        return lax.dot_general(one_hot(shape, pairs), ref[...], NT, preferred_element_type=F32)

    to_right_ref[...] = (
        pick(wr_ref, ((0, last - 1), (1, last))) + pick(cr_ref, ((2, last - 1), (3, last)))
    ).astype(BF16)
    to_left_ref[...] = (pick(wl_ref, ((4, 0), (5, 1))) + pick(cl_ref, ((6, 0), (7, 1)))).astype(BF16)


def edges(xw, xc):
    count, breadth = xw.shape
    tiles = breadth // 128
    first = pl.BlockSpec((count, 128), lambda i: (0, 0))
    final = pl.BlockSpec((count, 128), lambda i: (0, tiles - 1))
    whole = pl.BlockSpec((16, count), lambda i: (0, 0))
    shape = jax.ShapeDtypeStruct((16, count), BF16)
    return pl.pallas_call(
        edges_kernel,
        grid=(1,),
        in_specs=[first, first, final, final],
        out_specs=[whole, whole],
        out_shape=[shape, shape],
        compiler_params=params(),
        name="edges",
    )(xw, xc, xw, xc)


def convs_kernel(
    channels, height, breadth,
    flags_ref,
    xw_ref, xc_ref, up_ref, down_ref, side_ref, side_up_ref, side_down_ref,
    w1_ref, w2f_ref, w1f_ref, bias_ref, target_ref,
    packed_ref, act_in_ref, act_mid_ref, g_mid_ref,
    wx, cx, sa, sc, sg, gw,
):
    ch = channels
    wide = breadth + 128
    core = slice(0, breadth)
    rim = slice(breadth, wide)
    body = height * ch

    for at, (target, up_at) in enumerate(((wx, 0), (cx, 1))):
        target[2 * ch : 2 * ch + body, core] = (xw_ref if at == 0 else xc_ref)[...]
        target[0 : 2 * ch, core] = up_ref[up_at * 2 * ch : (up_at + 1) * 2 * ch, :]
        target[2 * ch + body :, core] = down_ref[up_at * 2 * ch : (up_at + 1) * 2 * ch, :]
        low = 2 * at
        spread = one_hot((16, 128), ((low, 126), (low + 1, 127), (low + 4, 0), (low + 5, 1)))

        def side(ref):
            return lax.dot_general(ref[...], spread, TN, preferred_element_type=F32).astype(BF16)

        target[2 * ch : 2 * ch + body, rim] = side(side_ref)
        target[0 : 2 * ch, rim] = side(side_up_ref)
        target[2 * ch + body :, rim] = side(side_down_ref)

    def shifted(value):
        return (
            pltpu.roll(value, 1, 1).astype(BF16),
            value.astype(BF16),
            pltpu.roll(value, wide - 1, 1).astype(BF16),
        )

    def prepare(row, _):
        at = pl.multiple_of(row * ch, ch)
        out = pl.multiple_of(row * 3 * ch, ch)
        value = wx[pl.ds(at, ch), :].astype(F32)
        act = value * sigmoid(value)
        for shift, moved in enumerate(shifted(act)):
            sa[pl.ds(out + shift * ch, ch), :] = moved
        for shift, moved in enumerate(shifted(cx[pl.ds(at, ch), :].astype(F32))):
            sc[pl.ds(out + shift * ch, ch), :] = moved
        return 0

    lax.fori_loop(0, height + 4, prepare, 0)

    def keep_act(row, _):
        act_in_ref[pl.ds(pl.multiple_of(row * ch, ch), ch), :] = sa[
            pl.ds(pl.multiple_of((row + 1) * 3 * ch + ch, ch), ch), :
        ]
        return 0

    lax.fori_loop(0, height + 2, keep_act, 0)

    lane = lax.broadcasted_iota(jnp.int32, (2 * ch, wide), 1)
    sub = lax.broadcasted_iota(jnp.int32, (2 * ch, wide), 0)
    lane_ok = (
        (lane < breadth)
        | ((lane == breadth) & (flags_ref[3] == 1))
        | ((lane == wide - 1) & (flags_ref[2] == 1))
    )

    def middle(pair, _):
        row = pair * 2
        window = pl.ds(pl.multiple_of(row * 3 * ch, ch), 12 * ch)
        here = pl.ds(pl.multiple_of((row + 1) * ch, ch), 2 * ch)
        conv = jnp.dot(w1_ref[...], sa[window, :], preferred_element_type=F32)
        a_mid = (wx[here, :].astype(F32) + conv + bias_ref[:, 0:1]).astype(BF16).astype(F32)
        back = jnp.dot(w2f_ref[...], sc[window, :], preferred_element_type=F32)
        sigma = sigmoid(a_mid)
        slope = sigma * (1.0 + a_mid * (1.0 - sigma))
        grad = cx[here, :].astype(F32) + slope * back
        top_ok = (row > 0) | (flags_ref[0] == 1)
        low_ok = (row < height) | (flags_ref[1] == 1)
        good = lane_ok & (((sub < ch) & top_ok) | ((sub >= ch) & low_ok))
        act = jnp.where(good, a_mid * sigma, 0.0)
        grad = jnp.where(good, grad, 0.0)
        act_mid_ref[pl.ds(pl.multiple_of(row * ch, ch), 2 * ch), :] = act.astype(BF16)
        out = pl.multiple_of(row * 3 * ch, ch)
        for shift, moved in enumerate(shifted(grad)):
            sg[pl.ds(out + shift * ch, ch), :] = moved[:ch]
            sg[pl.ds(out + (3 + shift) * ch, ch), :] = moved[ch:]
        return 0

    lax.fori_loop(0, height // 2 + 1, middle, 0)

    def last(pair, _):
        row = pair * 2
        base = pl.multiple_of(row * 3 * ch, ch)
        back = jnp.dot(w1f_ref[...], sg[pl.ds(base, 12 * ch), core], preferred_element_type=F32)
        value = wx[pl.ds(pl.multiple_of((row + 2) * ch, ch), 2 * ch), core].astype(F32)
        sigma = sigmoid(value)
        slope = sigma * (1.0 + value * (1.0 - sigma))
        mid = jnp.concatenate(
            [sg[pl.ds(base + 4 * ch, ch), core], sg[pl.ds(base + 7 * ch, ch), core]], axis=0
        )
        at = pl.ds(pl.multiple_of(row * ch, ch), 2 * ch)
        g_mid_ref[at, :] = mid
        gw[at, :] = (mid.astype(F32) + slope * back).astype(BF16)
        return 0

    lax.fori_loop(0, height // 2, last, 0)

    size = 256
    strip = BLOCK * ch

    def pack(part, _):
        start = pl.multiple_of(part * size, size)
        row_at = lax.broadcasted_iota(jnp.int32, (size, breadth), 0) + start
        total = None
        for band in range(height // BLOCK):
            chosen = (row_at == target_ref[band : band + 1, :]).astype(F32).astype(BF16)
            term = lax.dot_general(
                chosen, gw[band * strip : (band + 1) * strip, :], NT, preferred_element_type=F32
            )
            total = term if total is None else total + term
        packed_ref[pl.ds(start, size), :] = total.astype(BF16)
        return 0

    lax.fori_loop(0, packed_ref.shape[0] // size, pack, 0)


def convs(sizes, flags, operands, slots):
    channels, height, breadth = sizes
    wide = breadth + 128
    vmem = pl.BlockSpec(memory_space=pltpu.VMEM)
    outs = [
        jax.ShapeDtypeStruct((slots * BLOCK, BLOCK * channels), BF16),
        jax.ShapeDtypeStruct(((height + 2) * channels, wide), BF16),
        jax.ShapeDtypeStruct(((height + 2) * channels, wide), BF16),
        jax.ShapeDtypeStruct((height * channels, breadth), BF16),
    ]
    return pl.pallas_call(
        functools.partial(convs_kernel, channels, height, breadth),
        in_specs=[pl.BlockSpec(memory_space=pltpu.SMEM)] + [vmem] * len(operands),
        out_specs=[vmem] * len(outs),
        out_shape=outs,
        scratch_shapes=[
            pltpu.VMEM(((height + 4) * channels, wide), BF16),
            pltpu.VMEM(((height + 4) * channels, wide), BF16),
            pltpu.VMEM(((height + 4) * 3 * channels, wide), BF16),
            pltpu.VMEM(((height + 4) * 3 * channels, wide), BF16),
            pltpu.VMEM(((height + 2) * 3 * channels, wide), BF16),
            pltpu.VMEM((height * channels, breadth), BF16),
        ],
        compiler_params=params(),
        name="convs",
    )(flags, *operands)


def correlate_kernel(
    channels, height, breadth,
    act_in_ref, act_mid_ref, g_mid_ref, xc_ref, out_ref, s1, s2, acc1, acc2, b1, b2,
):
    ch = channels
    wide = breadth + 128
    core = slice(0, breadth)

    def prepare(row, _):
        at = pl.multiple_of(row * ch, ch)
        out = pl.multiple_of(row * 3 * ch, ch)
        for source, target in ((act_in_ref, s1), (act_mid_ref, s2)):
            value = source[pl.ds(at, ch), :].astype(F32)
            target[pl.ds(out, ch), :] = pltpu.roll(value, 1, 1)[:, core].astype(BF16)
            target[pl.ds(out + ch, ch), :] = source[pl.ds(at, ch), core]
            target[pl.ds(out + 2 * ch, ch), :] = pltpu.roll(value, wide - 1, 1)[:, core].astype(BF16)
        return 0

    lax.fori_loop(0, height + 2, prepare, 0)
    for ref in (acc1, acc2, b1, b2):
        ref[...] = jnp.zeros_like(ref)
    ones = jnp.ones((16, breadth), BF16)

    def add(pair, _):
        window = pl.ds(pl.multiple_of(pair * 6 * ch, ch), 12 * ch)
        here = pl.ds(pl.multiple_of(pair * 2 * ch, ch), 2 * ch)
        for image, grads, acc, bias in ((s1, g_mid_ref, acc1, b1), (s2, xc_ref, acc2, b2)):
            grad = grads[here, :]
            acc[...] += lax.dot_general(image[window, :], grad, NT, preferred_element_type=F32)
            bias[...] += lax.dot_general(ones, grad, NT, preferred_element_type=F32)
        return 0

    lax.fori_loop(0, height // 2, add, 0)

    def fold(acc, bias):
        taps = acc[0 : 9 * ch, :] + pltpu.roll(acc[3 * ch : 12 * ch, :], ch, 1)
        return taps, bias[0:8, :] + pltpu.roll(bias[0:8, :], ch, 1)

    first, first_bias = fold(acc1, b1)
    second, second_bias = fold(acc2, b2)
    low = lax.broadcasted_iota(jnp.int32, (9 * ch, 2 * ch), 1) < ch
    out_ref[0 : 9 * ch, :] = jnp.where(low, first, pltpu.roll(second, ch, 1))
    out_ref[9 * ch :, :] = jnp.where(low[0:8], first_bias, pltpu.roll(second_bias, ch, 1))


def correlate(sizes, act_in, act_mid, g_mid, xc):
    channels, height, breadth = sizes
    vmem = pl.BlockSpec(memory_space=pltpu.VMEM)
    flops = 2 * 2 * 12 * channels * 2 * channels * breadth * (height // 2)
    return pl.pallas_call(
        functools.partial(correlate_kernel, channels, height, breadth),
        in_specs=[vmem] * 4,
        out_specs=vmem,
        out_shape=jax.ShapeDtypeStruct((9 * channels + 8, 2 * channels), F32),
        scratch_shapes=[
            pltpu.VMEM(((height + 2) * 3 * channels, breadth), BF16),
            pltpu.VMEM(((height + 2) * 3 * channels, breadth), BF16),
            pltpu.VMEM((12 * channels, 2 * channels), F32),
            pltpu.VMEM((12 * channels, 2 * channels), F32),
            pltpu.VMEM((16, 2 * channels), F32),
            pltpu.VMEM((16, 2 * channels), F32),
        ],
        compiler_params=params(),
        cost_estimate=pl.CostEstimate(flops=flops, bytes_accessed=10**7, transcendentals=0),
        name="correlate",
    )(act_in, act_mid, g_mid, xc)


def unpack_kernel(channels, block_rows, arrived_ref, owner_ref, out_ref, flat):
    rows, depth = arrived_ref.shape
    part = out_ref.shape[3]
    lanes = out_ref.shape[4]

    @pl.when(pl.program_id(1) == 0)
    def _():
        flat[...] = arrived_ref[...].T

    column = pl.program_id(1) * lanes + lax.broadcasted_iota(jnp.int32, (rows, lanes), 1)
    breadth = lanes * pl.num_programs(1)
    for band in range(block_rows):
        chosen = (owner_ref[...] == column + band * breadth).astype(F32).astype(BF16)
        summed = jnp.dot(flat[...], chosen, preferred_element_type=F32)
        cube = summed.reshape(part, channels, lanes)
        out_ref[:, band, 0, :, :] = jnp.swapaxes(cube, 0, 1)


def unpack(sizes, arrived, owner):
    channels, height, breadth = sizes
    block_rows = height // BLOCK
    rows = arrived.shape[0]
    part = 8
    lanes = 128
    return pl.pallas_call(
        functools.partial(unpack_kernel, channels, block_rows),
        grid=(BLOCK // part, breadth // lanes),
        in_specs=[
            pl.BlockSpec((rows, part * channels), lambda h, x: (0, h)),
            pl.BlockSpec((rows, 1), lambda h, x: (0, 0)),
        ],
        out_specs=pl.BlockSpec(
            (channels, block_rows, 1, part, lanes), lambda h, x: (0, 0, h, 0, x)
        ),
        out_shape=jax.ShapeDtypeStruct((channels, block_rows, BLOCK // part, part, breadth), F32),
        scratch_shapes=[pltpu.VMEM((part * channels, rows), BF16)],
        compiler_params=params(),
        name="unpack",
    )(arrived, owner)


def pair_weights(kernel):
    taps = jnp.transpose(kernel, (0, 2, 3, 1)).reshape(kernel.shape[0], -1)
    third = taps.shape[1] // 3
    return jnp.concatenate(
        [jnp.pad(taps, ((0, 0), (0, third))), jnp.pad(taps, ((0, 0), (third, 0)))], axis=0
    )


def flipped(kernel):
    return jnp.transpose(kernel[:, :, ::-1, ::-1], (1, 0, 2, 3))


def shift_pairs(axis, step):
    count = lax.axis_size(axis)
    return [(i, i + step) for i in range(count) if 0 <= i + step < count]


def total_over_devices(terms, devices):
    me = lax.axis_index(AXES)
    bit = me % 2
    halves = terms.reshape(2, terms.shape[0] // 2, terms.shape[1])
    swap = [(i, i ^ 1) for i in range(devices)]
    mine = lax.dynamic_index_in_dim(halves, bit, 0, keepdims=False)
    away = lax.dynamic_index_in_dim(halves, 1 - bit, 0, keepdims=False)
    total = mine + lax.ppermute(away, AXES, swap)
    step = 2
    while step < devices:
        total = total + lax.ppermute(total, AXES, [(i, i ^ step) for i in range(devices)])
        step *= 2
    other = lax.ppermute(total, AXES, swap)
    first = jnp.where(bit == 0, total, other)
    second = jnp.where(bit == 0, other, total)
    return jnp.concatenate([first, second], axis=0)


def body(warped, cotangent, w_first, b_first, w_second, source_tile, source_block):
    sizes = warped.shape
    channels, height, breadth = sizes
    row_count = lax.axis_size("rows")
    col_count = lax.axis_size("cols")
    devices = row_count * col_count
    slots = devices * CAP
    factor = 1.0 / math.sqrt(height * row_count * breadth * col_count)
    row_at = lax.axis_index("rows")
    col_at = lax.axis_index("cols")
    me = lax.axis_index(AXES)

    block_rows = height // BLOCK
    count = source_tile.size
    target = source_tile.reshape(count)
    same = target[:, None] == target[None, :]
    earlier = jnp.arange(count)[None, :] < jnp.arange(count)[:, None]
    ranking = jnp.sum((same & earlier).astype(jnp.int32), axis=1)
    places = target * CAP + ranking
    target_row = (
        places.reshape(block_rows, -1, 1) * BLOCK + jnp.arange(BLOCK, dtype=jnp.int32)
    ).reshape(block_rows, breadth)
    hits = places[:, None] == jnp.arange(slots, dtype=jnp.int32)[None, :]
    labels = jnp.sum(jnp.where(hits, source_block.reshape(count, 1) + 1, 0), axis=0) - 1

    xw, xc = reorder(warped, cotangent)
    to_right, to_left = edges(xw, xc)
    rim = 2 * channels
    to_down = jnp.concatenate([xw[-rim:], xc[-rim:]], axis=0)
    to_up = jnp.concatenate([xw[:rim], xc[:rim]], axis=0)
    side = lax.ppermute(to_right, "cols", shift_pairs("cols", 1)) + lax.ppermute(
        to_left, "cols", shift_pairs("cols", -1)
    )
    up = lax.ppermute(to_down, "rows", shift_pairs("rows", 1))
    down = lax.ppermute(to_up, "rows", shift_pairs("rows", -1))
    side_up = lax.ppermute(side[:, -rim:], "rows", shift_pairs("rows", 1))
    side_down = lax.ppermute(side[:, :rim], "rows", shift_pairs("rows", -1))

    flags = jnp.stack(
        [row_at > 0, row_at < row_count - 1, col_at > 0, col_at < col_count - 1]
    ).astype(jnp.int32)
    bias = jnp.broadcast_to(jnp.tile(b_first, 2)[:, None], (2 * channels, 128))
    packed, act_in, act_mid, g_mid = convs(
        sizes,
        flags,
        (
            xw, xc, up, down, side, side_up, side_down,
            pair_weights(w_first), pair_weights(flipped(w_second)), pair_weights(flipped(w_first)),
            bias, target_row,
        ),
        slots,
    )
    arrived = lax.all_to_all(
        packed.reshape(devices, CAP * BLOCK, BLOCK * channels),
        AXES,
        split_axis=0,
        concat_axis=0,
        tiled=True,
    )

    terms = correlate(sizes, act_in, act_mid, g_mid, xc)
    mine = jnp.arange(devices, dtype=jnp.int32)[:, None] == me
    table = jnp.where(mine, labels.astype(F32)[None, :], 0.0).reshape(-1, 128)
    used = terms.shape[0] + table.shape[0]
    fill = jnp.zeros((-used % 16, 128), F32)
    summed = total_over_devices(jnp.concatenate([terms, table, fill], axis=0), devices)
    owners = lax.dynamic_slice_in_dim(
        summed[terms.shape[0] : used].reshape(devices, slots), me * CAP, CAP, axis=1
    ).astype(jnp.int32)
    owner_row = (
        owners.reshape(slots, 1) * BLOCK + jnp.arange(BLOCK, dtype=jnp.int32)[None, :]
    ).reshape(slots * BLOCK, 1)
    owner_row = jnp.where(owner_row < 0, -(2**20), owner_row)

    frame = unpack(sizes, arrived.reshape(slots * BLOCK, BLOCK * channels), owner_row)
    taps = (
        summed[: 9 * channels].reshape(3, 3, channels, 2, channels).transpose(3, 4, 2, 0, 1) * factor
    )
    biases = summed[9 * channels].reshape(2, channels) * factor
    return (frame.reshape(sizes), taps[0], biases[0], taps[1], biases[1])


def solution(mesh):
    in_specs = (
        P(None, "rows", "cols"),
        P(None, "rows", "cols"),
        P(),
        P(),
        P(),
        P("rows", "cols"),
        P("rows", "cols"),
    )
    out_specs = (P(None, "rows", "cols"), P(), P(), P(), P())
    return jax.shard_map(body, mesh=mesh, in_specs=in_specs, out_specs=out_specs, check_vma=False)
```

time: 545 us -> 154 us (0.28); the launches traced: 537 us -> 153 us
  local copies, waits for them, and re-layouts: 185 us -> 8.57 us
  waiting for transfers between devices: 130 us -> 33.5 us
  matrix products: 74.8 us -> 0 us
  Pallas kernels: 0 us -> 73.1 us
  blocking collectives: 43 us -> 0 us
  other arithmetic: 43.3 us -> 5.46 us
  starting transfers between devices: 46.6 us -> 31.8 us
  between operations: 14.9 us -> 0.98 us
    psum x1 -> x0, waiting for transfers between devices: 130 us -> none  [body(): lax.psum((w_first_term, b_first_term, w_second_term, b_second_term), ('ro...]
    conv_general_dilated x15 -> x0, local copies, waits for them, and re-layouts: 107 us -> none  [conv_valid(): lax.conv_general_dilated(source[None], kernel, (1, 1), 'VALID', dimension...]
    pallas_call x0 -> x5, Pallas kernels: none -> 73.1 us  [the longest x1 31.8 us: convs(): pl.pallas_call(functools.partial(convs_kernel, channels, height, breadth)...]
    psum x1 -> x0, blocking collectives: 43 us -> none  [body(): lax.psum((w_first_term, b_first_term, w_second_term, b_second_term), ('ro...]
    dot_general x19 -> x0, matrix products: 37.6 us -> none  [the longest x18 31.3 us: correlate(): jnp.einsum('ohw,ihw->oi', grads, window, preferred_element_type=jnp.float32)]
    conv_general_dilated x3 -> x0, matrix products: 37.2 us -> none  [conv_valid(): lax.conv_general_dilated(source[None], kernel, (1, 1), 'VALID', dimension...]
    ppermute x12, waiting for transfers between devices: 0.03 us -> 33.5 us  [the longest x4 26.9 us: total_over_devices(): lax.ppermute(total, AXES, [(i, i ^ step) for i in range(devices)])]
    transpose x2 -> x1, local copies, waits for them, and re-layouts: 16.2 us -> 0.15 us  [pair_weights(): taps = jnp.transpose(kernel, (0, 2, 3, 1)).reshape(kernel.shape[0], -1)]
  transfers between devices with their start and end apart: 15 -> 13, of which waited for: 1 -> 8; matrix products, arithmetic and copies ran while one was open for 27% -> 7% of each run, Pallas kernels for 0% -> 15%
where the time goes in v1:
time: 154 us; the launch traced here: 153 us
  Pallas kernels  73.1 us (47%)
  waiting for transfers between devices  33.5 us (22%)
  starting transfers between devices  31.8 us (21%)
  local copies, waits for them, and re-layouts  8.57 us (6%)
  other arithmetic  5.46 us (4%)
    pallas_call x1, Pallas kernels, convs(): pl.pallas_call(functools.partial(convs_kernel, channels, height, breadth)...  31.8 us
    ppermute x4, waiting for transfers between devices, total_over_devices(): lax.ppermute(total, AXES, [(i, i ^ step) for i in range(devices)])  26.9 us
    pallas_call x1, Pallas kernels, correlate(): pl.pallas_call(functools.partial(correlate_kernel, channels, height, brea...  20.6 us
    pallas_call x1, Pallas kernels, unpack(): pl.pallas_call(functools.partial(unpack_kernel, channels, block_rows), gr...  10.6 us
    ppermute x4, starting transfers between devices, total_over_devices(): lax.ppermute(total, AXES, [(i, i ^ step) for i in range(devices)])  8.37 us
    all_to_all x1, starting transfers between devices, body(): lax.all_to_all(packed.reshape(devices, CAP * BLOCK, BLOCK * channels), AX...  7.6 us
    pallas_call x1, Pallas kernels, reorder(): pl.pallas_call(reorder_kernel, grid=(height // step, breadth // lanes), i...  7.25 us
    ppermute x1, starting transfers between devices, body(): up = lax.ppermute(to_down, 'rows', shift_pairs('rows', 1))  5.62 us
  transfers between devices with their start and end apart: 13, of which 8 were waited for; matrix products, arithmetic and copies ran while one was open for 7% of the time, Pallas kernels for 15%

profile of v1, /device:TPU:0, one launch (start us, length us, event | category | flops | bytes accessed | tf_op | source)
XLA Modules:
  0.0 153.4 jit_solution(18158990654313853964)
XLA Ops:
  0.6 7.3 %reorder.1 = (bf16[2048,512]{1,0:T(8,128)(2,1)}, bf16[2048,512]{1,0:T(8,128)(2,1)}) custom-call(bf16[64,32,512]{2,1,0:T(8,128)(2,1)} %w_ref.1, bf16[64,32,512]{2,1,0:T(8,128)(2,1)} %c_ref.1), custom_call_target="tpu_custom_call" | custom-call | tf_op jit(solution)/shard_map/reorder/pallas_call | solution.py:53
  7.9 1.1 fusion.11
  9.0 1.3 collective-permute-start.1
  10.4 5.6 %collective-permute-start = (bf16[256,512]{1,0:T(8,128)(2,1)S(1)}, bf16[256,512]{1,0:T(8,128)(2,1)S(1)}, u32[]{:S(2)}, u32[]{:S(2)}) collective-permute-start(bf16[256,512]{1,0:T(8,128)(2,1)S(1)} %pad_maximum_fusion.1), channel_id=1, source_target_pairs={{0,4},{4,8},{8,12},{12,16},{16,20},{20,24},{24,28},{1,5},{5,9},{9,... | collective-permute-start | bytes 786440 | tf_op jit(solution)/shard_map/ppermute | solution.py:425
  16.0 2.9 %edges.1 = (bf16[16,2048]{1,0:T(8,128)(2,1)}, bf16[16,2048]{1,0:T(8,128)(2,1)}) custom-call(bf16[2048,512]{1,0:T(8,128)(2,1)} %get-tuple-element.13.wl_ref.wr_ref.xw_ref, bf16[2048,512]{1,0:T(8,128)(2,1)} %get-tuple-element.14.cl_ref.cr_ref.xc_ref, bf16[2048,512]{1,0:T(8,128)(2,1)} %get-tuple-element.13.wl_ref.wr_ref.xw_ref, ...), custom_call_target="tpu_custom_call" | custom-call | tf_op jit(solution)/shard_map/edges/pallas_call | solution.py:85
  18.9 1.6 %collective-permute-start.2 = (bf16[16,2048]{1,0:T(8,128)(2,1)}, bf16[16,2048]{1,0:T(8,128)(2,1)S(1)}, u32[]{:S(2)}, u32[]{:S(2)}) collective-permute-start(bf16[16,2048]{1,0:T(8,128)(2,1)} %get-tuple-element.15), channel_id=1, source_target_pairs={{0,1},{1,2},{2,3},{4,5},{5,6},{6,7},{8,9},{9,10},{10,11},{12,13},{... | collective-permute-start | bytes 196616 | tf_op jit(solution)/shard_map/ppermute | solution.py:422
  20.5 1.3 collective-permute-start.3
  21.9 0.2 convert_reduce_fusion
  22.2 0.1 add.128
  22.5 0.1 copy.26
  22.6 0.1 copy.27
  22.8 0.1 copy.29
  22.9 0.1 copy.31
  23.1 0.6 broadcast_add_fusion.target_ref
  23.7 0.9 fusion.7
  24.5 0.8 fusion.9.w1f_ref
  25.3 0.6 collective-permute-done.3
  26.0 4.3 %collective-permute-start.4 = (bf16[16,128]{1,0:T(8,128)(2,1)S(1)}, bf16[16,128]{1,0:T(8,128)(2,1)S(1)}, u32[]{:S(2)}, u32[]{:S(2)}) collective-permute-start(bf16[16,128]{1,0:T(8,128)(2,1)S(1)} %get-tuple-element.40), channel_id=1, source_target_pairs={{0,4},{4,8},{8,12},{12,16},{16,20},{20,24},{24,28},{1,5},{5,9},{9,... | collective-permute-start | bytes 12296 | tf_op jit(solution)/shard_map/ppermute | solution.py:427
  30.3 1.3 collective-permute-start.5
  31.6 0.6 add_convert_fusion.flags_ref
  32.3 3.5 %collective-permute-done.5.side_down_ref = bf16[16,128]{1,0:T(8,128)(2,1)S(1)} collective-permute-done((bf16[16,128]{1,0:T(8,128)(2,1)S(1)}, bf16[16,128]{1,0:T(8,128)(2,1)S(1)}, u32[]{:S(2)}, u32[]{:S(2)}) %collective-permute-start.5) | collective-permute-done | bytes 4128 | tf_op jit(solution)/shard_map/ppermute | solution.py:428
  35.8 0.8 broadcast_in_dim.61.bias_ref
  36.6 31.8 %convs.1 = (bf16[1024,1024]{1,0:T(8,128)(2,1)}, bf16[2176,640]{1,0:T(8,128)(2,1)}, bf16[2176,640]{1,0:T(8,128)(2,1)}, bf16[2048,512]{1,0:T(8,128)(2,1)}) custom-call(s32[4]{0:T(128)} %add_convert_fusion.flags_ref, bf16[2048,512]{1,0:T(8,128)(2,1)} %get-tuple-element.13.wl_ref.wr_ref.xw_ref, bf16[2048,512]{1,0:T(8,128)(2,1)} %get-tuple-element.14.cl_ref.cr_ref.xc_ref, ...), custom_call_target="tpu_custom_call" | custom-call | tf_op jit(solution)/shard_map/convs/pallas_call | solution.py:230
  68.4 7.6 %all-to-all-start = ((bf16[32,32,1024]{2,1,0:T(8,128)(2,1)}), bf16[32,32,1024]{2,1,0:T(8,128)(2,1)S(1)}, u32[]{:S(2)}, u32[]{:S(2)}) async-start(bf16[32,32,1024]{2,1,0:T(8,128)(2,1)} %bitcast.30), calls=%async_computation | async-start | bytes 4194304 | tf_op jit(solution)/shard_map/all_to_all | solution.py:444
  76.3 0.1 select_reduce_fusion
  76.6 20.6 %correlate.1 = f32[584,128]{1,0:T(8,128)} custom-call(bf16[2176,640]{1,0:T(8,128)(2,1)} %get-tuple-element.18.act_in_ref, bf16[2176,640]{1,0:T(8,128)(2,1)} %get-tuple-element.19.act_mid_ref, bf16[2048,512]{1,0:T(8,128)(2,1)} %get-tuple-element.20.g_mid_ref, bf16[2048,512]{1,0:T(8,128)(2,1)} %get-tuple-element.14.cl_ref.cr_ref.xc_ref), custom_call_target="tpu_custom_call" | custom-call | flops 3221225472 | bytes 10000000 | tf_op jit(solution)/shard_map/correlate/pallas_call | solution.py:297
  97.2 1.1 maximum_maximum_fusion
  98.3 0.3 collective-permute-start.6
  98.7 1.1 collective-permute-done.6
  99.8 1.9 %collective-permute-start.7 = (f32[304,128]{1,0:T(8,128)S(1)}, f32[304,128]{1,0:T(8,128)S(1)}, u32[]{:S(2)}, u32[]{:S(2)}) collective-permute-start(f32[304,128]{1,0:T(8,128)S(1)} %bitcast_add_fusion), channel_id=1, source_target_pairs={{0,2},{1,3},{2,0},{3,1},{4,6},{5,7},{6,4},{7,5},{8,10},{9,11},{10,... | collective-permute-start | bytes 466952 | tf_op jit(solution)/shard_map/ppermute | solution.py:384
  101.7 5.5 %collective-permute-done.7 = f32[304,128]{1,0:T(8,128)S(1)} collective-permute-done((f32[304,128]{1,0:T(8,128)S(1)}, f32[304,128]{1,0:T(8,128)S(1)}, u32[]{:S(2)}, u32[]{:S(2)}) %collective-permute-start.7) | collective-permute-done | bytes 155680 | tf_op jit(solution)/shard_map/ppermute | solution.py:384
  107.1 2.5 %collective-permute-start.8 = (f32[304,128]{1,0:T(8,128)S(1)}, f32[304,128]{1,0:T(8,128)S(1)}, u32[]{:S(2)}, u32[]{:S(2)}) collective-permute-start(f32[304,128]{1,0:T(8,128)S(1)} %add.142), channel_id=1, source_target_pairs={{0,4},{1,5},{2,6},{3,7},{4,0},{5,1},{6,2},{7,3},{8,12},{9,13},{10,... | collective-permute-start | bytes 466952 | tf_op jit(solution)/shard_map/ppermute | solution.py:384
  109.6 4.7 %collective-permute-done.8 = f32[304,128]{1,0:T(8,128)S(1)} collective-permute-done((f32[304,128]{1,0:T(8,128)S(1)}, f32[304,128]{1,0:T(8,128)S(1)}, u32[]{:S(2)}, u32[]{:S(2)}) %collective-permute-start.8) | collective-permute-done | bytes 155680 | tf_op jit(solution)/shard_map/ppermute | solution.py:384
  114.3 3.8 %collective-permute-start.9 = (f32[304,128]{1,0:T(8,128)S(1)}, f32[304,128]{1,0:T(8,128)S(1)}, u32[]{:S(2)}, u32[]{:S(2)}) collective-permute-start(f32[304,128]{1,0:T(8,128)S(1)} %add.143), channel_id=1, source_target_pairs={{0,8},{1,9},{2,10},{3,11},{4,12},{5,13},{6,14},{7,15},{8,0},{9,1},... | collective-permute-start | bytes 466952 | tf_op jit(solution)/shard_map/ppermute | solution.py:384
  118.1 7.9 %collective-permute-done.9 = f32[304,128]{1,0:T(8,128)S(1)} collective-permute-done((f32[304,128]{1,0:T(8,128)S(1)}, f32[304,128]{1,0:T(8,128)S(1)}, u32[]{:S(2)}, u32[]{:S(2)}) %collective-permute-start.9) | collective-permute-done | bytes 155680 | tf_op jit(solution)/shard_map/ppermute | solution.py:384
  126.0 0.3 collective-permute-start.10
  126.2 8.9 %collective-permute-done.10 = f32[304,128]{1,0:T(8,128)S(1)} collective-permute-done((f32[304,128]{1,0:T(8,128)S(1)}, f32[304,128]{1,0:T(8,128)S(1)}, u32[]{:S(2)}, u32[]{:S(2)}) %collective-permute-start.10) | collective-permute-done | bytes 155680 | tf_op jit(solution)/shard_map/ppermute | solution.py:384
  135.2 1.4 collective-permute-done.11
  136.7 0.4 mul.75
  137.1 0.6 fusion.13
  137.6 0.9 copy.35
  138.5 0.9 copy.36
  139.5 0.1 mul.72
  139.7 0.3 add.151
  140.0 0.6 slice_bitcast_fusion
  140.6 0.9 compare_select_fusion.owner_ref
  141.5 1.3 copy-done
  142.8 10.6 %unpack.1 = f32[64,2,2,8,512]{4,3,2,1,0:T(8,128)} custom-call(bf16[1024,1024]{1,0:T(8,128)(2,1)} %bitcast.27, s32[1024,1]{1,0:T(8,128)} %compare_select_fusion.owner_ref), custom_call_target="tpu_custom_call" | custom-call | tf_op jit(solution)/shard_map/unpack/pallas_call | solution.py:340
  (66 shorter events, 1.5 us)
Async XLA Ops:
  9.0 26.8 %collective-permute-start.1 = (bf16[256,512]{1,0:T(8,128)(2,1)S(1)}, bf16[256,512]{1,0:T(8,128)(2,1)S(1)}, u32[]{:S(2)}, u32[]{:S(2)}) collective-permute-start(bf16[256,512]{1,0:T(8,128)(2,1)S(1)} %pad_maximum_fusion.2), channel_id=1, source_target_pairs={{4,0},{8,4},{12,8},{16,12},{20,16},{24,20},{28,24},{5,1},{9,5},{13... | collective-permute-start | bytes 786440 | tf_op jit(solution)/shard_map/ppermute | solution.py:426
  10.4 11.4 %copy-start.8 = (s32[2,32]{1,0:T(2,128)S(1)}, s32[2,32]{1,0:T(2,128)}, u32[]{:S(2)}) copy-start(s32[2,32]{1,0:T(2,128)} %param.12) | copy-start | bytes 772
  10.4 12.0 %copy-start.1 = (bf16[64,64,3,3]{1,0,3,2:T(8,128)(2,1)S(1)}, bf16[64,64,3,3]{1,0,3,2:T(8,128)(2,1)}, u32[]{:S(2)}) copy-start(bf16[64,64,3,3]{1,0,3,2:T(8,128)(2,1)} %param.9) | copy-start | bytes 221188
  10.4 12.4 %copy-start.5 = (bf16[64,64,3,3]{1,0,3,2:T(8,128)(2,1)S(1)}, bf16[64,64,3,3]{1,0,3,2:T(8,128)(2,1)}, u32[]{:S(2)}) copy-start(bf16[64,64,3,3]{1,0,3,2:T(8,128)(2,1)} %param.11) | copy-start | bytes 221188
  10.4 12.7 %copy-start.9 = (s32[2,32]{1,0:T(2,128)S(1)}, s32[2,32]{1,0:T(2,128)}, u32[]{:S(2)}) copy-start(s32[2,32]{1,0:T(2,128)} %param.13) | copy-start | bytes 772
  10.4 25.4 %collective-permute-start = (bf16[256,512]{1,0:T(8,128)(2,1)S(1)}, bf16[256,512]{1,0:T(8,128)(2,1)S(1)}, u32[]{:S(2)}, u32[]{:S(2)}) collective-permute-start(bf16[256,512]{1,0:T(8,128)(2,1)S(1)} %pad_maximum_fusion.1), channel_id=1, source_target_pairs={{0,4},{4,8},{8,12},{12,16},{16,20},{20,24},{24,28},{1,5},{5,9},{9,... | collective-permute-start | bytes 786440 | tf_op jit(solution)/shard_map/ppermute | solution.py:425
  18.9 13.3 %copy-start.10 = (f32[64]{0:T(128)S(1)}, f32[64]{0:T(128)}, u32[]{:S(2)}) copy-start(f32[64]{0:T(128)} %param.10) | copy-start | bytes 772
  18.9 6.4 %collective-permute-start.2 = (bf16[16,2048]{1,0:T(8,128)(2,1)}, bf16[16,2048]{1,0:T(8,128)(2,1)S(1)}, u32[]{:S(2)}, u32[]{:S(2)}) collective-permute-start(bf16[16,2048]{1,0:T(8,128)(2,1)} %get-tuple-element.15), channel_id=1, source_target_pairs={{0,1},{1,2},{2,3},{4,5},{5,6},{6,7},{8,9},{9,10},{10,11},{12,13},{... | collective-permute-start | bytes 196616 | tf_op jit(solution)/shard_map/ppermute | solution.py:422
  20.5 5.5 %collective-permute-start.3 = (bf16[16,2048]{1,0:T(8,128)(2,1)}, bf16[16,2048]{1,0:T(8,128)(2,1)S(1)}, u32[]{:S(2)}, u32[]{:S(2)}) collective-permute-start(bf16[16,2048]{1,0:T(8,128)(2,1)} %get-tuple-element.16), channel_id=1, source_target_pairs={{1,0},{2,1},{3,2},{5,4},{6,5},{7,6},{9,8},{10,9},{11,10},{13,12},{... | collective-permute-start | bytes 196616 | tf_op jit(solution)/shard_map/ppermute | solution.py:422
  26.0 10.6 %copy-start.2 = (bf16[16,2048]{1,0:T(8,128)(2,1)}, bf16[16,2048]{1,0:T(8,128)(2,1)S(1)}, u32[]{:S(2)}) copy-start(bf16[16,2048]{1,0:T(8,128)(2,1)S(1)} %add.125.side_ref) | copy-start | bytes 196612
  26.0 6.3 %collective-permute-start.4 = (bf16[16,128]{1,0:T(8,128)(2,1)S(1)}, bf16[16,128]{1,0:T(8,128)(2,1)S(1)}, u32[]{:S(2)}, u32[]{:S(2)}) collective-permute-start(bf16[16,128]{1,0:T(8,128)(2,1)S(1)} %get-tuple-element.40), channel_id=1, source_target_pairs={{0,4},{4,8},{8,12},{12,16},{16,20},{20,24},{24,28},{1,5},{5,9},{9,... | collective-permute-start | bytes 12296 | tf_op jit(solution)/shard_map/ppermute | solution.py:427
  30.3 5.5 %collective-permute-start.5 = (bf16[16,128]{1,0:T(8,128)(2,1)S(1)}, bf16[16,128]{1,0:T(8,128)(2,1)S(1)}, u32[]{:S(2)}, u32[]{:S(2)}) collective-permute-start(bf16[16,128]{1,0:T(8,128)(2,1)S(1)} %get-tuple-element.39), channel_id=1, source_target_pairs={{4,0},{8,4},{12,8},{16,12},{20,16},{24,20},{28,24},{5,1},{9,5},{13... | collective-permute-start | bytes 12296 | tf_op jit(solution)/shard_map/ppermute | solution.py:428
  32.3 4.3 %copy-start.6 = (bf16[16,128]{1,0:T(8,128)(2,1)}, bf16[16,128]{1,0:T(8,128)(2,1)S(1)}, u32[]{:S(2)}) copy-start(bf16[16,128]{1,0:T(8,128)(2,1)S(1)} %collective-permute-done.4.side_up_ref) | copy-start | bytes 12292
  35.8 0.8 copy-start.7
  35.8 0.8 copy-start.3
  35.8 0.8 copy-start.4
  68.4 73.1 %all-to-all-start = ((bf16[32,32,1024]{2,1,0:T(8,128)(2,1)}), bf16[32,32,1024]{2,1,0:T(8,128)(2,1)S(1)}, u32[]{:S(2)}, u32[]{:S(2)}) async-start(bf16[32,32,1024]{2,1,0:T(8,128)(2,1)} %bitcast.30), calls=%async_computation | async-start | bytes 4194304 | tf_op jit(solution)/shard_map/all_to_all | solution.py:444
  98.3 1.4 collective-permute-start.6
  99.8 7.3 %collective-permute-start.7 = (f32[304,128]{1,0:T(8,128)S(1)}, f32[304,128]{1,0:T(8,128)S(1)}, u32[]{:S(2)}, u32[]{:S(2)}) collective-permute-start(f32[304,128]{1,0:T(8,128)S(1)} %bitcast_add_fusion), channel_id=1, source_target_pairs={{0,2},{1,3},{2,0},{3,1},{4,6},{5,7},{6,4},{7,5},{8,10},{9,11},{10,... | collective-permute-start | bytes 466952 | tf_op jit(solution)/shard_map/ppermute | solution.py:384
  107.1 7.1 %collective-permute-start.8 = (f32[304,128]{1,0:T(8,128)S(1)}, f32[304,128]{1,0:T(8,128)S(1)}, u32[]{:S(2)}, u32[]{:S(2)}) collective-permute-start(f32[304,128]{1,0:T(8,128)S(1)} %add.142), channel_id=1, source_target_pairs={{0,4},{1,5},{2,6},{3,7},{4,0},{5,1},{6,2},{7,3},{8,12},{9,13},{10,... | collective-permute-start | bytes 466952 | tf_op jit(solution)/shard_map/ppermute | solution.py:384
  114.3 11.7 %collective-permute-start.9 = (f32[304,128]{1,0:T(8,128)S(1)}, f32[304,128]{1,0:T(8,128)S(1)}, u32[]{:S(2)}, u32[]{:S(2)}) collective-permute-start(f32[304,128]{1,0:T(8,128)S(1)} %add.143), channel_id=1, source_target_pairs={{0,8},{1,9},{2,10},{3,11},{4,12},{5,13},{6,14},{7,15},{8,0},{9,1},... | collective-permute-start | bytes 466952 | tf_op jit(solution)/shard_map/ppermute | solution.py:384
  126.0 9.2 %collective-permute-start.10 = (f32[304,128]{1,0:T(8,128)S(1)}, f32[304,128]{1,0:T(8,128)S(1)}, u32[]{:S(2)}, u32[]{:S(2)}) collective-permute-start(f32[304,128]{1,0:T(8,128)S(1)} %add.144), channel_id=1, source_target_pairs={{0,16},{1,17},{2,18},{3,19},{4,20},{5,21},{6,22},{7,23},{8,24},{9,... | collective-permute-start | bytes 466952 | tf_op jit(solution)/shard_map/ppermute | solution.py:384
  135.2 1.4 collective-permute-start.11
  141.5 1.3 copy-start

commit v2 on v0

v2 whole, which is shorter than its diff:
```python
import functools
import math

import jax
import jax.numpy as jnp
from jax import lax
from jax.experimental import pallas as pl
from jax.experimental.pallas import tpu as pltpu
from jax.sharding import PartitionSpec as P

BLOCK = 16
CAP = 2
AXES = ("rows", "cols")
BF16 = jnp.bfloat16
F32 = jnp.float32
NT = (((1,), (1,)), ((), ()))
TN = (((0,), (0,)), ((), ()))
VMEM_BYTES = 60 * 2**20


def params(**extra):
    return pltpu.CompilerParams(vmem_limit_bytes=VMEM_BYTES, **extra)


def sigmoid(value):
    return 0.5 * jnp.tanh(0.5 * value) + 0.5


def one_hot(shape, pairs):
    row = lax.broadcasted_iota(jnp.int32, shape, 0)
    col = lax.broadcasted_iota(jnp.int32, shape, 1)
    hit = jnp.zeros(shape, jnp.bool_)
    for at_row, at_col in pairs:
        hit = hit | ((row == at_row) & (col == at_col))
    return hit.astype(F32).astype(BF16)


def shifted(value):
    wide = value.shape[1]
    return (
        pltpu.roll(value, 1, 1).astype(BF16),
        value.astype(BF16),
        pltpu.roll(value, wide - 1, 1).astype(BF16),
    )


def slope_of(value, sigma):
    return sigma * (1.0 + value * (1.0 - sigma))


def at_row(row, rows, channels):
    return pl.ds(pl.multiple_of(row * channels, channels), rows * channels)


def reorder_kernel(w_ref, c_ref, xw_ref, xc_ref, to_right_ref, to_left_ref, to_up_ref, to_down_ref):
    channels, rows, lanes = w_ref.shape
    rim = 2 * channels
    kept = []
    for source, target in ((w_ref, xw_ref), (c_ref, xc_ref)):
        value = source[...].astype(F32)
        swapped = jnp.swapaxes(value, 0, 1).reshape(rows * channels, lanes).astype(BF16)
        target[...] = swapped
        kept.append(swapped)

    @pl.when(pl.program_id(1) == 0)
    def _():
        to_up_ref[0:rim, :] = kept[0][0:rim]
        to_up_ref[rim:, :] = kept[1][0:rim]

    @pl.when(pl.program_id(1) == pl.num_programs(1) - 1)
    def _():
        to_down_ref[0:rim, :] = kept[0][rows * channels - rim :]
        to_down_ref[rim:, :] = kept[1][rows * channels - rim :]

    here = pl.ds(pl.multiple_of(pl.program_id(1) * rows * channels, 128), rows * channels)

    def pick(tile, w_pairs, c_pairs):
        return sum(
            lax.dot_general(
                one_hot((16, 128), pairs), value[:, tile], NT, preferred_element_type=F32
            )
            for value, pairs in zip(kept, (w_pairs, c_pairs))
        ).astype(BF16)

    @pl.when(pl.program_id(0) == pl.num_programs(0) - 1)
    def _():
        final = slice(lanes - 128, lanes)
        to_right_ref[:, here] = pick(final, ((0, 126), (1, 127)), ((2, 126), (3, 127)))

    @pl.when(pl.program_id(0) == 0)
    def _():
        to_left_ref[:, here] = pick(slice(0, 128), ((4, 0), (5, 1)), ((6, 0), (7, 1)))


def reorder(warped, cotangent):
    channels, height, breadth = warped.shape
    step = 16
    lanes = 256
    spec_in = pl.BlockSpec((channels, step, lanes), lambda x, h: (0, h, x))
    spec_out = pl.BlockSpec((step * channels, lanes), lambda x, h: (h, x))
    spec_edge = pl.BlockSpec((16, height * channels), lambda x, h: (0, 0))
    spec_rim = pl.BlockSpec((4 * channels, lanes), lambda x, h: (0, x))
    shape = jax.ShapeDtypeStruct((height * channels, breadth), BF16)
    edge = jax.ShapeDtypeStruct((16, height * channels), BF16)
    rim = jax.ShapeDtypeStruct((4 * channels, breadth), BF16)
    return pl.pallas_call(
        reorder_kernel,
        grid=(breadth // lanes, height // step),
        in_specs=[spec_in, spec_in],
        out_specs=[spec_out, spec_out, spec_edge, spec_edge, spec_rim, spec_rim],
        out_shape=[shape, shape, edge, edge, rim, rim],
        compiler_params=params(),
        name="reorder",
    )(warped, cotangent)


def spread_sides(side, first):
    spread = one_hot((16, 128), ((first, 126), (first + 1, 127), (first + 4, 0), (first + 5, 1)))
    return lax.dot_general(side, spread, TN, preferred_element_type=F32).astype(BF16)


def lane_mask(flags_ref, lane, breadth):
    wide = breadth + 128
    return (
        (lane < breadth)
        | ((lane == breadth) & (flags_ref[3] == 1))
        | ((lane == wide - 1) & (flags_ref[2] == 1))
    )


def middle_step(w1_ref, w2f_ref, bias_ref, value, cot, act_window, cot_window):
    conv = jnp.dot(w1_ref[...], act_window, preferred_element_type=F32)
    back = jnp.dot(w2f_ref[...], cot_window, preferred_element_type=F32)
    a_mid = (value.astype(F32) + conv + bias_ref[:, 0:1]).astype(BF16).astype(F32)
    sigma = sigmoid(a_mid)
    return a_mid * sigma, cot.astype(F32) + slope_of(a_mid, sigma) * back


def rim_masked(value, rim_ok, breadth):
    return jnp.concatenate(
        [value[:, :breadth], jnp.where(rim_ok, value[:, breadth:], 0.0)], axis=1
    )


def chosen_blocks(target_ref, band, start, size, breadth):
    row_at = lax.broadcasted_iota(jnp.int32, (size, breadth), 0) + start
    return (row_at == target_ref[band : band + 1, :]).astype(F32).astype(BF16)


def inner_kernel(
    channels, height, breadth,
    flags_ref, xw_ref, xc_ref, side_ref, w1_ref, w2f_ref, w1f_ref, bias_ref, target_ref,
    packed_ref, act_in_ref, act_mid_ref, g_ref, gw_mid_ref,
    wx, cx, sa, sc, sg, gw, act_in, act_mid, grads, packed, sem_in, sem_out,
):
    ch = channels
    wide = breadth + 128
    core = slice(0, breadth)
    rim = slice(breadth, wide)
    loads = [
        pltpu.make_async_copy(xw_ref, wx.at[:, core], sem_in.at[0]),
        pltpu.make_async_copy(xc_ref, cx.at[:, core], sem_in.at[1]),
    ]
    stores = [
        pltpu.make_async_copy(act_in, act_in_ref.at[ch : ch + height * ch, :], sem_out.at[0]),
        pltpu.make_async_copy(act_mid, act_mid_ref.at[2 * ch : height * ch, :], sem_out.at[1]),
        pltpu.make_async_copy(grads, g_ref.at[ch : (height - 1) * ch, :], sem_out.at[2]),
        pltpu.make_async_copy(packed, packed_ref.at[:, 2 * ch : (BLOCK - 2) * ch], sem_out.at[3]),
        pltpu.make_async_copy(
            gw.at[(BLOCK - 2) * ch : (BLOCK + 2) * ch, :], gw_mid_ref, sem_out.at[4]
        ),
    ]
    for load in loads:
        load.start()
    wx[:, rim] = spread_sides(side_ref[...], 0)
    cx[:, rim] = spread_sides(side_ref[...], 2)
    for load in loads:
        load.wait()

    def prepare(row, _):
        here = at_row(row, 1, ch)
        out = pl.multiple_of(row * 3 * ch, ch)
        value = wx[here, :].astype(F32)
        moved = shifted(value * sigmoid(value))
        act_in[here, :] = moved[1]
        for shift in range(3):
            sa[pl.ds(out + shift * ch, ch), :] = moved[shift]
        moved = shifted(cx[here, :].astype(F32))
        for shift in range(3):
            sc[pl.ds(out + shift * ch, ch), :] = moved[shift]
        return 0

    lax.fori_loop(0, height, prepare, 0, unroll=UNROLL_PREPARE)
    stores[0].start()
    lane = lax.broadcasted_iota(jnp.int32, (2 * ch, 128), 1) + breadth
    rim_ok = lane_mask(flags_ref, lane, breadth)

    def middle(pair, _):
        row = pair * 2
        window = at_row(row * 3, 12, ch)
        here = at_row(row + 1, 2, ch)
        act, grad = middle_step(
            w1_ref, w2f_ref, bias_ref, wx[here, :], cx[here, :], sa[window, :], sc[window, :]
        )
        out = at_row(row, 2, ch)
        act_mid[out, :] = rim_masked(act, rim_ok, breadth).astype(BF16)
        moved = shifted(rim_masked(grad, rim_ok, breadth))
        grads[out, :] = moved[1]
        for shift in range(3):
            sg[at_row(row * 3 + shift, 1, ch), :] = moved[shift][:ch]
            sg[at_row(row * 3 + 3 + shift, 1, ch), :] = moved[shift][ch:]
        return 0

    lax.fori_loop(0, height // 2 - 1, middle, 0, unroll=UNROLL_MIDDLE)
    stores[1].start()
    stores[2].start()

    def last(pair, _):
        row = pair * 2
        back = jnp.dot(w1f_ref[...], sg[at_row(row * 3, 12, ch), core], preferred_element_type=F32)
        here = at_row(row + 2, 2, ch)
        value = wx[here, core].astype(F32)
        mid = grads[at_row(row + 1, 2, ch), core].astype(F32)
        gw[here, :] = (mid + slope_of(value, sigmoid(value)) * back).astype(BF16)
        return 0

    lax.fori_loop(0, height // 2 - 2, last, 0, unroll=UNROLL_LAST)
    stores[4].start()

    size = 256
    strip = BLOCK * ch

    def pack(part, _):
        start = pl.multiple_of(part * size, size)
        total = None
        for band in range(height // BLOCK):
            chosen = chosen_blocks(target_ref, band, start, size, breadth)
            rows = slice(band * strip + 2 * ch, (band + 1) * strip - 2 * ch)
            term = lax.dot_general(chosen, gw[rows, :], NT, preferred_element_type=F32)
            total = term if total is None else total + term
        packed[pl.ds(start, size), :] = total.astype(BF16)
        return 0

    lax.fori_loop(0, packed.shape[0] // size, pack, 0)
    stores[3].start()
    for store in stores:
        store.wait()


UNROLL_PREPARE = 8
UNROLL_MIDDLE = 5
UNROLL_LAST = 7


def inner(sizes, flags, operands, slots):
    channels, height, breadth = sizes
    wide = breadth + 128
    vmem = pl.BlockSpec(memory_space=pltpu.VMEM)
    hbm = pl.BlockSpec(memory_space=pl.ANY)
    outs = [
        jax.ShapeDtypeStruct((slots * BLOCK, BLOCK * channels), BF16),
        jax.ShapeDtypeStruct(((height + 2) * channels, wide), BF16),
        jax.ShapeDtypeStruct(((height + 2) * channels, wide), BF16),
        jax.ShapeDtypeStruct((height * channels, wide), BF16),
        jax.ShapeDtypeStruct((4 * channels, breadth), BF16),
    ]
    flops = 2 * 3 * 12 * channels * 2 * channels * wide * (height // 2)
    return pl.pallas_call(
        functools.partial(inner_kernel, channels, height, breadth),
        in_specs=[pl.BlockSpec(memory_space=pltpu.SMEM), hbm, hbm] + [vmem] * (len(operands) - 2),
        out_specs=[hbm] * len(outs),
        out_shape=outs,
        scratch_shapes=[
            pltpu.VMEM((height * channels, wide), BF16),
            pltpu.VMEM((height * channels, wide), BF16),
            pltpu.VMEM((height * 3 * channels, wide), BF16),
            pltpu.VMEM((height * 3 * channels, wide), BF16),
            pltpu.VMEM(((height - 2) * 3 * channels, wide), BF16),
            pltpu.VMEM((height * channels, breadth), BF16),
            pltpu.VMEM((height * channels, wide), BF16),
            pltpu.VMEM(((height - 2) * channels, wide), BF16),
            pltpu.VMEM(((height - 2) * channels, wide), BF16),
            pltpu.VMEM((slots * BLOCK, (BLOCK - 4) * channels), BF16),
            pltpu.SemaphoreType.DMA((2,)),
            pltpu.SemaphoreType.DMA((5,)),
        ],
        compiler_params=params(),
        cost_estimate=pl.CostEstimate(flops=flops, bytes_accessed=2 * 10**7, transcendentals=10**6),
        name="inner",
    )(flags, *operands)


def outer_kernel(
    channels, height, breadth,
    flags_ref, xw_ref, xc_ref, up_ref, down_ref, side_ref, side_up_ref, side_down_ref,
    w1_ref, w2f_ref, w1f_ref, bias_ref, target_ref, gw_mid_ref,
    packed_in, act_in_in, act_mid_in, g_in,
    packed_ref, act_in_ref, act_mid_ref, g_ref,
    wx, cx, sa, sc, sg, near, gw, act_in, act_mid, grads, packed, sem_in, sem_out,
):
    ch = channels
    wide = breadth + 128
    core = slice(0, breadth)
    rim = slice(breadth, wide)
    body = height * ch
    rows2 = 2 * ch
    loads = []

    def load(source, target):
        copy = pltpu.make_async_copy(source, target, sem_in.at[len(loads)])
        copy.start()
        loads.append(copy)

    load(xw_ref.at[0:rows2, :], wx.at[rows2 : 2 * rows2, core])
    load(xc_ref.at[0:rows2, :], cx.at[rows2 : 2 * rows2, core])
    load(xw_ref.at[body - rows2 : body, :], wx.at[2 * rows2 : 3 * rows2, core])
    load(xc_ref.at[body - rows2 : body, :], cx.at[2 * rows2 : 3 * rows2, core])
    load(up_ref.at[0:rows2, :], wx.at[0:rows2, core])
    load(up_ref.at[rows2 : 2 * rows2, :], cx.at[0:rows2, core])
    load(down_ref.at[0:rows2, :], wx.at[3 * rows2 : 4 * rows2, core])
    load(down_ref.at[rows2 : 2 * rows2, :], cx.at[3 * rows2 : 4 * rows2, core])
    load(g_in.at[ch : 3 * ch, :], near.at[0:rows2, :])
    load(g_in.at[body - 3 * ch : body - ch, :], near.at[rows2 : 2 * rows2, :])
    for target, first in ((wx, 0), (cx, 2)):
        target[0:rows2, rim] = spread_sides(side_up_ref[...], first)
        target[rows2 : 2 * rows2, rim] = spread_sides(side_ref[:, 0:rows2], first)
        target[2 * rows2 : 3 * rows2, rim] = spread_sides(side_ref[:, body - rows2 : body], first)
        target[3 * rows2 : 4 * rows2, rim] = spread_sides(side_down_ref[...], first)
    for copy in loads:
        copy.wait()
    lane = lax.broadcasted_iota(jnp.int32, (2 * ch, 128), 1) + breadth
    rim_ok = lane_mask(flags_ref, lane, breadth)
    sub = lax.broadcasted_iota(jnp.int32, (2 * ch, wide), 0)

    for half in range(2):
        base = half * 2 * rows2
        for row in range(4):
            here = slice(base + row * ch, base + (row + 1) * ch)
            value = wx[here, :].astype(F32)
            moved = shifted(value * sigmoid(value))
            if row == 1 + half:
                act_in[half * ch : (half + 1) * ch, :] = moved[1]
            for shift in range(3):
                sa[(row * 3 + shift) * ch : (row * 3 + shift + 1) * ch, :] = moved[shift]
            moved = shifted(cx[here, :].astype(F32))
            for shift in range(3):
                sc[(row * 3 + shift) * ch : (row * 3 + shift + 1) * ch, :] = moved[shift]
        here = slice(base + ch, base + 3 * ch)
        act, grad = middle_step(
            w1_ref, w2f_ref, bias_ref, wx[here, :], cx[here, :], sa[...], sc[...]
        )
        good = ((sub >= ch) if half == 0 else (sub < ch)) | (flags_ref[half] == 1)
        act = jnp.where(good, rim_masked(act, rim_ok, breadth), 0.0)
        grad = jnp.where(good, rim_masked(grad, rim_ok, breadth), 0.0)
        act_mid[half * rows2 : (half + 1) * rows2, :] = act.astype(BF16)
        mine = shifted(grad)
        other = shifted(near[half * rows2 : (half + 1) * rows2, :].astype(F32))
        own = mine[1][ch:] if half == 0 else mine[1][:ch]
        grads[half * ch : (half + 1) * ch, :] = own
        order = (mine, other) if half == 0 else (other, mine)
        for pair in range(2):
            for row in range(2):
                for shift in range(3):
                    out = ((pair * 2 + row) * 3 + shift) * ch
                    sg[out : out + ch, :] = order[pair][shift][row * ch : (row + 1) * ch]
        back = jnp.dot(w1f_ref[...], sg[:, core], preferred_element_type=F32)
        inside = slice(rows2, 2 * rows2) if half == 0 else slice(2 * rows2, 3 * rows2)
        value = wx[inside, core].astype(F32)
        mid = jnp.concatenate([order[0][1][ch:, core], order[1][1][:ch, core]], axis=0).astype(F32)
        gw[half * rows2 : (half + 1) * rows2, :] = (
            mid + slope_of(value, sigmoid(value)) * back
        ).astype(BF16)

    stores = [
        (act_in.at[0:ch, :], act_in_ref.at[0:ch, :]),
        (act_in.at[ch : 2 * ch, :], act_in_ref.at[body + ch : body + 2 * ch, :]),
        (act_mid.at[0:rows2, :], act_mid_ref.at[0:rows2, :]),
        (act_mid.at[rows2 : 2 * rows2, :], act_mid_ref.at[body : body + 2 * ch, :]),
        (grads.at[0:ch, :], g_ref.at[0:ch, :]),
        (grads.at[ch : 2 * ch, :], g_ref.at[body - ch : body, :]),
        (packed.at[:, 0:rows2], packed_ref.at[:, 0:rows2]),
        (packed.at[:, rows2 : 2 * rows2], packed_ref.at[:, (BLOCK - 2) * ch : BLOCK * ch]),
    ]
    stores = [
        pltpu.make_async_copy(source, target, sem_out.at[at])
        for at, (source, target) in enumerate(stores)
    ]
    for store in stores[:6]:
        store.start()
    first = jnp.concatenate([gw[0:rows2, :], gw_mid_ref[0:rows2, :]], axis=0)
    second = jnp.concatenate([gw_mid_ref[rows2 : 2 * rows2, :], gw[rows2 : 2 * rows2, :]], axis=0)
    size = 256

    def pack(part, _):
        start = pl.multiple_of(part * size, size)
        total = sum(
            lax.dot_general(
                chosen_blocks(target_ref, band, start, size, breadth),
                rows,
                NT,
                preferred_element_type=F32,
            )
            for band, rows in enumerate((first, second))
        )
        packed[pl.ds(start, size), :] = total.astype(BF16)
        return 0

    lax.fori_loop(0, packed.shape[0] // size, pack, 0)
    for store in stores[6:]:
        store.start()
    for store in stores:
        store.wait()


def outer(sizes, flags, operands, state, slots):
    channels, height, breadth = sizes
    wide = breadth + 128
    vmem = pl.BlockSpec(memory_space=pltpu.VMEM)
    hbm = pl.BlockSpec(memory_space=pl.ANY)
    inputs = 1 + len(operands)
    return pl.pallas_call(
        functools.partial(outer_kernel, channels, height, breadth),
        in_specs=[pl.BlockSpec(memory_space=pltpu.SMEM)]
        + [hbm] * 4
        + [vmem] * (len(operands) - 4)
        + [hbm] * len(state),
        out_specs=[hbm] * len(state),
        out_shape=[jax.ShapeDtypeStruct(item.shape, item.dtype) for item in state],
        input_output_aliases={inputs + at: at for at in range(len(state))},
        scratch_shapes=[
            pltpu.VMEM((8 * channels, wide), BF16),
            pltpu.VMEM((8 * channels, wide), BF16),
            pltpu.VMEM((12 * channels, wide), BF16),
            pltpu.VMEM((12 * channels, wide), BF16),
            pltpu.VMEM((12 * channels, wide), BF16),
            pltpu.VMEM((4 * channels, wide), BF16),
            pltpu.VMEM((4 * channels, breadth), BF16),
            pltpu.VMEM((2 * channels, wide), BF16),
            pltpu.VMEM((4 * channels, wide), BF16),
            pltpu.VMEM((2 * channels, wide), BF16),
            pltpu.VMEM((slots * BLOCK, 4 * channels), BF16),
            pltpu.SemaphoreType.DMA((10,)),
            pltpu.SemaphoreType.DMA((8,)),
        ],
        compiler_params=params(),
        name="outer",
    )(flags, *operands, *state)


def correlate_kernel(
    channels, height, breadth,
    act_in_ref, act_mid_ref, g_ref, xc_ref, out_ref,
    image1, image2, g, c, s1, s2, acc1, acc2, sum1, sum2, sem,
):
    ch = channels
    wide = breadth + 128
    core = slice(0, breadth)
    loads = [
        pltpu.make_async_copy(source, target, sem.at[at])
        for at, (source, target) in enumerate(
            ((g_ref.at[:, core], g), (xc_ref, c), (act_in_ref, image1), (act_mid_ref, image2))
        )
    ]
    for load in loads:
        load.start()
    for ref in (acc1, acc2, sum1, sum2):
        ref[...] = jnp.zeros_like(ref)
    empty = jnp.zeros((ch, wide - breadth), F32)

    def prepare(row, source, target, total):
        value = source[at_row(row, 1, ch), :].astype(F32)
        total[...] += value
        right, here, left = shifted(jnp.concatenate([value, empty], axis=1))
        for shift, moved in enumerate((left, here, right)):
            target[at_row(row * 3 + shift, 1, ch), :] = moved

    def add(pair, image, grads, acc):
        acc[...] += lax.dot_general(
            grads[at_row(pair * 6, 6, ch), :],
            image[at_row(pair * 2, 4, ch), :],
            NT,
            preferred_element_type=F32,
        )

    loads[0].wait()
    loads[1].wait()

    def step(row, _):
        prepare(row, g, s1, sum1)
        prepare(row, c, s2, sum2)
        return 0

    def products(pair, _):
        add(pair, image1, s1, acc1)
        add(pair, image2, s2, acc2)
        return 0

    lax.fori_loop(0, height, step, 0, unroll=4)
    loads[2].wait()
    loads[3].wait()
    lax.fori_loop(0, height // 2, products, 0, unroll=4)

    first, second = (
        acc[0 : 3 * ch, :] + pltpu.roll(acc[3 * ch : 6 * ch, :], 3 * ch, 1) for acc in (acc1, acc2)
    )
    second = pltpu.roll(second, ch, 1)
    low = lax.broadcasted_iota(jnp.int32, (3 * ch, 128), 1) < ch
    out_ref[0 : 3 * ch, :] = first[:, 0:128]
    out_ref[3 * ch : 6 * ch, :] = jnp.where(low, first[:, 128:256], second[:, 0:128])
    out_ref[6 * ch : 9 * ch, :] = second[:, 128:256]
    sums = jnp.concatenate(
        [jnp.sum(total[...], axis=1, keepdims=True) for total in (sum1, sum2)], axis=0
    )
    out_ref[9 * ch :, :] = jnp.broadcast_to(sums, (2 * ch, 2 * ch)).T[0:8, :]


def correlate(sizes, act_in, act_mid, g_mid, xc):
    channels, height, breadth = sizes
    wide = breadth + 128
    hbm = pl.BlockSpec(memory_space=pl.ANY)
    flops = 2 * 2 * 12 * channels * 2 * channels * breadth * (height // 2)
    return pl.pallas_call(
        functools.partial(correlate_kernel, channels, height, breadth),
        in_specs=[hbm] * 4,
        out_specs=pl.BlockSpec(memory_space=pltpu.VMEM),
        out_shape=jax.ShapeDtypeStruct((9 * channels + 8, 2 * channels), F32),
        scratch_shapes=[
            pltpu.VMEM(((height + 2) * channels, wide), BF16),
            pltpu.VMEM(((height + 2) * channels, wide), BF16),
            pltpu.VMEM((height * channels, breadth), BF16),
            pltpu.VMEM((height * channels, breadth), BF16),
            pltpu.VMEM((height * 3 * channels, wide), BF16),
            pltpu.VMEM((height * 3 * channels, wide), BF16),
            pltpu.VMEM((6 * channels, 4 * channels), F32),
            pltpu.VMEM((6 * channels, 4 * channels), F32),
            pltpu.VMEM((channels, breadth), F32),
            pltpu.VMEM((channels, breadth), F32),
            pltpu.SemaphoreType.DMA((4,)),
        ],
        compiler_params=params(),
        cost_estimate=pl.CostEstimate(flops=flops, bytes_accessed=10**7, transcendentals=0),
        name="correlate",
    )(act_in, act_mid, g_mid, xc)


def unpack_kernel(channels, devices, me_ref, table_ref, arrived_ref, out_ref, chosen):
    block_rows, part, breadth = out_ref.shape[1], out_ref.shape[3], out_ref.shape[4]

    @pl.when(pl.program_id(0) == 0)
    def _():
        shape = (CAP * BLOCK, block_rows * breadth)
        sub = lax.broadcasted_iota(jnp.int32, shape, 0)
        place = lax.broadcasted_iota(jnp.int32, shape, 1) - sub % BLOCK
        second = sub >= BLOCK

        def select(source, _):
            at = (source * devices + me_ref[0]) * CAP
            owners = [
                table_ref[(at + rank) // 128, (at + rank) % 128] * BLOCK for rank in range(CAP)
            ]
            wanted = jnp.where(second, owners[1], owners[0])
            chosen[pl.ds(pl.multiple_of(source * CAP * BLOCK, CAP * BLOCK), CAP * BLOCK), :] = (
                (place == wanted).astype(F32).astype(BF16)
            )
            return 0

        lax.fori_loop(0, devices, select, 0, unroll=4)

    flat = arrived_ref[...].T
    for band in range(block_rows):
        summed = jnp.dot(
            flat, chosen[:, band * breadth : (band + 1) * breadth], preferred_element_type=F32
        )
        cube = summed.reshape(part, channels, breadth)
        out_ref[:, band, 0, :, :] = jnp.swapaxes(cube, 0, 1)


def unpack(sizes, me, table, arrived, devices):
    channels, height, breadth = sizes
    block_rows = height // BLOCK
    rows = arrived.shape[0]
    part = 8
    smem = pl.BlockSpec(memory_space=pltpu.SMEM)
    return pl.pallas_call(
        functools.partial(unpack_kernel, channels, devices),
        grid=(BLOCK // part,),
        in_specs=[smem, smem, pl.BlockSpec((rows, part * channels), lambda h: (0, h))],
        out_specs=pl.BlockSpec((channels, block_rows, 1, part, breadth), lambda h: (0, 0, h, 0, 0)),
        out_shape=jax.ShapeDtypeStruct((channels, block_rows, BLOCK // part, part, breadth), F32),
        scratch_shapes=[pltpu.VMEM((rows, block_rows * breadth), BF16)],
        compiler_params=params(),
        name="unpack",
    )(me, table, arrived)


def pair_weights(kernel):
    taps = jnp.transpose(kernel, (0, 2, 3, 1)).reshape(kernel.shape[0], -1)
    third = taps.shape[1] // 3
    return jnp.concatenate(
        [jnp.pad(taps, ((0, 0), (0, third))), jnp.pad(taps, ((0, 0), (third, 0)))], axis=0
    )


def flipped(kernel):
    return jnp.transpose(kernel[:, :, ::-1, ::-1], (1, 0, 2, 3))


def shift_pairs(axis, step):
    count = lax.axis_size(axis)
    return [(i, i + step) for i in range(count) if 0 <= i + step < count]


def total_over_devices(terms, devices):
    me = lax.axis_index(AXES)
    swap = lambda value, step: lax.ppermute(value, AXES, [(i, i ^ step) for i in range(devices)])
    total = terms
    for step in (1, 2):
        bit = (me // step) % 2
        half = total.shape[0] // 2
        mine = lax.dynamic_slice_in_dim(total, bit * half, half, 0)
        away = lax.dynamic_slice_in_dim(total, (1 - bit) * half, half, 0)
        total = mine + swap(away, step)
    step = 4
    while step < devices:
        total = total + swap(total, step)
        step *= 2
    for step in (2, 1):
        bit = (me // step) % 2
        other = swap(total, step)
        total = jnp.concatenate(
            [jnp.where(bit == 0, total, other), jnp.where(bit == 0, other, total)], axis=0
        )
    return total


def body(warped, cotangent, w_first, b_first, w_second, source_tile, source_block):
    sizes = warped.shape
    channels, height, breadth = sizes
    row_count = lax.axis_size("rows")
    col_count = lax.axis_size("cols")
    devices = row_count * col_count
    slots = devices * CAP
    factor = 1.0 / math.sqrt(height * row_count * breadth * col_count)
    row_at = lax.axis_index("rows")
    col_at = lax.axis_index("cols")
    me = lax.axis_index(AXES)

    block_rows = height // BLOCK
    count = source_tile.size
    target = source_tile.reshape(count)
    same = target[:, None] == target[None, :]
    earlier = jnp.arange(count)[None, :] < jnp.arange(count)[:, None]
    ranking = jnp.sum((same & earlier).astype(jnp.int32), axis=1)
    places = target * CAP + ranking
    target_row = (
        places.reshape(block_rows, -1, 1) * BLOCK + jnp.arange(BLOCK, dtype=jnp.int32)
    ).reshape(block_rows, breadth)
    hits = places[:, None] == jnp.arange(slots, dtype=jnp.int32)[None, :]
    labels = jnp.sum(jnp.where(hits, source_block.reshape(count, 1) + 1, 0), axis=0) - 1

    xw, xc, to_right, to_left, to_up, to_down = reorder(warped, cotangent)
    rim = 2 * channels
    side = lax.ppermute(to_right, "cols", shift_pairs("cols", 1)) + lax.ppermute(
        to_left, "cols", shift_pairs("cols", -1)
    )
    up = lax.ppermute(to_down, "rows", shift_pairs("rows", 1))
    down = lax.ppermute(to_up, "rows", shift_pairs("rows", -1))
    side_up = lax.ppermute(side[:, -rim:], "rows", shift_pairs("rows", 1))
    side_down = lax.ppermute(side[:, :rim], "rows", shift_pairs("rows", -1))

    flags = jnp.stack(
        [row_at > 0, row_at < row_count - 1, col_at > 0, col_at < col_count - 1]
    ).astype(jnp.int32)
    bias = jnp.broadcast_to(jnp.tile(b_first, 2)[:, None], (2 * channels, 128))
    first = pair_weights(w_first)
    second_back = pair_weights(flipped(w_second))
    first_back = pair_weights(flipped(w_first))
    *state, gw_mid = inner(
        sizes, flags, (xw, xc, side, first, second_back, first_back, bias, target_row), slots
    )
    packed, act_in, act_mid, g_mid = outer(
        sizes,
        flags,
        (
            xw, xc, up, down, side, side_up, side_down,
            first, second_back, first_back, bias, target_row, gw_mid,
        ),
        state,
        slots,
    )
    arrived = lax.all_to_all(
        packed.reshape(devices, CAP * BLOCK, BLOCK * channels),
        AXES,
        split_axis=0,
        concat_axis=0,
        tiled=True,
    )

    terms = correlate(sizes, act_in, act_mid, g_mid, xc)
    mine = jnp.arange(devices, dtype=jnp.int32)[:, None] == me
    table = jnp.where(mine, labels.astype(F32)[None, :], 0.0).reshape(-1, 128)
    used = terms.shape[0] + table.shape[0]
    fill = jnp.zeros((-used % 32, 128), F32)
    summed = total_over_devices(jnp.concatenate([terms, table, fill], axis=0), devices)
    owners = summed[terms.shape[0] : used].astype(jnp.int32)
    frame = unpack(
        sizes, me.reshape(1), owners, arrived.reshape(slots * BLOCK, BLOCK * channels), devices
    )
    tiles = summed[: 9 * channels].reshape(3, 3 * channels, 128)
    taps = (
        jnp.concatenate([tiles[0], tiles[1], tiles[2]], axis=1)
        .reshape(3, channels, 2, 3, channels)
        .transpose(2, 1, 4, 3, 0)
        * factor
    )
    biases = summed[9 * channels].reshape(2, channels) * factor
    return (frame.reshape(sizes), taps[0], biases[0], taps[1], biases[1])


def solution(mesh):
    in_specs = (
        P(None, "rows", "cols"),
        P(None, "rows", "cols"),
        P(),
        P(),
        P(),
        P("rows", "cols"),
        P("rows", "cols"),
    )
    out_specs = (P(None, "rows", "cols"), P(), P(), P(), P())
    return jax.shard_map(body, mesh=mesh, in_specs=in_specs, out_specs=out_specs, check_vma=False)
```

time: 545 us -> 135 us (0.25); the launches traced: 537 us -> 134 us
  local copies, waits for them, and re-layouts: 185 us -> 6.96 us
  waiting for transfers between devices: 130 us -> 29.2 us
  matrix products: 74.8 us -> 0 us
  Pallas kernels: 0 us -> 52.1 us
  blocking collectives: 43 us -> 0 us
  other arithmetic: 43.3 us -> 4.99 us
  between operations: 14.9 us -> 1.06 us
  starting transfers between devices: 46.6 us -> 40.1 us
    psum x1 -> x0, waiting for transfers between devices: 130 us -> none  [body(): lax.psum((w_first_term, b_first_term, w_second_term, b_second_term), ('ro...]
    conv_general_dilated x15 -> x0, local copies, waits for them, and re-layouts: 107 us -> none  [conv_valid(): lax.conv_general_dilated(source[None], kernel, (1, 1), 'VALID', dimension...]
    pallas_call x0 -> x5, Pallas kernels: none -> 52.1 us  [the longest x1 19.2 us: inner(): pl.pallas_call(functools.partial(inner_kernel, channels, height, breadth)...]
    psum x1 -> x0, blocking collectives: 43 us -> none  [body(): lax.psum((w_first_term, b_first_term, w_second_term, b_second_term), ('ro...]
    dot_general x19 -> x0, matrix products: 37.6 us -> none  [the longest x18 31.3 us: correlate(): jnp.einsum('ohw,ihw->oi', grads, window, preferred_element_type=jnp.float32)]
    conv_general_dilated x3 -> x0, matrix products: 37.2 us -> none  [conv_valid(): lax.conv_general_dilated(source[None], kernel, (1, 1), 'VALID', dimension...]
    ppermute x12 -> x13, waiting for transfers between devices: 0.03 us -> 29.2 us  [the longest x7 29.2 us: total_over_devices(): lax.ppermute(value, AXES, [(i, i ^ step) for i in range(devices)])]
    transpose x2 -> x1, local copies, waits for them, and re-layouts: 16.2 us -> 0.15 us  [pair_weights(): taps = jnp.transpose(kernel, (0, 2, 3, 1)).reshape(kernel.shape[0], -1)]
  transfers between devices with their start and end apart: 15 -> 14, of which waited for: 1 -> 7; matrix products, arithmetic and copies ran while one was open for 27% -> 7% of each run, Pallas kernels for 0% -> 24%
where the time goes in v2:
time: 135 us; the launch traced here: 134 us
  Pallas kernels  52.1 us (39%)
  starting transfers between devices  40.1 us (30%)
  waiting for transfers between devices  29.2 us (22%)
  local copies, waits for them, and re-layouts  6.96 us (5%)
  other arithmetic  4.99 us (4%)
    ppermute x7, waiting for transfers between devices, total_over_devices(): lax.ppermute(value, AXES, [(i, i ^ step) for i in range(devices)])  29.2 us
    pallas_call x1, Pallas kernels, inner(): pl.pallas_call(functools.partial(inner_kernel, channels, height, breadth)...  19.2 us
    ppermute x7, starting transfers between devices, total_over_devices(): lax.ppermute(value, AXES, [(i, i ^ step) for i in range(devices)])  14.5 us
    pallas_call x1, Pallas kernels, correlate(): pl.pallas_call(functools.partial(correlate_kernel, channels, height, brea...  12.6 us
    all_to_all x1, starting transfers between devices, body(): lax.all_to_all(packed.reshape(devices, CAP * BLOCK, BLOCK * channels), AX...  10.6 us
    pallas_call x1, Pallas kernels, outer(): pl.pallas_call(functools.partial(outer_kernel, channels, height, breadth)...  7.29 us
    pallas_call x1, Pallas kernels, reorder(): pl.pallas_call(reorder_kernel, grid=(breadth // lanes, height // step), i...  6.68 us
    pallas_call x1, Pallas kernels, unpack(): pl.pallas_call(functools.partial(unpack_kernel, channels, devices), grid=...  6.32 us
  transfers between devices with their start and end apart: 14, of which 7 were waited for; matrix products, arithmetic and copies ran while one was open for 7% of the time, Pallas kernels for 24%

profile of v2, /device:TPU:0, one launch (start us, length us, event | category | flops | bytes accessed | tf_op | source)
XLA Modules:
  0.0 134.4 jit_solution(9190733151403249064)
XLA Ops:
  0.7 6.7 %reorder.1 = (bf16[2048,512]{1,0:T(8,128)(2,1)}, bf16[2048,512]{1,0:T(8,128)(2,1)}, bf16[16,2048]{1,0:T(8,128)(2,1)}, bf16[16,2048]{1,0:T(8,128)(2,1)}, bf16[256...) custom-call(bf16[64,32,512]{2,1,0:T(8,128)(2,1)} %w_ref.1, bf16[64,32,512]{2,1,0:T(8,128)(2,1)} %c_ref.1), custom_call_target="tpu_custom_call" | custom-call | tf_op jit(solution)/shard_map/reorder/pallas_call | solution.py:106
  7.4 2.3 %collective-permute-start.2 = (bf16[16,2048]{1,0:T(8,128)(2,1)}, bf16[16,2048]{1,0:T(8,128)(2,1)S(1)}, u32[]{:S(2)}, u32[]{:S(2)}) collective-permute-start(bf16[16,2048]{1,0:T(8,128)(2,1)} %get-tuple-element.24), channel_id=1, source_target_pairs={{0,1},{1,2},{2,3},{4,5},{5,6},{6,7},{8,9},{9,10},{10,11},{12,13},{... | collective-permute-start | bytes 196616 | tf_op jit(solution)/shard_map/ppermute | solution.py:663
  9.7 1.3 collective-permute-start.3
  11.0 4.2 %collective-permute-start = (bf16[256,512]{1,0:T(8,128)(2,1)}, bf16[256,512]{1,0:T(8,128)(2,1)S(1)}, u32[]{:S(2)}, u32[]{:S(2)}) collective-permute-start(bf16[256,512]{1,0:T(8,128)(2,1)} %get-tuple-element.22), channel_id=1, source_target_pairs={{0,4},{4,8},{8,12},{12,16},{16,20},{20,24},{24,28},{1,5},{5,9},{9,... | collective-permute-start | bytes 786440 | tf_op jit(solution)/shard_map/ppermute | solution.py:666
  15.3 1.3 collective-permute-start.1
  16.7 0.2 convert_reduce_fusion
  17.0 0.1 add.113
  17.3 0.1 copy.29
  17.4 0.1 copy.30
  17.6 0.1 copy.32
  17.7 0.1 copy.34
  17.9 0.8 fusion.11.w1f_ref
  18.8 0.1 broadcast_in_dim.58
  19.0 0.6 broadcast_add_fusion.target_ref
  19.6 0.9 fusion.9
  20.5 0.6 add_convert_fusion.flags_ref
  21.1 4.5 %collective-permute-start.4 = (bf16[16,128]{1,0:T(8,128)(2,1)S(1)}, bf16[16,128]{1,0:T(8,128)(2,1)S(1)}, u32[]{:S(2)}, u32[]{:S(2)}) collective-permute-start(bf16[16,128]{1,0:T(8,128)(2,1)S(1)} %get-tuple-element.52), channel_id=1, source_target_pairs={{0,4},{4,8},{8,12},{12,16},{16,20},{20,24},{24,28},{1,5},{5,9},{9,... | collective-permute-start | bytes 12296 | tf_op jit(solution)/shard_map/ppermute | solution.py:668
  25.6 1.3 collective-permute-start.5
  26.9 0.7 broadcast_in_dim.56.bias_ref
  27.6 19.2 %inner.1 = (bf16[1024,1024]{1,0:T(8,128)(2,1)}, bf16[2176,640]{1,0:T(8,128)(2,1)}, bf16[2176,640]{1,0:T(8,128)(2,1)}, bf16[2048,640]{1,0:T(8,128)(2,1)}, bf16[256,512]{1,0:T(8,128)(2,1)}) custom-call(s32[4]{0:T(128)} %add_convert_fusion.flags_ref, bf16[2048,512]{1,0:T(8,128)(2,1)} %get-tuple-element.20.xw_ref, bf16[2048,512]{1,0:T(8,128)(2,1)} %get-tuple-element.21.xc_ref, ...), custom_call_target="tpu_custom_call" | custom-call | flops 6039797760 | bytes 20000000 | tf_op jit(solution)/shard_map/inner/pallas_call | solution.py:268
  47.0 0.5 copy-done.6
  47.5 0.1 copy-done.3
  47.7 7.3 %outer.1 = (bf16[1024,1024]{1,0:T(8,128)(2,1)}, bf16[2176,640]{1,0:T(8,128)(2,1)}, bf16[2176,640]{1,0:T(8,128)(2,1)}, bf16[2048,640]{1,0:T(8,128)(2,1)}) custom-call(s32[4]{0:T(128)} %add_convert_fusion.flags_ref, bf16[2048,512]{1,0:T(8,128)(2,1)} %get-tuple-element.20.xw_ref, ...), custom_call_target="tpu_custom_call", output_to_operand_aliasing={{0}: (14, {}), {1}: (15, {}), {2}: (16, {}), {3}: (17, {})} | custom-call | tf_op jit(solution)/shard_map/outer/pallas_call | solution.py:421
  55.0 10.6 %all-to-all-start = ((bf16[32,32,1024]{2,1,0:T(8,128)(2,1)}), bf16[32,32,1024]{2,1,0:T(8,128)(2,1)S(1)}, u32[]{:S(2)}, u32[]{:S(2)}) async-start(bf16[32,32,1024]{2,1,0:T(8,128)(2,1)} %bitcast.25), calls=%async_computation | async-start | bytes 4194304 | tf_op jit(solution)/shard_map/all_to_all | solution.py:691
  65.6 0.1 select_reduce_fusion
  65.9 12.6 %correlate.1 = f32[584,128]{1,0:T(8,128)} custom-call(bf16[2176,640]{1,0:T(8,128)(2,1)} %get-tuple-element.31.act_in_ref, bf16[2176,640]{1,0:T(8,128)(2,1)} %get-tuple-element.32.act_mid_ref, bf16[2048,640]{1,0:T(8,128)(2,1)} %get-tuple-element.33.g_ref, bf16[2048,512]{1,0:T(8,128)(2,1)} %get-tuple-element.21.xc_ref), custom_call_target="tpu_custom_call" | custom-call | flops 3221225472 | bytes 10000000 | tf_op jit(solution)/shard_map/correlate/pallas_call | solution.py:522
  78.5 1.1 maximum_maximum_fusion
  79.6 0.1 collective-permute-start.6
  79.8 1.3 collective-permute-done.6
  81.1 1.7 %collective-permute-start.7 = (f32[152,128]{1,0:T(8,128)S(1)}, f32[152,128]{1,0:T(8,128)S(1)}, u32[]{:S(2)}, u32[]{:S(2)}) collective-permute-start(f32[152,128]{1,0:T(8,128)S(1)} %constant_dynamic-slice_fusion.1), channel_id=1, source_target_pairs={{0,2},{1,3},{2,0},{3,1},{4,6},{5,7},{6,4},{7,5},{8,10},{9,11},{10,... | collective-permute-start | bytes 233480 | tf_op jit(solution)/shard_map/ppermute | solution.py:615
  82.8 3.3 %collective-permute-done.7 = f32[152,128]{1,0:T(8,128)S(1)} collective-permute-done((f32[152,128]{1,0:T(8,128)S(1)}, f32[152,128]{1,0:T(8,128)S(1)}, u32[]{:S(2)}, u32[]{:S(2)}) %collective-permute-start.7) | collective-permute-done | bytes 77856 | tf_op jit(solution)/shard_map/ppermute | solution.py:615
  86.1 3.0 %collective-permute-start.8 = (f32[152,128]{1,0:T(8,128)S(1)}, f32[152,128]{1,0:T(8,128)S(1)}, u32[]{:S(2)}, u32[]{:S(2)}) collective-permute-start(f32[152,128]{1,0:T(8,128)S(1)} %dynamic-slice_add_fusion.1), channel_id=1, source_target_pairs={{0,4},{1,5},{2,6},{3,7},{4,0},{5,1},{6,2},{7,3},{8,12},{9,13},{10,... | collective-permute-start | bytes 233480 | tf_op jit(solution)/shard_map/ppermute | solution.py:615
  89.1 2.6 %collective-permute-done.8 = f32[152,128]{1,0:T(8,128)S(1)} collective-permute-done((f32[152,128]{1,0:T(8,128)S(1)}, f32[152,128]{1,0:T(8,128)S(1)}, u32[]{:S(2)}, u32[]{:S(2)}) %collective-permute-start.8) | collective-permute-done | bytes 77856 | tf_op jit(solution)/shard_map/ppermute | solution.py:615
  91.7 3.5 %collective-permute-start.9 = (f32[152,128]{1,0:T(8,128)S(1)}, f32[152,128]{1,0:T(8,128)S(1)}, u32[]{:S(2)}, u32[]{:S(2)}) collective-permute-start(f32[152,128]{1,0:T(8,128)S(1)} %add.128), channel_id=1, source_target_pairs={{0,8},{1,9},{2,10},{3,11},{4,12},{5,13},{6,14},{7,15},{8,0},{9,1},... | collective-permute-start | bytes 233480 | tf_op jit(solution)/shard_map/ppermute | solution.py:615
  95.2 6.5 %collective-permute-done.9 = f32[152,128]{1,0:T(8,128)S(1)} collective-permute-done((f32[152,128]{1,0:T(8,128)S(1)}, f32[152,128]{1,0:T(8,128)S(1)}, u32[]{:S(2)}, u32[]{:S(2)}) %collective-permute-start.9) | collective-permute-done | bytes 77856 | tf_op jit(solution)/shard_map/ppermute | solution.py:615
  101.7 4.7 %collective-permute-start.10 = (f32[152,128]{1,0:T(8,128)S(1)}, f32[152,128]{1,0:T(8,128)S(1)}, u32[]{:S(2)}, u32[]{:S(2)}) collective-permute-start(f32[152,128]{1,0:T(8,128)S(1)} %add.129), channel_id=1, source_target_pairs={{0,16},{1,17},{2,18},{3,19},{4,20},{5,21},{6,22},{7,23},{8,24},{9,... | collective-permute-start | bytes 233480 | tf_op jit(solution)/shard_map/ppermute | solution.py:615
  106.4 11.1 %collective-permute-done.10 = f32[152,128]{1,0:T(8,128)S(1)} collective-permute-done((f32[152,128]{1,0:T(8,128)S(1)}, f32[152,128]{1,0:T(8,128)S(1)}, u32[]{:S(2)}, u32[]{:S(2)}) %collective-permute-start.10) | collective-permute-done | bytes 77856 | tf_op jit(solution)/shard_map/ppermute | solution.py:615
  117.6 1.5 %collective-permute-start.11 = (f32[152,128]{1,0:T(8,128)S(1)}, f32[152,128]{1,0:T(8,128)S(1)}, u32[]{:S(2)}, u32[]{:S(2)}) collective-permute-start(f32[152,128]{1,0:T(8,128)S(1)} %add.130), channel_id=1, source_target_pairs={{0,2},{1,3},{2,0},{3,1},{4,6},{5,7},{6,4},{7,5},{8,10},{9,11},{10,... | collective-permute-start | bytes 233480 | tf_op jit(solution)/shard_map/ppermute | solution.py:615
  119.0 3.0 %collective-permute-done.11 = f32[152,128]{1,0:T(8,128)S(1)} collective-permute-done((f32[152,128]{1,0:T(8,128)S(1)}, f32[152,128]{1,0:T(8,128)S(1)}, u32[]{:S(2)}, u32[]{:S(2)}) %collective-permute-start.11) | collective-permute-done | bytes 77856 | tf_op jit(solution)/shard_map/ppermute | solution.py:615
  122.1 1.4 %collective-permute-done.12 = f32[304,128]{1,0:T(8,128)S(1)} collective-permute-done((f32[304,128]{1,0:T(8,128)S(1)}, f32[304,128]{1,0:T(8,128)S(1)}, u32[]{:S(2)}, u32[]{:S(2)}) %collective-permute-start.12) | collective-permute-done | bytes 155680 | tf_op jit(solution)/shard_map/ppermute | solution.py:615
  123.6 0.4 mul.70
  124.0 0.1 slice_bitcast_fusion
  124.1 0.7 copy.36
  124.9 0.7 copy.37
  125.6 0.6 slice_bitcast_fusion.2
  126.2 0.6 slice_convert_fusion.table_ref
  126.8 1.3 copy-done
  128.1 6.3 %unpack.1 = f32[64,2,2,8,512]{4,3,2,1,0:T(8,128)} custom-call(s32[1]{0:T(128)} %bitcast.me_ref, s32[16,128]{1,0:T(8,128)} %slice_convert_fusion.table_ref, bf16[1024,1024]{1,0:T(8,128)(2,1)} %bitcast.26), custom_call_target="tpu_custom_call" | custom-call | tf_op jit(solution)/shard_map/unpack/pallas_call | solution.py:584
  (64 shorter events, 1.2 us)
Async XLA Ops:
  0.6 15.9 %copy-start.8 = (s32[2,32]{1,0:T(2,128)S(1)}, s32[2,32]{1,0:T(2,128)}, u32[]{:S(2)}) copy-start(s32[2,32]{1,0:T(2,128)} %param.12) | copy-start | bytes 772
  0.6 16.6 %copy-start.1 = (bf16[64,64,3,3]{1,0,3,2:T(8,128)(2,1)S(1)}, bf16[64,64,3,3]{1,0,3,2:T(8,128)(2,1)}, u32[]{:S(2)}) copy-start(bf16[64,64,3,3]{1,0,3,2:T(8,128)(2,1)} %param.9) | copy-start | bytes 221188
  0.7 16.9 %copy-start.5 = (bf16[64,64,3,3]{1,0,3,2:T(8,128)(2,1)S(1)}, bf16[64,64,3,3]{1,0,3,2:T(8,128)(2,1)}, u32[]{:S(2)}) copy-start(bf16[64,64,3,3]{1,0,3,2:T(8,128)(2,1)} %param.11) | copy-start | bytes 221188
  0.7 18.0 %copy-start.10 = (f32[64]{0:T(128)S(1)}, f32[64]{0:T(128)}, u32[]{:S(2)}) copy-start(f32[64]{0:T(128)} %param.10) | copy-start | bytes 772
  0.7 18.2 %copy-start.9 = (s32[2,32]{1,0:T(2,128)S(1)}, s32[2,32]{1,0:T(2,128)}, u32[]{:S(2)}) copy-start(s32[2,32]{1,0:T(2,128)} %param.13) | copy-start | bytes 772
  7.4 13.7 %collective-permute-start.2 = (bf16[16,2048]{1,0:T(8,128)(2,1)}, bf16[16,2048]{1,0:T(8,128)(2,1)S(1)}, u32[]{:S(2)}, u32[]{:S(2)}) collective-permute-start(bf16[16,2048]{1,0:T(8,128)(2,1)} %get-tuple-element.24), channel_id=1, source_target_pairs={{0,1},{1,2},{2,3},{4,5},{5,6},{6,7},{8,9},{9,10},{10,11},{12,13},{... | collective-permute-start | bytes 196616 | tf_op jit(solution)/shard_map/ppermute | solution.py:663
  9.7 11.3 %collective-permute-start.3 = (bf16[16,2048]{1,0:T(8,128)(2,1)}, bf16[16,2048]{1,0:T(8,128)(2,1)S(1)}, u32[]{:S(2)}, u32[]{:S(2)}) collective-permute-start(bf16[16,2048]{1,0:T(8,128)(2,1)} %get-tuple-element.25), channel_id=1, source_target_pairs={{1,0},{2,1},{3,2},{5,4},{6,5},{7,6},{9,8},{10,9},{11,10},{13,12},{... | collective-permute-start | bytes 196616 | tf_op jit(solution)/shard_map/ppermute | solution.py:663
  11.0 35.9 %collective-permute-start = (bf16[256,512]{1,0:T(8,128)(2,1)}, bf16[256,512]{1,0:T(8,128)(2,1)S(1)}, u32[]{:S(2)}, u32[]{:S(2)}) collective-permute-start(bf16[256,512]{1,0:T(8,128)(2,1)} %get-tuple-element.22), channel_id=1, source_target_pairs={{0,4},{4,8},{8,12},{12,16},{16,20},{20,24},{24,28},{1,5},{5,9},{9,... | collective-permute-start | bytes 786440 | tf_op jit(solution)/shard_map/ppermute | solution.py:666
  15.3 31.7 %collective-permute-start.1 = (bf16[256,512]{1,0:T(8,128)(2,1)}, bf16[256,512]{1,0:T(8,128)(2,1)S(1)}, u32[]{:S(2)}, u32[]{:S(2)}) collective-permute-start(bf16[256,512]{1,0:T(8,128)(2,1)} %get-tuple-element.23), channel_id=1, source_target_pairs={{4,0},{8,4},{12,8},{16,12},{20,16},{24,20},{28,24},{5,1},{9,5},{13... | collective-permute-start | bytes 786440 | tf_op jit(solution)/shard_map/ppermute | solution.py:667
  21.1 6.6 %copy-start.2 = (bf16[16,2048]{1,0:T(8,128)(2,1)}, bf16[16,2048]{1,0:T(8,128)(2,1)S(1)}, u32[]{:S(2)}) copy-start(bf16[16,2048]{1,0:T(8,128)(2,1)S(1)} %add.110.side_ref) | copy-start | bytes 196612
  21.1 25.8 %collective-permute-start.4 = (bf16[16,128]{1,0:T(8,128)(2,1)S(1)}, bf16[16,128]{1,0:T(8,128)(2,1)S(1)}, u32[]{:S(2)}, u32[]{:S(2)}) collective-permute-start(bf16[16,128]{1,0:T(8,128)(2,1)S(1)} %get-tuple-element.52), channel_id=1, source_target_pairs={{0,4},{4,8},{8,12},{12,16},{16,20},{20,24},{24,28},{1,5},{5,9},{9,... | collective-permute-start | bytes 12296 | tf_op jit(solution)/shard_map/ppermute | solution.py:668
  25.6 21.3 %collective-permute-start.5 = (bf16[16,128]{1,0:T(8,128)(2,1)S(1)}, bf16[16,128]{1,0:T(8,128)(2,1)S(1)}, u32[]{:S(2)}, u32[]{:S(2)}) collective-permute-start(bf16[16,128]{1,0:T(8,128)(2,1)S(1)} %get-tuple-element.51), channel_id=1, source_target_pairs={{4,0},{8,4},{12,8},{16,12},{20,16},{24,20},{28,24},{5,1},{9,5},{13... | collective-permute-start | bytes 12296 | tf_op jit(solution)/shard_map/ppermute | solution.py:669
  46.9 0.6 copy-start.6
  46.9 0.6 copy-start.7
  46.9 0.7 copy-start.3
  47.0 0.8 copy-start.4
  55.0 71.8 %all-to-all-start = ((bf16[32,32,1024]{2,1,0:T(8,128)(2,1)}), bf16[32,32,1024]{2,1,0:T(8,128)(2,1)S(1)}, u32[]{:S(2)}, u32[]{:S(2)}) async-start(bf16[32,32,1024]{2,1,0:T(8,128)(2,1)} %bitcast.25), calls=%async_computation | async-start | bytes 4194304 | tf_op jit(solution)/shard_map/all_to_all | solution.py:691
  79.6 1.4 %collective-permute-start.6 = (f32[304,128]{1,0:T(8,128)S(1)}, f32[304,128]{1,0:T(8,128)S(1)}, u32[]{:S(2)}, u32[]{:S(2)}) collective-permute-start(f32[304,128]{1,0:T(8,128)S(1)} %constant_dynamic-slice_fusion), channel_id=1, source_target_pairs={{0,1},{1,0},{2,3},{3,2},{4,5},{5,4},{6,7},{7,6},{8,9},{9,8},{10,11... | collective-permute-start | bytes 466952 | tf_op jit(solution)/shard_map/ppermute | solution.py:615
  81.1 5.0 %collective-permute-start.7 = (f32[152,128]{1,0:T(8,128)S(1)}, f32[152,128]{1,0:T(8,128)S(1)}, u32[]{:S(2)}, u32[]{:S(2)}) collective-permute-start(f32[152,128]{1,0:T(8,128)S(1)} %constant_dynamic-slice_fusion.1), channel_id=1, source_target_pairs={{0,2},{1,3},{2,0},{3,1},{4,6},{5,7},{6,4},{7,5},{8,10},{9,11},{10,... | collective-permute-start | bytes 233480 | tf_op jit(solution)/shard_map/ppermute | solution.py:615
  86.1 5.6 %collective-permute-start.8 = (f32[152,128]{1,0:T(8,128)S(1)}, f32[152,128]{1,0:T(8,128)S(1)}, u32[]{:S(2)}, u32[]{:S(2)}) collective-permute-start(f32[152,128]{1,0:T(8,128)S(1)} %dynamic-slice_add_fusion.1), channel_id=1, source_target_pairs={{0,4},{1,5},{2,6},{3,7},{4,0},{5,1},{6,2},{7,3},{8,12},{9,13},{10,... | collective-permute-start | bytes 233480 | tf_op jit(solution)/shard_map/ppermute | solution.py:615
  91.7 10.0 %collective-permute-start.9 = (f32[152,128]{1,0:T(8,128)S(1)}, f32[152,128]{1,0:T(8,128)S(1)}, u32[]{:S(2)}, u32[]{:S(2)}) collective-permute-start(f32[152,128]{1,0:T(8,128)S(1)} %add.128), channel_id=1, source_target_pairs={{0,8},{1,9},{2,10},{3,11},{4,12},{5,13},{6,14},{7,15},{8,0},{9,1},... | collective-permute-start | bytes 233480 | tf_op jit(solution)/shard_map/ppermute | solution.py:615
  101.7 15.8 %collective-permute-start.10 = (f32[152,128]{1,0:T(8,128)S(1)}, f32[152,128]{1,0:T(8,128)S(1)}, u32[]{:S(2)}, u32[]{:S(2)}) collective-permute-start(f32[152,128]{1,0:T(8,128)S(1)} %add.129), channel_id=1, source_target_pairs={{0,16},{1,17},{2,18},{3,19},{4,20},{5,21},{6,22},{7,23},{8,24},{9,... | collective-permute-start | bytes 233480 | tf_op jit(solution)/shard_map/ppermute | solution.py:615
  117.6 4.5 %collective-permute-start.11 = (f32[152,128]{1,0:T(8,128)S(1)}, f32[152,128]{1,0:T(8,128)S(1)}, u32[]{:S(2)}, u32[]{:S(2)}) collective-permute-start(f32[152,128]{1,0:T(8,128)S(1)} %add.130), channel_id=1, source_target_pairs={{0,2},{1,3},{2,0},{3,1},{4,6},{5,7},{6,4},{7,5},{8,10},{9,11},{10,... | collective-permute-start | bytes 233480 | tf_op jit(solution)/shard_map/ppermute | solution.py:615
  122.1 1.4 %collective-permute-start.12 = (f32[304,128]{1,0:T(8,128)S(1)}, f32[304,128]{1,0:T(8,128)S(1)}, u32[]{:S(2)}, u32[]{:S(2)}) collective-permute-start(f32[304,128]{1,0:T(8,128)S(1)} %pad_maximum_fusion.1), channel_id=1, source_target_pairs={{0,1},{1,0},{2,3},{3,2},{4,5},{5,4},{6,7},{7,6},{8,9},{9,8},{10,11... | collective-permute-start | bytes 466952 | tf_op jit(solution)/shard_map/ppermute | solution.py:615
  126.8 1.3 copy-start

commit v3 on v2

--- a/solution.py
+++ b/solution.py
@@ -15,7 +15,7 @@
 F32 = jnp.float32
 NT = (((1,), (1,)), ((), ()))
 TN = (((0,), (0,)), ((), ()))
-VMEM_BYTES = 60 * 2**20
+VMEM_BYTES = 63 * 2**20
 
 
 def params(**extra):
@@ -52,8 +52,36 @@
     return pl.ds(pl.multiple_of(row * channels, channels), rows * channels)
 
 
-def reorder_kernel(w_ref, c_ref, xw_ref, xc_ref, to_right_ref, to_left_ref, to_up_ref, to_down_ref):
+def pair_weights(taps_ref, out_ref, flip):
+    ch = taps_ref.shape[2]
+    out_ref[...] = jnp.zeros_like(out_ref)
+    for row in range(3):
+        for col in range(3):
+            if flip:
+                tap = taps_ref[2 - row, 2 - col].astype(F32).T.astype(BF16)
+            else:
+                tap = taps_ref[row, col]
+            at = (row * 3 + col) * ch
+            out_ref[0:ch, at : at + ch] = tap
+            out_ref[ch : 2 * ch, at + 3 * ch : at + 4 * ch] = tap
+
+
+def reorder_kernel(
+    w_ref, c_ref, first_ref, second_ref, b_ref,
+    xw_ref, xc_ref, to_right_ref, to_left_ref, to_up_ref, to_down_ref,
+    w1_ref, w2f_ref, w1f_ref, bias_ref,
+):
     channels, rows, lanes = w_ref.shape
+
+    @pl.when((pl.program_id(0) == 0) & (pl.program_id(1) == 1))
+    def _():
+        pair_weights(first_ref, w1_ref, False)
+        pair_weights(second_ref, w2f_ref, True)
+        pair_weights(first_ref, w1f_ref, True)
+        column = jnp.broadcast_to(b_ref[...], (2 * channels, channels)).T
+        bias_ref[0:channels, :] = column
+        bias_ref[channels:, :] = column
+
     rim = 2 * channels
     kept = []
     for source, target in ((w_ref, xw_ref), (c_ref, xc_ref)):
@@ -92,8 +120,9 @@
         to_left_ref[:, here] = pick(slice(0, 128), ((4, 0), (5, 1)), ((6, 0), (7, 1)))
 
 
-def reorder(warped, cotangent):
+def reorder(warped, cotangent, w_first, w_second, b_first):
     channels, height, breadth = warped.shape
+    whole = lambda shape: pl.BlockSpec(shape, lambda x, h: (0,) * len(shape))
     step = 16
     lanes = 256
     spec_in = pl.BlockSpec((channels, step, lanes), lambda x, h: (0, h, x))
@@ -103,15 +132,27 @@
     shape = jax.ShapeDtypeStruct((height * channels, breadth), BF16)
     edge = jax.ShapeDtypeStruct((16, height * channels), BF16)
     rim = jax.ShapeDtypeStruct((4 * channels, breadth), BF16)
+    weights = jax.ShapeDtypeStruct((2 * channels, 12 * channels), BF16)
+    bias = jax.ShapeDtypeStruct((2 * channels, 2 * channels), F32)
     return pl.pallas_call(
         reorder_kernel,
         grid=(breadth // lanes, height // step),
-        in_specs=[spec_in, spec_in],
-        out_specs=[spec_out, spec_out, spec_edge, spec_edge, spec_rim, spec_rim],
-        out_shape=[shape, shape, edge, edge, rim, rim],
+        in_specs=[spec_in, spec_in]
+        + [whole(w_first.shape[2:] + w_first.shape[:2])] * 2
+        + [whole((1, channels))],
+        out_specs=[spec_out, spec_out, spec_edge, spec_edge, spec_rim, spec_rim]
+        + [whole(weights.shape)] * 3
+        + [whole(bias.shape)],
+        out_shape=[shape, shape, edge, edge, rim, rim, weights, weights, weights, bias],
         compiler_params=params(),
         name="reorder",
-    )(warped, cotangent)
+    )(
+        warped,
+        cotangent,
+        jnp.transpose(w_first, (2, 3, 0, 1)),
+        jnp.transpose(w_second, (2, 3, 0, 1)),
+        b_first[None, :],
+    )
 
 
 def spread_sides(side, first):
@@ -119,13 +160,12 @@
     return lax.dot_general(side, spread, TN, preferred_element_type=F32).astype(BF16)
 
 
-def lane_mask(flags_ref, lane, breadth):
-    wide = breadth + 128
-    return (
-        (lane < breadth)
-        | ((lane == breadth) & (flags_ref[3] == 1))
-        | ((lane == wide - 1) & (flags_ref[2] == 1))
-    )
+def rim_mask(channels):
+    lane = lax.broadcasted_iota(jnp.int32, (2 * channels, 128), 1)
+    col = lax.axis_index("cols")
+    right = jnp.where(col < lax.axis_size("cols") - 1, 0, -1)
+    left = jnp.where(col > 0, 127, -1)
+    return (lane == right) | (lane == left)
 
 
 def middle_step(w1_ref, w2f_ref, bias_ref, value, cot, act_window, cot_window):
@@ -149,7 +189,7 @@
 
 def inner_kernel(
     channels, height, breadth,
-    flags_ref, xw_ref, xc_ref, side_ref, w1_ref, w2f_ref, w1f_ref, bias_ref, target_ref,
+    xw_ref, xc_ref, side_ref, w1_ref, w2f_ref, w1f_ref, bias_ref, target_ref, label_ref,
     packed_ref, act_in_ref, act_mid_ref, g_ref, gw_mid_ref,
     wx, cx, sa, sc, sg, gw, act_in, act_mid, grads, packed, sem_in, sem_out,
 ):
@@ -157,25 +197,32 @@
     wide = breadth + 128
     core = slice(0, breadth)
     rim = slice(breadth, wide)
+    step = height * ch // 4
     loads = [
-        pltpu.make_async_copy(xw_ref, wx.at[:, core], sem_in.at[0]),
-        pltpu.make_async_copy(xc_ref, cx.at[:, core], sem_in.at[1]),
+        pltpu.make_async_copy(
+            source.at[at * step : (at + 1) * step, :],
+            target.at[at * step : (at + 1) * step, core],
+            sem_in.at[2 * at + which],
+        )
+        for at in range(4)
+        for which, (source, target) in enumerate(((xw_ref, wx), (xc_ref, cx)))
     ]
     stores = [
         pltpu.make_async_copy(act_in, act_in_ref.at[ch : ch + height * ch, :], sem_out.at[0]),
         pltpu.make_async_copy(act_mid, act_mid_ref.at[2 * ch : height * ch, :], sem_out.at[1]),
         pltpu.make_async_copy(grads, g_ref.at[ch : (height - 1) * ch, :], sem_out.at[2]),
-        pltpu.make_async_copy(packed, packed_ref.at[:, 2 * ch : (BLOCK - 2) * ch], sem_out.at[3]),
+        pltpu.make_async_copy(
+            label_ref, packed_ref.at[:, DEPTH * CAP * BLOCK : DEPTH * CAP * BLOCK + 16, :], sem_out.at[3]
+        ),
         pltpu.make_async_copy(
             gw.at[(BLOCK - 2) * ch : (BLOCK + 2) * ch, :], gw_mid_ref, sem_out.at[4]
         ),
     ]
     for load in loads:
         load.start()
+    stores[3].start()
     wx[:, rim] = spread_sides(side_ref[...], 0)
     cx[:, rim] = spread_sides(side_ref[...], 2)
-    for load in loads:
-        load.wait()
 
     def prepare(row, _):
         here = at_row(row, 1, ch)
@@ -190,10 +237,12 @@
             sc[pl.ds(out + shift * ch, ch), :] = moved[shift]
         return 0
 
-    lax.fori_loop(0, height, prepare, 0, unroll=UNROLL_PREPARE)
+    for at in range(4):
+        loads[2 * at].wait()
+        loads[2 * at + 1].wait()
+        lax.fori_loop(at * height // 4, (at + 1) * height // 4, prepare, 0, unroll=UNROLL_PREPARE)
     stores[0].start()
-    lane = lax.broadcasted_iota(jnp.int32, (2 * ch, 128), 1) + breadth
-    rim_ok = lane_mask(flags_ref, lane, breadth)
+    rim_ok = rim_mask(ch)
 
     def middle(pair, _):
         row = pair * 2
@@ -238,27 +287,38 @@
             rows = slice(band * strip + 2 * ch, (band + 1) * strip - 2 * ch)
             term = lax.dot_general(chosen, gw[rows, :], NT, preferred_element_type=F32)
             total = term if total is None else total + term
-        packed[pl.ds(start, size), :] = total.astype(BF16)
+        total = total.astype(BF16).reshape(size // rows_to, rows_to, total.shape[1])
+        packed[pl.ds(part * (size // rows_to), size // rows_to), :, :] = total
         return 0
 
-    lax.fori_loop(0, packed.shape[0] // size, pack, 0)
-    stores[3].start()
+    rows_to = CAP * BLOCK
+    lax.fori_loop(0, packed.shape[0] * rows_to // size, pack, 0)
+    for at in range(1, DEPTH - 1):
+        stores.append(
+            pltpu.make_async_copy(
+                packed.at[:, :, (at - 1) * 128 : at * 128],
+                packed_ref.at[:, at * rows_to : (at + 1) * rows_to, :],
+                sem_out.at[4 + at],
+            )
+        )
+        stores[-1].start()
     for store in stores:
         store.wait()
 
 
+DEPTH = 8
 UNROLL_PREPARE = 8
 UNROLL_MIDDLE = 5
 UNROLL_LAST = 7
 
 
-def inner(sizes, flags, operands, slots):
+def inner(sizes, operands, slots):
     channels, height, breadth = sizes
     wide = breadth + 128
     vmem = pl.BlockSpec(memory_space=pltpu.VMEM)
     hbm = pl.BlockSpec(memory_space=pl.ANY)
     outs = [
-        jax.ShapeDtypeStruct((slots * BLOCK, BLOCK * channels), BF16),
+        jax.ShapeDtypeStruct((slots // CAP, DEPTH * CAP * BLOCK + 16, 128), BF16),
         jax.ShapeDtypeStruct(((height + 2) * channels, wide), BF16),
         jax.ShapeDtypeStruct(((height + 2) * channels, wide), BF16),
         jax.ShapeDtypeStruct((height * channels, wide), BF16),
@@ -267,7 +327,7 @@
     flops = 2 * 3 * 12 * channels * 2 * channels * wide * (height // 2)
     return pl.pallas_call(
         functools.partial(inner_kernel, channels, height, breadth),
-        in_specs=[pl.BlockSpec(memory_space=pltpu.SMEM), hbm, hbm] + [vmem] * (len(operands) - 2),
+        in_specs=[hbm, hbm] + [vmem] * (len(operands) - 3) + [hbm],
         out_specs=[hbm] * len(outs),
         out_shape=outs,
         scratch_shapes=[
@@ -280,23 +340,24 @@
             pltpu.VMEM((height * channels, wide), BF16),
             pltpu.VMEM(((height - 2) * channels, wide), BF16),
             pltpu.VMEM(((height - 2) * channels, wide), BF16),
-            pltpu.VMEM((slots * BLOCK, (BLOCK - 4) * channels), BF16),
-            pltpu.SemaphoreType.DMA((2,)),
-            pltpu.SemaphoreType.DMA((5,)),
+            pltpu.VMEM((slots // CAP, CAP * BLOCK, (BLOCK - 4) * channels), BF16),
+            pltpu.SemaphoreType.DMA((8,)),
+            pltpu.SemaphoreType.DMA((3 + DEPTH,)),
         ],
         compiler_params=params(),
         cost_estimate=pl.CostEstimate(flops=flops, bytes_accessed=2 * 10**7, transcendentals=10**6),
         name="inner",
-    )(flags, *operands)
+    )(*operands)
 
 
 def outer_kernel(
     channels, height, breadth,
-    flags_ref, xw_ref, xc_ref, up_ref, down_ref, side_ref, side_up_ref, side_down_ref,
+    xw_ref, xc_ref, up_ref, down_ref, side_ref,
     w1_ref, w2f_ref, w1f_ref, bias_ref, target_ref, gw_mid_ref,
     packed_in, act_in_in, act_mid_in, g_in,
     packed_ref, act_in_ref, act_mid_ref, g_ref,
-    wx, cx, sa, sc, sg, near, gw, act_in, act_mid, grads, packed, sem_in, sem_out,
+    wx, cx, sa_both, sc_both, sg_both, near, gw, act_in, act_mid, grads, packed, chosen, corner,
+    sem_in, sem_out,
 ):
     ch = channels
     wide = breadth + 128
@@ -311,6 +372,8 @@
         copy.start()
         loads.append(copy)
 
+    load(up_ref.at[2 * rows2 : 2 * rows2 + 16, 0:rows2], corner.at[0])
+    load(down_ref.at[2 * rows2 : 2 * rows2 + 16, 0:rows2], corner.at[1])
     load(xw_ref.at[0:rows2, :], wx.at[rows2 : 2 * rows2, core])
     load(xc_ref.at[0:rows2, :], cx.at[rows2 : 2 * rows2, core])
     load(xw_ref.at[body - rows2 : body, :], wx.at[2 * rows2 : 3 * rows2, core])
@@ -322,18 +385,30 @@
     load(g_in.at[ch : 3 * ch, :], near.at[0:rows2, :])
     load(g_in.at[body - 3 * ch : body - ch, :], near.at[rows2 : 2 * rows2, :])
     for target, first in ((wx, 0), (cx, 2)):
-        target[0:rows2, rim] = spread_sides(side_up_ref[...], first)
         target[rows2 : 2 * rows2, rim] = spread_sides(side_ref[:, 0:rows2], first)
         target[2 * rows2 : 3 * rows2, rim] = spread_sides(side_ref[:, body - rows2 : body], first)
-        target[3 * rows2 : 4 * rows2, rim] = spread_sides(side_down_ref[...], first)
+    size = 256
+
+    def choose(part, _):
+        start = pl.multiple_of(part * size, size)
+        for band in range(2):
+            chosen[pl.ds(start, size), band * breadth : (band + 1) * breadth] = chosen_blocks(
+                target_ref, band, start, size, breadth
+            )
+        return 0
+
+    lax.fori_loop(0, chosen.shape[0] // size, choose, 0)
     for copy in loads:
         copy.wait()
-    lane = lax.broadcasted_iota(jnp.int32, (2 * ch, 128), 1) + breadth
-    rim_ok = lane_mask(flags_ref, lane, breadth)
+    for target, first in ((wx, 0), (cx, 2)):
+        target[0:rows2, rim] = spread_sides(corner[0], first)
+        target[3 * rows2 : 4 * rows2, rim] = spread_sides(corner[1], first)
+    rim_ok = rim_mask(ch)
     sub = lax.broadcasted_iota(jnp.int32, (2 * ch, wide), 0)
 
     for half in range(2):
         base = half * 2 * rows2
+        sa, sc, sg = sa_both.at[half], sc_both.at[half], sg_both.at[half]
         for row in range(4):
             here = slice(base + row * ch, base + (row + 1) * ch)
             value = wx[here, :].astype(F32)
@@ -349,7 +424,9 @@
         act, grad = middle_step(
             w1_ref, w2f_ref, bias_ref, wx[here, :], cx[here, :], sa[...], sc[...]
         )
-        good = ((sub >= ch) if half == 0 else (sub < ch)) | (flags_ref[half] == 1)
+        inside_at = 0 if half == 0 else lax.axis_size("rows") - 1
+        limit = jnp.where(lax.axis_index("rows") == inside_at, ch, 0 if half == 0 else 2 * ch)
+        good = (sub >= limit) if half == 0 else (sub < limit)
         act = jnp.where(good, rim_masked(act, rim_ok, breadth), 0.0)
         grad = jnp.where(good, rim_masked(grad, rim_ok, breadth), 0.0)
         act_mid[half * rows2 : (half + 1) * rows2, :] = act.astype(BF16)
@@ -371,6 +448,7 @@
             mid + slope_of(value, sigmoid(value)) * back
         ).astype(BF16)
 
+    rows_to = CAP * BLOCK
     stores = [
         (act_in.at[0:ch, :], act_in_ref.at[0:ch, :]),
         (act_in.at[ch : 2 * ch, :], act_in_ref.at[body + ch : body + 2 * ch, :]),
@@ -378,8 +456,11 @@
         (act_mid.at[rows2 : 2 * rows2, :], act_mid_ref.at[body : body + 2 * ch, :]),
         (grads.at[0:ch, :], g_ref.at[0:ch, :]),
         (grads.at[ch : 2 * ch, :], g_ref.at[body - ch : body, :]),
-        (packed.at[:, 0:rows2], packed_ref.at[:, 0:rows2]),
-        (packed.at[:, rows2 : 2 * rows2], packed_ref.at[:, (BLOCK - 2) * ch : BLOCK * ch]),
+        (packed.at[:, :, 0:rows2], packed_ref.at[:, 0:rows_to, :]),
+        (
+            packed.at[:, :, rows2 : 2 * rows2],
+            packed_ref.at[:, (DEPTH - 1) * rows_to : DEPTH * rows_to, :],
+        ),
     ]
     stores = [
         pltpu.make_async_copy(source, target, sem_out.at[at])
@@ -387,41 +468,43 @@
     ]
     for store in stores[:6]:
         store.start()
-    first = jnp.concatenate([gw[0:rows2, :], gw_mid_ref[0:rows2, :]], axis=0)
-    second = jnp.concatenate([gw_mid_ref[rows2 : 2 * rows2, :], gw[rows2 : 2 * rows2, :]], axis=0)
-    size = 256
+    both = (
+        jnp.concatenate([gw[0:rows2, :], gw_mid_ref[0:rows2, :]], axis=0),
+        jnp.concatenate([gw_mid_ref[rows2 : 2 * rows2, :], gw[rows2 : 2 * rows2, :]], axis=0),
+    )
 
     def pack(part, _):
-        start = pl.multiple_of(part * size, size)
+        rows = pl.ds(pl.multiple_of(part * size, size), size)
         total = sum(
             lax.dot_general(
-                chosen_blocks(target_ref, band, start, size, breadth),
-                rows,
+                chosen[rows, band * breadth : (band + 1) * breadth],
+                both[band],
                 NT,
                 preferred_element_type=F32,
             )
-            for band, rows in enumerate((first, second))
+            for band in range(2)
+        ).astype(BF16)
+        packed[pl.ds(part * (size // rows_to), size // rows_to), :, :] = total.reshape(
+            size // rows_to, rows_to, total.shape[1]
         )
-        packed[pl.ds(start, size), :] = total.astype(BF16)
         return 0
 
-    lax.fori_loop(0, packed.shape[0] // size, pack, 0)
+    lax.fori_loop(0, chosen.shape[0] // size, pack, 0)
     for store in stores[6:]:
         store.start()
     for store in stores:
         store.wait()
 
 
-def outer(sizes, flags, operands, state, slots):
+def outer(sizes, operands, state, slots):
     channels, height, breadth = sizes
     wide = breadth + 128
     vmem = pl.BlockSpec(memory_space=pltpu.VMEM)
     hbm = pl.BlockSpec(memory_space=pl.ANY)
-    inputs = 1 + len(operands)
+    inputs = len(operands)
     return pl.pallas_call(
         functools.partial(outer_kernel, channels, height, breadth),
-        in_specs=[pl.BlockSpec(memory_space=pltpu.SMEM)]
-        + [hbm] * 4
+        in_specs=[hbm] * 4
         + [vmem] * (len(operands) - 4)
         + [hbm] * len(state),
         out_specs=[hbm] * len(state),
@@ -430,21 +513,23 @@
         scratch_shapes=[
             pltpu.VMEM((8 * channels, wide), BF16),
             pltpu.VMEM((8 * channels, wide), BF16),
-            pltpu.VMEM((12 * channels, wide), BF16),
-            pltpu.VMEM((12 * channels, wide), BF16),
-            pltpu.VMEM((12 * channels, wide), BF16),
+            pltpu.VMEM((2, 12 * channels, wide), BF16),
+            pltpu.VMEM((2, 12 * channels, wide), BF16),
+            pltpu.VMEM((2, 12 * channels, wide), BF16),
             pltpu.VMEM((4 * channels, wide), BF16),
             pltpu.VMEM((4 * channels, breadth), BF16),
             pltpu.VMEM((2 * channels, wide), BF16),
             pltpu.VMEM((4 * channels, wide), BF16),
             pltpu.VMEM((2 * channels, wide), BF16),
-            pltpu.VMEM((slots * BLOCK, 4 * channels), BF16),
-            pltpu.SemaphoreType.DMA((10,)),
+            pltpu.VMEM((slots // CAP, CAP * BLOCK, 4 * channels), BF16),
+            pltpu.VMEM((slots * BLOCK, 2 * breadth), BF16),
+            pltpu.VMEM((2, 16, 2 * channels), BF16),
+            pltpu.SemaphoreType.DMA((12,)),
             pltpu.SemaphoreType.DMA((8,)),
         ],
         compiler_params=params(),
         name="outer",
-    )(flags, *operands, *state)
+    )(*operands, *state)
 
 
 def correlate_kernel(
@@ -543,66 +628,62 @@
     )(act_in, act_mid, g_mid, xc)
 
 
-def unpack_kernel(channels, devices, me_ref, table_ref, arrived_ref, out_ref, chosen):
+def unpack_kernel(channels, arrived_ref, label_ref, out_ref, chosen, flat):
+    devices = arrived_ref.shape[0]
     block_rows, part, breadth = out_ref.shape[1], out_ref.shape[3], out_ref.shape[4]
+    rows_to = CAP * BLOCK
 
     @pl.when(pl.program_id(0) == 0)
     def _():
-        shape = (CAP * BLOCK, block_rows * breadth)
-        sub = lax.broadcasted_iota(jnp.int32, shape, 0)
-        place = lax.broadcasted_iota(jnp.int32, shape, 1) - sub % BLOCK
-        second = sub >= BLOCK
+        shape = (BLOCK, block_rows * breadth)
+        place = lax.broadcasted_iota(jnp.int32, shape, 1) - lax.broadcasted_iota(jnp.int32, shape, 0)
+        place = place.astype(F32)
 
         def select(source, _):
-            at = (source * devices + me_ref[0]) * CAP
-            owners = [
-                table_ref[(at + rank) // 128, (at + rank) % 128] * BLOCK for rank in range(CAP)
-            ]
-            wanted = jnp.where(second, owners[1], owners[0])
-            chosen[pl.ds(pl.multiple_of(source * CAP * BLOCK, CAP * BLOCK), CAP * BLOCK), :] = (
-                (place == wanted).astype(F32).astype(BF16)
-            )
+            label = label_ref[source].astype(F32) * BLOCK
+            for rank in range(CAP):
+                at = rank * (128 // CAP)
+                hit = (place == label[:, at : at + 1]).astype(F32).astype(BF16)
+                row = pl.multiple_of(source * rows_to + rank * BLOCK, BLOCK)
+                chosen[pl.ds(row, BLOCK), :] = hit
             return 0
 
         lax.fori_loop(0, devices, select, 0, unroll=4)
 
-    flat = arrived_ref[...].T
+    for at in range(arrived_ref.shape[1] // rows_to):
+        tile = arrived_ref[:, at * rows_to : (at + 1) * rows_to, :]
+        flat[at * 128 : (at + 1) * 128, :] = tile.reshape(devices * rows_to, 128).T
     for band in range(block_rows):
         summed = jnp.dot(
-            flat, chosen[:, band * breadth : (band + 1) * breadth], preferred_element_type=F32
+            flat[...], chosen[:, band * breadth : (band + 1) * breadth], preferred_element_type=F32
         )
         cube = summed.reshape(part, channels, breadth)
         out_ref[:, band, 0, :, :] = jnp.swapaxes(cube, 0, 1)
 
 
-def unpack(sizes, me, table, arrived, devices):
+def unpack(sizes, arrived):
     channels, height, breadth = sizes
     block_rows = height // BLOCK
-    rows = arrived.shape[0]
+    devices = arrived.shape[0]
+    rows_to = CAP * BLOCK
     part = 8
-    smem = pl.BlockSpec(memory_space=pltpu.SMEM)
+    tiles = DEPTH * part // BLOCK
     return pl.pallas_call(
-        functools.partial(unpack_kernel, channels, devices),
+        functools.partial(unpack_kernel, channels),
         grid=(BLOCK // part,),
-        in_specs=[smem, smem, pl.BlockSpec((rows, part * channels), lambda h: (0, h))],
+        in_specs=[
+            pl.BlockSpec((devices, tiles * rows_to, 128), lambda h: (0, h, 0)),
+            pl.BlockSpec((devices, 16, 128), lambda h: (0, DEPTH * rows_to // 16, 0)),
+        ],
         out_specs=pl.BlockSpec((channels, block_rows, 1, part, breadth), lambda h: (0, 0, h, 0, 0)),
         out_shape=jax.ShapeDtypeStruct((channels, block_rows, BLOCK // part, part, breadth), F32),
-        scratch_shapes=[pltpu.VMEM((rows, block_rows * breadth), BF16)],
+        scratch_shapes=[
+            pltpu.VMEM((devices * rows_to, block_rows * breadth), BF16),
+            pltpu.VMEM((part * channels, devices * rows_to), BF16),
+        ],
         compiler_params=params(),
         name="unpack",
-    )(me, table, arrived)
-
-
-def pair_weights(kernel):
-    taps = jnp.transpose(kernel, (0, 2, 3, 1)).reshape(kernel.shape[0], -1)
-    third = taps.shape[1] // 3
-    return jnp.concatenate(
-        [jnp.pad(taps, ((0, 0), (0, third))), jnp.pad(taps, ((0, 0), (third, 0)))], axis=0
-    )
-
-
-def flipped(kernel):
-    return jnp.transpose(kernel[:, :, ::-1, ::-1], (1, 0, 2, 3))
+    )(arrived, arrived)
 
 
 def shift_pairs(axis, step):
@@ -610,27 +691,57 @@
     return [(i, i + step) for i in range(count) if 0 <= i + step < count]
 
 
-def total_over_devices(terms, devices):
+def finish_kernel(channels, factor, total_ref, other_ref, w1_ref, w2_ref, b1_ref, b2_ref, terms):
+    ch = channels
+    half = total_ref.shape[0]
+    bit = lax.rem(lax.axis_index("rows") * lax.axis_size("cols") + lax.axis_index("cols"), 2)
+    terms[pl.ds(pl.multiple_of(bit * half, 8), half), :] = total_ref[...] * factor
+    terms[pl.ds(pl.multiple_of((1 - bit) * half, 8), half), :] = other_ref[...] * factor
+    tile = lambda at: terms[at * 3 * ch : (at + 1) * 3 * ch, :]
+    for out, parts in ((w1_ref, ((0, 0), (0, 1), (1, 0))), (w2_ref, ((1, 1), (2, 0), (2, 1)))):
+        for row, (at, side) in enumerate(parts):
+            value = pltpu.roll(tile(at), ch, 1) if side else tile(at)
+            for col in range(3):
+                out[row, col] = value[col * ch : (col + 1) * ch, 0:ch]
+    bias = terms[9 * ch : 9 * ch + 8, :]
+    b1_ref[...] = bias[0:1, 0:ch]
+    b2_ref[...] = pltpu.roll(bias, ch, 1)[0:1, 0:ch]
+
+
+def finish(channels, factor, total, other):
+    vmem = pl.BlockSpec(memory_space=pltpu.VMEM)
+    kernel = jax.ShapeDtypeStruct((3, 3, channels, channels), F32)
+    bias = jax.ShapeDtypeStruct((1, channels), F32)
+    w1, w2, b1, b2 = pl.pallas_call(
+        functools.partial(finish_kernel, channels, factor),
+        in_specs=[vmem, vmem],
+        out_specs=[vmem] * 4,
+        out_shape=[kernel, kernel, bias, bias],
+        scratch_shapes=[pltpu.VMEM((2 * total.shape[0], 128), F32)],
+        compiler_params=params(),
+        name="finish",
+    )(total, other)
+    order = (2, 3, 0, 1)
+    return jnp.transpose(w1, order), b1[0], jnp.transpose(w2, order), b2[0]
+
+
+def total_over_devices(terms, devices, frame_of):
     me = lax.axis_index(AXES)
     swap = lambda value, step: lax.ppermute(value, AXES, [(i, i ^ step) for i in range(devices)])
-    total = terms
-    for step in (1, 2):
-        bit = (me // step) % 2
-        half = total.shape[0] // 2
-        mine = lax.dynamic_slice_in_dim(total, bit * half, half, 0)
-        away = lax.dynamic_slice_in_dim(total, (1 - bit) * half, half, 0)
-        total = mine + swap(away, step)
-    step = 4
-    while step < devices:
+    bit = me % 2
+    half = terms.shape[0] // 2
+    mine = lax.dynamic_slice_in_dim(terms, bit * half, half, 0)
+    away = lax.dynamic_slice_in_dim(terms, (1 - bit) * half, half, 0)
+    total = mine + swap(away, 1)
+    step = 2
+    while 2 * step < devices:
         total = total + swap(total, step)
         step *= 2
-    for step in (2, 1):
-        bit = (me // step) % 2
-        other = swap(total, step)
-        total = jnp.concatenate(
-            [jnp.where(bit == 0, total, other), jnp.where(bit == 0, other, total)], axis=0
-        )
-    return total
+    other = swap(total, step)
+    frame = frame_of()
+    other, frame = lax.optimization_barrier((other, frame))
+    total = total + other
+    return total, swap(total, 1), frame
 
 
 def body(warped, cotangent, w_first, b_first, w_second, source_tile, source_block):
@@ -641,8 +752,6 @@
     devices = row_count * col_count
     slots = devices * CAP
     factor = 1.0 / math.sqrt(height * row_count * breadth * col_count)
-    row_at = lax.axis_index("rows")
-    col_at = lax.axis_index("cols")
     me = lax.axis_index(AXES)
 
     block_rows = height // BLOCK
@@ -657,64 +766,45 @@
     ).reshape(block_rows, breadth)
     hits = places[:, None] == jnp.arange(slots, dtype=jnp.int32)[None, :]
     labels = jnp.sum(jnp.where(hits, source_block.reshape(count, 1) + 1, 0), axis=0) - 1
-
-    xw, xc, to_right, to_left, to_up, to_down = reorder(warped, cotangent)
+    labels = jnp.broadcast_to(
+        jnp.repeat(labels.reshape(devices, 1, CAP), 128 // CAP, axis=2), (devices, 16, 128)
+    ).astype(BF16)
+
+    xw, xc, to_right, to_left, to_up, to_down, first, second_back, first_back, bias = reorder(
+        warped, cotangent, w_first, w_second, b_first
+    )
     rim = 2 * channels
     side = lax.ppermute(to_right, "cols", shift_pairs("cols", 1)) + lax.ppermute(
         to_left, "cols", shift_pairs("cols", -1)
     )
+    fill = ((0, 0), (0, breadth - rim))
+    to_down = jnp.concatenate([to_down, jnp.pad(side[:, -rim:], fill)], axis=0)
+    to_up = jnp.concatenate([to_up, jnp.pad(side[:, :rim], fill)], axis=0)
     up = lax.ppermute(to_down, "rows", shift_pairs("rows", 1))
     down = lax.ppermute(to_up, "rows", shift_pairs("rows", -1))
-    side_up = lax.ppermute(side[:, -rim:], "rows", shift_pairs("rows", 1))
-    side_down = lax.ppermute(side[:, :rim], "rows", shift_pairs("rows", -1))
-
-    flags = jnp.stack(
-        [row_at > 0, row_at < row_count - 1, col_at > 0, col_at < col_count - 1]
-    ).astype(jnp.int32)
-    bias = jnp.broadcast_to(jnp.tile(b_first, 2)[:, None], (2 * channels, 128))
-    first = pair_weights(w_first)
-    second_back = pair_weights(flipped(w_second))
-    first_back = pair_weights(flipped(w_first))
+
     *state, gw_mid = inner(
-        sizes, flags, (xw, xc, side, first, second_back, first_back, bias, target_row), slots
+        sizes, (xw, xc, side, first, second_back, first_back, bias, target_row, labels), slots
     )
     packed, act_in, act_mid, g_mid = outer(
         sizes,
-        flags,
         (
-            xw, xc, up, down, side, side_up, side_down,
+            xw, xc, up, down, side,
             first, second_back, first_back, bias, target_row, gw_mid,
         ),
         state,
         slots,
     )
-    arrived = lax.all_to_all(
-        packed.reshape(devices, CAP * BLOCK, BLOCK * channels),
-        AXES,
-        split_axis=0,
-        concat_axis=0,
-        tiled=True,
-    )
+    arrived = lax.all_to_all(packed, AXES, split_axis=0, concat_axis=0, tiled=True)
 
     terms = correlate(sizes, act_in, act_mid, g_mid, xc)
-    mine = jnp.arange(devices, dtype=jnp.int32)[:, None] == me
-    table = jnp.where(mine, labels.astype(F32)[None, :], 0.0).reshape(-1, 128)
-    used = terms.shape[0] + table.shape[0]
-    fill = jnp.zeros((-used % 32, 128), F32)
-    summed = total_over_devices(jnp.concatenate([terms, table, fill], axis=0), devices)
-    owners = summed[terms.shape[0] : used].astype(jnp.int32)
-    frame = unpack(
-        sizes, me.reshape(1), owners, arrived.reshape(slots * BLOCK, BLOCK * channels), devices
-    )
-    tiles = summed[: 9 * channels].reshape(3, 3 * channels, 128)
-    taps = (
-        jnp.concatenate([tiles[0], tiles[1], tiles[2]], axis=1)
-        .reshape(3, channels, 2, 3, channels)
-        .transpose(2, 1, 4, 3, 0)
-        * factor
-    )
-    biases = summed[9 * channels].reshape(2, channels) * factor
-    return (frame.reshape(sizes), taps[0], biases[0], taps[1], biases[1])
+    fill = jnp.zeros((-terms.shape[0] % 16, 128), F32)
+    total, other, frame = total_over_devices(
+        jnp.concatenate([terms, fill], axis=0),
+        devices,
+        lambda: unpack(sizes, arrived),
+    )
+    return (frame.reshape(sizes), *finish(channels, factor, total, other))
 
 
 def solution(mesh):

time: 135 us -> 125 us (0.926)
  starting transfers between devices: 40.1 us -> 23.6 us
  waiting for transfers between devices: 29.2 us -> 37.8 us
  local copies, waits for them, and re-layouts: 6.96 us -> 3.79 us
  Pallas kernels: 52.1 us -> 54 us
    all_to_all x1, waiting for transfers between devices: 0.01 us -> 10.8 us  [body(): lax.all_to_all(packed, AXES, split_axis=0, concat_axis=0, tiled=True)]
    ppermute x7 -> x6, starting transfers between devices: 14.5 us -> 6.68 us  [total_over_devices(): lax.ppermute(value, AXES, [(i, i ^ step) for i in range(devices)])]
    ppermute x2 -> x0, starting transfers between devices: 5.84 us -> none  [the longest x1 4.55 us: body(): side_up = lax.ppermute(side[:, -rim:], 'rows', shift_pairs('rows', 1))]
    ppermute x7 -> x6, waiting for transfers between devices: 29.2 us -> 24.6 us  [total_over_devices(): lax.ppermute(value, AXES, [(i, i ^ step) for i in range(devices)])]
    all_to_all x1, starting transfers between devices: 10.6 us -> 6.69 us  [body(): lax.all_to_all(packed, AXES, split_axis=0, concat_axis=0, tiled=True)]
    ppermute x1, waiting for transfers between devices: 0.01 us -> 2.44 us  [body(): lax.ppermute(to_left, 'cols', shift_pairs('cols', -1))]
    unnamed x24 -> x14, local copies, waits for them, and re-layouts: 3.61 us -> 1.38 us
    pallas_call x1 -> x2, Pallas kernels: 6.32 us -> 8.42 us  [the longest x1 6.5 us: unpack(): pl.pallas_call(functools.partial(unpack_kernel, channels), grid=(BLOCK //...]
  transfers between devices with their start and end apart: 14 -> 11, of which waited for: 7 -> 7; matrix products, arithmetic and copies ran while one was open for 7% -> 4% of each run, Pallas kernels for 24% -> 30%
where the time goes in v3:
time: 125 us; the launch traced here: 124 us
  Pallas kernels  54 us (43%)
  waiting for transfers between devices  37.8 us (30%)
  starting transfers between devices  23.6 us (19%)
  other arithmetic  3.88 us (3%)
  local copies, waits for them, and re-layouts  3.79 us (3%)
    ppermute x6, waiting for transfers between devices, total_over_devices(): lax.ppermute(value, AXES, [(i, i ^ step) for i in range(devices)])  24.6 us
    pallas_call x1, Pallas kernels, inner(): pl.pallas_call(functools.partial(inner_kernel, channels, height, breadth)...  18.3 us
    pallas_call x1, Pallas kernels, correlate(): pl.pallas_call(functools.partial(correlate_kernel, channels, height, brea...  12.6 us
    all_to_all x1, waiting for transfers between devices, body(): lax.all_to_all(packed, AXES, split_axis=0, concat_axis=0, tiled=True)  10.8 us
    pallas_call x1, Pallas kernels, outer(): pl.pallas_call(functools.partial(outer_kernel, channels, height, breadth)...  7.42 us
    pallas_call x1, Pallas kernels, reorder(): pl.pallas_call(reorder_kernel, grid=(breadth // lanes, height // step), i...  7.34 us
    all_to_all x1, starting transfers between devices, body(): lax.all_to_all(packed, AXES, split_axis=0, concat_axis=0, tiled=True)  6.69 us
    ppermute x6, starting transfers between devices, total_over_devices(): lax.ppermute(value, AXES, [(i, i ^ step) for i in range(devices)])  6.68 us
  transfers between devices with their start and end apart: 11, of which 7 were waited for; matrix products, arithmetic and copies ran while one was open for 4% of the time, Pallas kernels for 30%

profile of v3, /device:TPU:0, one launch (start us, length us, event | category | flops | bytes accessed | tf_op | source)
XLA Modules:
  0.0 124.0 jit_solution(11154440384164678237)
XLA Ops:
  0.6 0.0 copy-start.6
  0.7 7.3 %reorder.1 = (bf16[2048,512]{1,0:T(8,128)(2,1)}, bf16[2048,512]{1,0:T(8,128)(2,1)}, bf16[16,2048]{1,0:T(8,128)(2,1)}, bf16[16,2048]{1,0:T(8,128)(2,1)}, bf16[256...) custom-call(bf16[64,32,512]{2,1,0:T(8,128)(2,1)} %w_ref.1, ...), custom_call_target="tpu_custom_call" | custom-call | tf_op jit(solution)/shard_map/reorder/pallas_call | solution.py:137
  8.0 2.4 %collective-permute-start = (bf16[16,2048]{1,0:T(8,128)(2,1)}, bf16[16,2048]{1,0:T(8,128)(2,1)S(1)}, u32[]{:S(2)}, u32[]{:S(2)}) collective-permute-start(bf16[16,2048]{1,0:T(8,128)(2,1)} %get-tuple-element.33), channel_id=1, source_target_pairs={{0,1},{1,2},{2,3},{4,5},{5,6},{6,7},{8,9},{9,10},{10,11},{12,13},{... | collective-permute-start | bytes 196616 | tf_op jit(solution)/shard_map/ppermute | solution.py:777
  10.4 1.3 %collective-permute-start.1 = (bf16[16,2048]{1,0:T(8,128)(2,1)}, bf16[16,2048]{1,0:T(8,128)(2,1)S(1)}, u32[]{:S(2)}, u32[]{:S(2)}) collective-permute-start(bf16[16,2048]{1,0:T(8,128)(2,1)} %get-tuple-element.34), channel_id=1, source_target_pairs={{1,0},{2,1},{3,2},{5,4},{6,5},{7,6},{9,8},{10,9},{11,10},{13,12},{... | collective-permute-start | bytes 196616 | tf_op jit(solution)/shard_map/ppermute | solution.py:777
  11.7 0.1 eq.13
  11.8 0.2 convert_reduce_fusion
  12.0 0.1 reduce_sum.21
  12.1 0.1 add.94
  12.1 0.1 add.85
  12.2 0.1 add.86
  12.3 0.1 add.88
  12.4 0.1 select_reduce_fusion
  12.5 0.6 broadcast_add_fusion.target_ref
  13.1 0.1 convert_element_type.15
  13.2 0.1 broadcast_in_dim.32
  13.3 0.1 convert_element_type.16
  13.4 0.0 collective-permute-done
  13.4 2.4 %collective-permute-done.1 = bf16[16,2048]{1,0:T(8,128)(2,1)S(1)} collective-permute-done((bf16[16,2048]{1,0:T(8,128)(2,1)}, bf16[16,2048]{1,0:T(8,128)(2,1)S(1)}, u32[]{:S(2)}, u32[]{:S(2)}) %collective-permute-start.1) | collective-permute-done | bytes 65568 | tf_op jit(solution)/shard_map/ppermute | solution.py:777
  15.9 1.0 pad_maximum_fusion
  16.9 1.3 %collective-permute-start.3 = (bf16[272,512]{1,0:T(8,128)(2,1)S(1)}, bf16[272,512]{1,0:T(8,128)(2,1)S(1)}, u32[]{:S(2)}, u32[]{:S(2)}) collective-permute-start(bf16[272,512]{1,0:T(8,128)(2,1)S(1)} %pad_maximum_fusion), channel_id=1, source_target_pairs={{4,0},{8,4},{12,8},{16,12},{20,16},{24,20},{28,24},{5,1},{9,5},{13... | collective-permute-start | bytes 835592 | tf_op jit(solution)/shard_map/ppermute | solution.py:784
  18.2 1.0 fusion.1
  19.2 5.3 %collective-permute-start.2 = (bf16[272,512]{1,0:T(8,128)(2,1)S(1)}, bf16[272,512]{1,0:T(8,128)(2,1)}, u32[]{:S(2)}, u32[]{:S(2)}) collective-permute-start(bf16[272,512]{1,0:T(8,128)(2,1)S(1)} %fusion.1), channel_id=1, source_target_pairs={{0,4},{4,8},{8,12},{12,16},{16,20},{20,24},{24,28},{1,5},{5,9},{9,... | collective-permute-start | bytes 835592 | tf_op jit(solution)/shard_map/ppermute | solution.py:783
  24.5 0.7 broadcast_in_dim.33.label_ref
  25.1 18.3 %inner.1 = (bf16[32,272,128]{2,1,0:T(8,128)(2,1)}, bf16[2176,640]{1,0:T(8,128)(2,1)}, bf16[2176,640]{1,0:T(8,128)(2,1)}, bf16[2048,640]{1,0:T(8,128)(2,1)}, bf16[256,512]{1,0:T(8,128)(2,1)}) custom-call(bf16[2048,512]{1,0:T(8,128)(2,1)} %get-tuple-element.30.xw_ref, bf16[2048,512]{1,0:T(8,128)(2,1)} %get-tuple-element.31.xc_ref, bf16[16,2048]{1,0:T(8,128)(2,1)} %copy-done.1, ...), custom_call_target="tpu_custom_call" | custom-call | flops 6039797760 | bytes 20000000 | tf_op jit(solution)/shard_map/inner/pallas_call | solution.py:328
  43.4 0.0 copy-start.2
  43.4 0.0 collective-permute-done.2.up_ref
  43.4 0.7 copy-done.2
  44.1 7.4 %outer.1 = (bf16[32,272,128]{2,1,0:T(8,128)(2,1)}, bf16[2176,640]{1,0:T(8,128)(2,1)}, bf16[2176,640]{1,0:T(8,128)(2,1)}, bf16[2048,640]{1,0:T(8,128)(2,1)}) custom-call(bf16[2048,512]{1,0:T(8,128)(2,1)} %get-tuple-element.30.xw_ref, ...), custom_call_target="tpu_custom_call", output_to_operand_aliasing={{0}: (11, {}), {1}: (12, {}), {2}: (13, {}), {3}: (14, {})} | custom-call | tf_op jit(solution)/shard_map/outer/pallas_call | solution.py:505
  51.6 6.7 %all-to-all-start = ((bf16[32,272,128]{2,1,0:T(8,128)(2,1)}), bf16[32,272,128]{2,1,0:T(8,128)(2,1)}, u32[]{:S(2)}, u32[]{:S(2)}) async-start(bf16[32,272,128]{2,1,0:T(8,128)(2,1)} %get-tuple-element.48), calls=%async_computation | async-start | bytes 4456448 | tf_op jit(solution)/shard_map/all_to_all | solution.py:798
  58.3 12.6 %correlate.1 = f32[584,128]{1,0:T(8,128)} custom-call(bf16[2176,640]{1,0:T(8,128)(2,1)} %get-tuple-element.45.act_in_ref, bf16[2176,640]{1,0:T(8,128)(2,1)} %get-tuple-element.46.act_mid_ref, bf16[2048,640]{1,0:T(8,128)(2,1)} %get-tuple-element.47.g_ref, bf16[2048,512]{1,0:T(8,128)(2,1)} %get-tuple-element.31.xc_ref), custom_call_target="tpu_custom_call" | custom-call | flops 3221225472 | bytes 10000000 | tf_op jit(solution)/shard_map/correlate/pallas_call | solution.py:607
  70.9 0.9 pad_dynamic-slice_fusion
  71.8 0.1 collective-permute-start.4
  71.9 1.4 %collective-permute-done.4 = f32[296,128]{1,0:T(8,128)S(1)} collective-permute-done((f32[296,128]{1,0:T(8,128)S(1)}, f32[296,128]{1,0:T(8,128)S(1)}, u32[]{:S(2)}, u32[]{:S(2)}) %collective-permute-start.4) | collective-permute-done | bytes 151584 | tf_op jit(solution)/shard_map/ppermute | solution.py:730
  73.3 0.9 fusion.2
  74.2 1.6 %collective-permute-start.5 = (f32[296,128]{1,0:T(8,128)S(1)}, f32[296,128]{1,0:T(8,128)S(1)}, u32[]{:S(2)}, u32[]{:S(2)}) collective-permute-start(f32[296,128]{1,0:T(8,128)S(1)} %fusion.2), channel_id=1, source_target_pairs={{0,2},{1,3},{2,0},{3,1},{4,6},{5,7},{6,4},{7,5},{8,10},{9,11},{10,... | collective-permute-start | bytes 454664 | tf_op jit(solution)/shard_map/ppermute | solution.py:730
  75.8 8.0 %collective-permute-done.5 = f32[296,128]{1,0:T(8,128)S(1)} collective-permute-done((f32[296,128]{1,0:T(8,128)S(1)}, f32[296,128]{1,0:T(8,128)S(1)}, u32[]{:S(2)}, u32[]{:S(2)}) %collective-permute-start.5) | collective-permute-done | bytes 151584 | tf_op jit(solution)/shard_map/ppermute | solution.py:730
  83.8 2.4 %collective-permute-start.6 = (f32[296,128]{1,0:T(8,128)S(1)}, f32[296,128]{1,0:T(8,128)S(1)}, u32[]{:S(2)}, u32[]{:S(2)}) collective-permute-start(f32[296,128]{1,0:T(8,128)S(1)} %add.100), channel_id=1, source_target_pairs={{0,4},{1,5},{2,6},{3,7},{4,0},{5,1},{6,2},{7,3},{8,12},{9,13},{10,... | collective-permute-start | bytes 454664 | tf_op jit(solution)/shard_map/ppermute | solution.py:730
  86.2 6.3 %collective-permute-done.6 = f32[296,128]{1,0:T(8,128)S(1)} collective-permute-done((f32[296,128]{1,0:T(8,128)S(1)}, f32[296,128]{1,0:T(8,128)S(1)}, u32[]{:S(2)}, u32[]{:S(2)}) %collective-permute-start.6) | collective-permute-done | bytes 151584 | tf_op jit(solution)/shard_map/ppermute | solution.py:730
  92.6 0.1 collective-permute-start.7
  92.6 7.5 %collective-permute-done.7 = f32[296,128]{1,0:T(8,128)S(1)} collective-permute-done((f32[296,128]{1,0:T(8,128)S(1)}, f32[296,128]{1,0:T(8,128)S(1)}, u32[]{:S(2)}, u32[]{:S(2)}) %collective-permute-start.7) | collective-permute-done | bytes 151584 | tf_op jit(solution)/shard_map/ppermute | solution.py:730
  100.2 2.5 %collective-permute-start.8 = (f32[296,128]{1,0:T(8,128)S(1)}, f32[296,128]{1,0:T(8,128)S(1)}, u32[]{:S(2)}, u32[]{:S(2)}) collective-permute-start(f32[296,128]{1,0:T(8,128)S(1)} %add.102), channel_id=1, source_target_pairs={{0,16},{1,17},{2,18},{3,19},{4,20},{5,21},{6,22},{7,23},{8,24},{9,... | collective-permute-start | bytes 454664 | tf_op jit(solution)/shard_map/ppermute | solution.py:730
  102.7 10.8 %all-to-all-done.arrived_ref.label_ref = bf16[32,272,128]{2,1,0:T(8,128)(2,1)} async-done(((bf16[32,272,128]{2,1,0:T(8,128)(2,1)}), bf16[32,272,128]{2,1,0:T(8,128)(2,1)}, u32[]{:S(2)}, u32[]{:S(2)}) %all-to-all-start) | async-done | bytes 2228256 | tf_op jit(solution)/shard_map/all_to_all | solution.py:798
  113.4 6.5 %unpack.1 = f32[64,2,2,8,512]{4,3,2,1,0:T(8,128)} custom-call(bf16[32,272,128]{2,1,0:T(8,128)(2,1)} %all-to-all-done.arrived_ref.label_ref, bf16[32,272,128]{2,1,0:T(8,128)(2,1)} %all-to-all-done.arrived_ref.label_ref), custom_call_target="tpu_custom_call" | custom-call | tf_op jit(solution)/shard_map/unpack/pallas_call | solution.py:671
  119.9 0.0 collective-permute-done.8
  120.0 0.1 collective-permute-start.9
  120.0 1.4 %collective-permute-done.9.other_ref = f32[296,128]{1,0:T(8,128)S(1)} collective-permute-done((f32[296,128]{1,0:T(8,128)S(1)}, f32[296,128]{1,0:T(8,128)S(1)}, u32[]{:S(2)}, u32[]{:S(2)}) %collective-permute-start.9) | collective-permute-done | bytes 151584 | tf_op jit(solution)/shard_map/ppermute | solution.py:730
  121.4 0.7 copy-done.3
  122.1 1.9 %finish.1 = (f32[3,3,64,64]{3,2,1,0:T(8,128)}, f32[3,3,64,64]{3,2,1,0:T(8,128)}, f32[1,64]{1,0:T(1,128)}, f32[1,64]{1,0:T(1,128)}) custom-call(f32[296,128]{1,0:T(8,128)} %copy-done, f32[296,128]{1,0:T(8,128)} %copy-done.3), custom_call_target="tpu_custom_call" | custom-call | tf_op jit(solution)/shard_map/finish/pallas_call | solution.py:715
  (23 shorter events, 0.2 us)
Async XLA Ops:
  0.6 15.3 %copy-start.6 = (pred[512]{0:T(512)(128)(4,1)S(1)}, pred[512]{0:T(512)(128)(4,1)}, u32[]{:S(2)}) copy-start(pred[512]{0:T(512)(128)(4,1)} %constant.15.clone.1) | copy-start | bytes 1540
  0.6 11.0 %copy-start.4 = (s32[2,32]{1,0:T(2,128)S(1)}, s32[2,32]{1,0:T(2,128)}, u32[]{:S(2)}) copy-start(s32[2,32]{1,0:T(2,128)} %param.12) | copy-start | bytes 772
  0.7 11.4 %copy-start.5 = (s32[2,32]{1,0:T(2,128)S(1)}, s32[2,32]{1,0:T(2,128)}, u32[]{:S(2)}) copy-start(s32[2,32]{1,0:T(2,128)} %param.13) | copy-start | bytes 772
  8.0 5.4 %collective-permute-start = (bf16[16,2048]{1,0:T(8,128)(2,1)}, bf16[16,2048]{1,0:T(8,128)(2,1)S(1)}, u32[]{:S(2)}, u32[]{:S(2)}) collective-permute-start(bf16[16,2048]{1,0:T(8,128)(2,1)} %get-tuple-element.33), channel_id=1, source_target_pairs={{0,1},{1,2},{2,3},{4,5},{5,6},{6,7},{8,9},{9,10},{10,11},{12,13},{... | collective-permute-start | bytes 196616 | tf_op jit(solution)/shard_map/ppermute | solution.py:777
  10.4 5.5 %collective-permute-start.1 = (bf16[16,2048]{1,0:T(8,128)(2,1)}, bf16[16,2048]{1,0:T(8,128)(2,1)S(1)}, u32[]{:S(2)}, u32[]{:S(2)}) collective-permute-start(bf16[16,2048]{1,0:T(8,128)(2,1)} %get-tuple-element.34), channel_id=1, source_target_pairs={{1,0},{2,1},{3,2},{5,4},{6,5},{7,6},{9,8},{10,9},{11,10},{13,12},{... | collective-permute-start | bytes 196616 | tf_op jit(solution)/shard_map/ppermute | solution.py:777
  15.9 9.2 %copy-start.1 = (bf16[16,2048]{1,0:T(8,128)(2,1)}, bf16[16,2048]{1,0:T(8,128)(2,1)S(1)}, u32[]{:S(2)}) copy-start(bf16[16,2048]{1,0:T(8,128)(2,1)S(1)} %add.83.side_ref) | copy-start | bytes 196612
  16.9 26.5 %collective-permute-start.3 = (bf16[272,512]{1,0:T(8,128)(2,1)S(1)}, bf16[272,512]{1,0:T(8,128)(2,1)S(1)}, u32[]{:S(2)}, u32[]{:S(2)}) collective-permute-start(bf16[272,512]{1,0:T(8,128)(2,1)S(1)} %pad_maximum_fusion), channel_id=1, source_target_pairs={{4,0},{8,4},{12,8},{16,12},{20,16},{24,20},{28,24},{5,1},{9,5},{13... | collective-permute-start | bytes 835592 | tf_op jit(solution)/shard_map/ppermute | solution.py:784
  19.2 24.2 %collective-permute-start.2 = (bf16[272,512]{1,0:T(8,128)(2,1)S(1)}, bf16[272,512]{1,0:T(8,128)(2,1)}, u32[]{:S(2)}, u32[]{:S(2)}) collective-permute-start(bf16[272,512]{1,0:T(8,128)(2,1)S(1)} %fusion.1), channel_id=1, source_target_pairs={{0,4},{4,8},{8,12},{12,16},{16,20},{20,24},{24,28},{1,5},{5,9},{9,... | collective-permute-start | bytes 835592 | tf_op jit(solution)/shard_map/ppermute | solution.py:783
  43.4 0.7 copy-start.2
  51.6 61.9 %all-to-all-start = ((bf16[32,272,128]{2,1,0:T(8,128)(2,1)}), bf16[32,272,128]{2,1,0:T(8,128)(2,1)}, u32[]{:S(2)}, u32[]{:S(2)}) async-start(bf16[32,272,128]{2,1,0:T(8,128)(2,1)} %get-tuple-element.48), calls=%async_computation | async-start | bytes 4456448 | tf_op jit(solution)/shard_map/all_to_all | solution.py:798
  71.8 1.4 %collective-permute-start.4 = (f32[296,128]{1,0:T(8,128)S(1)}, f32[296,128]{1,0:T(8,128)S(1)}, u32[]{:S(2)}, u32[]{:S(2)}) collective-permute-start(f32[296,128]{1,0:T(8,128)S(1)} %pad_dynamic-slice_fusion), channel_id=1, source_target_pairs={{0,1},{1,0},{2,3},{3,2},{4,5},{5,4},{6,7},{7,6},{8,9},{9,8},{10,11... | collective-permute-start | bytes 454664 | tf_op jit(solution)/shard_map/ppermute | solution.py:730
  74.2 9.6 %collective-permute-start.5 = (f32[296,128]{1,0:T(8,128)S(1)}, f32[296,128]{1,0:T(8,128)S(1)}, u32[]{:S(2)}, u32[]{:S(2)}) collective-permute-start(f32[296,128]{1,0:T(8,128)S(1)} %fusion.2), channel_id=1, source_target_pairs={{0,2},{1,3},{2,0},{3,1},{4,6},{5,7},{6,4},{7,5},{8,10},{9,11},{10,... | collective-permute-start | bytes 454664 | tf_op jit(solution)/shard_map/ppermute | solution.py:730
  83.8 8.7 %collective-permute-start.6 = (f32[296,128]{1,0:T(8,128)S(1)}, f32[296,128]{1,0:T(8,128)S(1)}, u32[]{:S(2)}, u32[]{:S(2)}) collective-permute-start(f32[296,128]{1,0:T(8,128)S(1)} %add.100), channel_id=1, source_target_pairs={{0,4},{1,5},{2,6},{3,7},{4,0},{5,1},{6,2},{7,3},{8,12},{9,13},{10,... | collective-permute-start | bytes 454664 | tf_op jit(solution)/shard_map/ppermute | solution.py:730
  92.6 7.6 %collective-permute-start.7 = (f32[296,128]{1,0:T(8,128)S(1)}, f32[296,128]{1,0:T(8,128)S(1)}, u32[]{:S(2)}, u32[]{:S(2)}) collective-permute-start(f32[296,128]{1,0:T(8,128)S(1)} %add.101), channel_id=1, source_target_pairs={{0,8},{1,9},{2,10},{3,11},{4,12},{5,13},{6,14},{7,15},{8,0},{9,1},... | collective-permute-start | bytes 454664 | tf_op jit(solution)/shard_map/ppermute | solution.py:730
  100.2 19.8 %collective-permute-start.8 = (f32[296,128]{1,0:T(8,128)S(1)}, f32[296,128]{1,0:T(8,128)S(1)}, u32[]{:S(2)}, u32[]{:S(2)}) collective-permute-start(f32[296,128]{1,0:T(8,128)S(1)} %add.102), channel_id=1, source_target_pairs={{0,16},{1,17},{2,18},{3,19},{4,20},{5,21},{6,22},{7,23},{8,24},{9,... | collective-permute-start | bytes 454664 | tf_op jit(solution)/shard_map/ppermute | solution.py:730
  120.0 1.5 %copy-start = (f32[296,128]{1,0:T(8,128)}, f32[296,128]{1,0:T(8,128)S(1)}, u32[]{:S(2)}) copy-start(f32[296,128]{1,0:T(8,128)S(1)} %add.103.total_ref) | copy-start | bytes 454660
  120.0 1.4 %collective-permute-start.9 = (f32[296,128]{1,0:T(8,128)S(1)}, f32[296,128]{1,0:T(8,128)S(1)}, u32[]{:S(2)}, u32[]{:S(2)}) collective-permute-start(f32[296,128]{1,0:T(8,128)S(1)} %add.103.total_ref), channel_id=1, source_target_pairs={{0,1},{1,0},{2,3},{3,2},{4,5},{5,4},{6,7},{7,6},{8,9},{9,8},{10,11... | collective-permute-start | bytes 454664 | tf_op jit(solution)/shard_map/ppermute | solution.py:730
  121.4 0.7 copy-start.3

commit v4 on v3

--- a/solution.py
+++ b/solution.py
@@ -36,16 +36,12 @@
 
 
 def shifted(value):
-    wide = value.shape[1]
-    return (
-        pltpu.roll(value, 1, 1).astype(BF16),
-        value.astype(BF16),
-        pltpu.roll(value, wide - 1, 1).astype(BF16),
-    )
+    value = value.astype(BF16)
+    return pltpu.roll(value, 1, 1), value, pltpu.roll(value, value.shape[1] - 1, 1)
 
 
 def slope_of(value, sigma):
-    return sigma * (1.0 + value * (1.0 - sigma))
+    return sigma + value * sigma * (1.0 - sigma)
 
 
 def at_row(row, rows, channels):
@@ -93,12 +89,14 @@
     @pl.when(pl.program_id(1) == 0)
     def _():
         to_up_ref[0:rim, :] = kept[0][0:rim]
-        to_up_ref[rim:, :] = kept[1][0:rim]
+        to_up_ref[rim : 2 * rim, :] = kept[1][0:rim]
+        to_up_ref[2 * rim :, :] = jnp.zeros((16, lanes), BF16)
 
     @pl.when(pl.program_id(1) == pl.num_programs(1) - 1)
     def _():
         to_down_ref[0:rim, :] = kept[0][rows * channels - rim :]
-        to_down_ref[rim:, :] = kept[1][rows * channels - rim :]
+        to_down_ref[rim : 2 * rim, :] = kept[1][rows * channels - rim :]
+        to_down_ref[2 * rim :, :] = jnp.zeros((16, lanes), BF16)
 
     here = pl.ds(pl.multiple_of(pl.program_id(1) * rows * channels, 128), rows * channels)
 
@@ -124,14 +122,14 @@
     channels, height, breadth = warped.shape
     whole = lambda shape: pl.BlockSpec(shape, lambda x, h: (0,) * len(shape))
     step = 16
-    lanes = 256
+    lanes = breadth
     spec_in = pl.BlockSpec((channels, step, lanes), lambda x, h: (0, h, x))
     spec_out = pl.BlockSpec((step * channels, lanes), lambda x, h: (h, x))
     spec_edge = pl.BlockSpec((16, height * channels), lambda x, h: (0, 0))
-    spec_rim = pl.BlockSpec((4 * channels, lanes), lambda x, h: (0, x))
+    spec_rim = pl.BlockSpec((4 * channels + 16, lanes), lambda x, h: (0, x))
     shape = jax.ShapeDtypeStruct((height * channels, breadth), BF16)
     edge = jax.ShapeDtypeStruct((16, height * channels), BF16)
-    rim = jax.ShapeDtypeStruct((4 * channels, breadth), BF16)
+    rim = jax.ShapeDtypeStruct((4 * channels + 16, breadth), BF16)
     weights = jax.ShapeDtypeStruct((2 * channels, 12 * channels), BF16)
     bias = jax.ShapeDtypeStruct((2 * channels, 2 * channels), F32)
     return pl.pallas_call(
@@ -191,7 +189,7 @@
     channels, height, breadth,
     xw_ref, xc_ref, side_ref, w1_ref, w2f_ref, w1f_ref, bias_ref, target_ref, label_ref,
     packed_ref, act_in_ref, act_mid_ref, g_ref, gw_mid_ref,
-    wx, cx, sa, sc, sg, gw, act_in, act_mid, grads, packed, sem_in, sem_out,
+    wx, cx, sa, sc, sg, gw, act_in, act_mid, grads, packed, label_rows, sem_in, sem_out,
 ):
     ch = channels
     wide = breadth + 128
@@ -212,7 +210,7 @@
         pltpu.make_async_copy(act_mid, act_mid_ref.at[2 * ch : height * ch, :], sem_out.at[1]),
         pltpu.make_async_copy(grads, g_ref.at[ch : (height - 1) * ch, :], sem_out.at[2]),
         pltpu.make_async_copy(
-            label_ref, packed_ref.at[:, DEPTH * CAP * BLOCK : DEPTH * CAP * BLOCK + 16, :], sem_out.at[3]
+            label_rows, packed_ref.at[:, DEPTH * CAP * BLOCK : DEPTH * CAP * BLOCK + 16, :], sem_out.at[3]
         ),
         pltpu.make_async_copy(
             gw.at[(BLOCK - 2) * ch : (BLOCK + 2) * ch, :], gw_mid_ref, sem_out.at[4]
@@ -220,6 +218,14 @@
     ]
     for load in loads:
         load.start()
+    upper = lax.broadcasted_iota(jnp.int32, (16, 128), 1) >= 128 // CAP
+
+    def label(device, _):
+        owner = jnp.where(upper, label_ref[device * CAP + 1], label_ref[device * CAP])
+        label_rows[device] = owner.astype(F32).astype(BF16)
+        return 0
+
+    lax.fori_loop(0, label_rows.shape[0], label, 0, unroll=4)
     stores[3].start()
     wx[:, rim] = spread_sides(side_ref[...], 0)
     cx[:, rim] = spread_sides(side_ref[...], 2)
@@ -232,16 +238,11 @@
         act_in[here, :] = moved[1]
         for shift in range(3):
             sa[pl.ds(out + shift * ch, ch), :] = moved[shift]
-        moved = shifted(cx[here, :].astype(F32))
+        moved = shifted(cx[here, :])
         for shift in range(3):
             sc[pl.ds(out + shift * ch, ch), :] = moved[shift]
         return 0
 
-    for at in range(4):
-        loads[2 * at].wait()
-        loads[2 * at + 1].wait()
-        lax.fori_loop(at * height // 4, (at + 1) * height // 4, prepare, 0, unroll=UNROLL_PREPARE)
-    stores[0].start()
     rim_ok = rim_mask(ch)
 
     def middle(pair, _):
@@ -260,7 +261,17 @@
             sg[at_row(row * 3 + 3 + shift, 1, ch), :] = moved[shift][ch:]
         return 0
 
-    lax.fori_loop(0, height // 2 - 1, middle, 0, unroll=UNROLL_MIDDLE)
+    quarter = height // 4
+    done = 0
+    for at in range(4):
+        loads[2 * at].wait()
+        loads[2 * at + 1].wait()
+        lax.fori_loop(at * quarter, (at + 1) * quarter, prepare, 0, unroll=UNROLL_PREPARE)
+        if at == 3:
+            stores[0].start()
+        ready = (at + 1) * quarter // 2 - 1
+        lax.fori_loop(done, ready, middle, 0, unroll=True)
+        done = ready
     stores[1].start()
     stores[2].start()
 
@@ -292,7 +303,7 @@
         return 0
 
     rows_to = CAP * BLOCK
-    lax.fori_loop(0, packed.shape[0] * rows_to // size, pack, 0)
+    lax.fori_loop(0, packed.shape[0] * rows_to // size, pack, 0, unroll=4)
     for at in range(1, DEPTH - 1):
         stores.append(
             pltpu.make_async_copy(
@@ -309,7 +320,7 @@
 DEPTH = 8
 UNROLL_PREPARE = 8
 UNROLL_MIDDLE = 5
-UNROLL_LAST = 7
+UNROLL_LAST = 14
 
 
 def inner(sizes, operands, slots):
@@ -327,7 +338,9 @@
     flops = 2 * 3 * 12 * channels * 2 * channels * wide * (height // 2)
     return pl.pallas_call(
         functools.partial(inner_kernel, channels, height, breadth),
-        in_specs=[hbm, hbm] + [vmem] * (len(operands) - 3) + [hbm],
+        in_specs=[hbm, hbm]
+        + [vmem] * (len(operands) - 3)
+        + [pl.BlockSpec(memory_space=pltpu.SMEM)],
         out_specs=[hbm] * len(outs),
         out_shape=outs,
         scratch_shapes=[
@@ -341,6 +354,7 @@
             pltpu.VMEM(((height - 2) * channels, wide), BF16),
             pltpu.VMEM(((height - 2) * channels, wide), BF16),
             pltpu.VMEM((slots // CAP, CAP * BLOCK, (BLOCK - 4) * channels), BF16),
+            pltpu.VMEM((slots // CAP, 16, 128), BF16),
             pltpu.SemaphoreType.DMA((8,)),
             pltpu.SemaphoreType.DMA((3 + DEPTH,)),
         ],
@@ -352,12 +366,12 @@
 
 def outer_kernel(
     channels, height, breadth,
-    xw_ref, xc_ref, up_ref, down_ref, side_ref,
-    w1_ref, w2f_ref, w1f_ref, bias_ref, target_ref, gw_mid_ref,
+    xw_ref, xc_ref, up_ref, down_ref, side_hbm,
+    w1_hbm, w2f_hbm, w1f_hbm, bias_hbm, target_hbm, gw_mid_hbm,
     packed_in, act_in_in, act_mid_in, g_in,
     packed_ref, act_in_ref, act_mid_ref, g_ref,
     wx, cx, sa_both, sc_both, sg_both, near, gw, act_in, act_mid, grads, packed, chosen, corner,
-    sem_in, sem_out,
+    side_ref, w1_ref, w2f_ref, w1f_ref, bias_ref, target_ref, gw_mid_ref, sem_in, sem_out,
 ):
     ch = channels
     wide = breadth + 128
@@ -372,6 +386,8 @@
         copy.start()
         loads.append(copy)
 
+    load(target_hbm, target_ref)
+    load(side_hbm, side_ref)
     load(up_ref.at[2 * rows2 : 2 * rows2 + 16, 0:rows2], corner.at[0])
     load(down_ref.at[2 * rows2 : 2 * rows2 + 16, 0:rows2], corner.at[1])
     load(xw_ref.at[0:rows2, :], wx.at[rows2 : 2 * rows2, core])
@@ -384,6 +400,13 @@
     load(down_ref.at[rows2 : 2 * rows2, :], cx.at[3 * rows2 : 4 * rows2, core])
     load(g_in.at[ch : 3 * ch, :], near.at[0:rows2, :])
     load(g_in.at[body - 3 * ch : body - ch, :], near.at[rows2 : 2 * rows2, :])
+    load(w1_hbm, w1_ref)
+    load(w2f_hbm, w2f_ref)
+    load(bias_hbm, bias_ref)
+    load(w1f_hbm, w1f_ref)
+    load(gw_mid_hbm, gw_mid_ref)
+    loads[0].wait()
+    loads[1].wait()
     for target, first in ((wx, 0), (cx, 2)):
         target[rows2 : 2 * rows2, rim] = spread_sides(side_ref[:, 0:rows2], first)
         target[2 * rows2 : 3 * rows2, rim] = spread_sides(side_ref[:, body - rows2 : body], first)
@@ -397,8 +420,8 @@
             )
         return 0
 
-    lax.fori_loop(0, chosen.shape[0] // size, choose, 0)
-    for copy in loads:
+    lax.fori_loop(0, chosen.shape[0] // size, choose, 0, unroll=4)
+    for copy in loads[2:]:
         copy.wait()
     for target, first in ((wx, 0), (cx, 2)):
         target[0:rows2, rim] = spread_sides(corner[0], first)
@@ -417,7 +440,7 @@
                 act_in[half * ch : (half + 1) * ch, :] = moved[1]
             for shift in range(3):
                 sa[(row * 3 + shift) * ch : (row * 3 + shift + 1) * ch, :] = moved[shift]
-            moved = shifted(cx[here, :].astype(F32))
+            moved = shifted(cx[here, :])
             for shift in range(3):
                 sc[(row * 3 + shift) * ch : (row * 3 + shift + 1) * ch, :] = moved[shift]
         here = slice(base + ch, base + 3 * ch)
@@ -489,7 +512,7 @@
         )
         return 0
 
-    lax.fori_loop(0, chosen.shape[0] // size, pack, 0)
+    lax.fori_loop(0, chosen.shape[0] // size, pack, 0, unroll=4)
     for store in stores[6:]:
         store.start()
     for store in stores:
@@ -499,14 +522,11 @@
 def outer(sizes, operands, state, slots):
     channels, height, breadth = sizes
     wide = breadth + 128
-    vmem = pl.BlockSpec(memory_space=pltpu.VMEM)
     hbm = pl.BlockSpec(memory_space=pl.ANY)
     inputs = len(operands)
     return pl.pallas_call(
         functools.partial(outer_kernel, channels, height, breadth),
-        in_specs=[hbm] * 4
-        + [vmem] * (len(operands) - 4)
-        + [hbm] * len(state),
+        in_specs=[hbm] * (inputs + len(state)),
         out_specs=[hbm] * len(state),
         out_shape=[jax.ShapeDtypeStruct(item.shape, item.dtype) for item in state],
         input_output_aliases={inputs + at: at for at in range(len(state))},
@@ -524,7 +544,8 @@
             pltpu.VMEM((slots // CAP, CAP * BLOCK, 4 * channels), BF16),
             pltpu.VMEM((slots * BLOCK, 2 * breadth), BF16),
             pltpu.VMEM((2, 16, 2 * channels), BF16),
-            pltpu.SemaphoreType.DMA((12,)),
+            *[pltpu.VMEM(item.shape, item.dtype) for item in operands[4:]],
+            pltpu.SemaphoreType.DMA((19,)),
             pltpu.SemaphoreType.DMA((8,)),
         ],
         compiler_params=params(),
@@ -766,10 +787,6 @@
     ).reshape(block_rows, breadth)
     hits = places[:, None] == jnp.arange(slots, dtype=jnp.int32)[None, :]
     labels = jnp.sum(jnp.where(hits, source_block.reshape(count, 1) + 1, 0), axis=0) - 1
-    labels = jnp.broadcast_to(
-        jnp.repeat(labels.reshape(devices, 1, CAP), 128 // CAP, axis=2), (devices, 16, 128)
-    ).astype(BF16)
-
     xw, xc, to_right, to_left, to_up, to_down, first, second_back, first_back, bias = reorder(
         warped, cotangent, w_first, w_second, b_first
     )
@@ -777,9 +794,8 @@
     side = lax.ppermute(to_right, "cols", shift_pairs("cols", 1)) + lax.ppermute(
         to_left, "cols", shift_pairs("cols", -1)
     )
-    fill = ((0, 0), (0, breadth - rim))
-    to_down = jnp.concatenate([to_down, jnp.pad(side[:, -rim:], fill)], axis=0)
-    to_up = jnp.concatenate([to_up, jnp.pad(side[:, :rim], fill)], axis=0)
+    to_down = lax.dynamic_update_slice(to_down, side[:, -rim:], (2 * rim, 0))
+    to_up = lax.dynamic_update_slice(to_up, side[:, :rim], (2 * rim, 0))
     up = lax.ppermute(to_down, "rows", shift_pairs("rows", 1))
     down = lax.ppermute(to_up, "rows", shift_pairs("rows", -1))
 

time: 125 us -> 117 us (0.936)
  Pallas kernels: 54 us -> 47.8 us
  starting transfers between devices: 23.6 us -> 26.5 us
  waiting for transfers between devices: 37.8 us -> 35.2 us
  other arithmetic: 3.88 us -> 2.43 us
    pallas_call x1, Pallas kernels: 18.3 us -> 15.1 us  [inner(): pl.pallas_call(functools.partial(inner_kernel, channels, height, breadth)...]
    ppermute x6, starting transfers between devices: 6.68 us -> 9.63 us  [total_over_devices(): lax.ppermute(value, AXES, [(i, i ^ step) for i in range(devices)])]
    ppermute x6, waiting for transfers between devices: 24.6 us -> 22.2 us  [total_over_devices(): lax.ppermute(value, AXES, [(i, i ^ step) for i in range(devices)])]
    concatenate x2 -> x0, other arithmetic: 1.94 us -> none  [the longest x1 0.97 us: body(): to_down = jnp.concatenate([to_down, jnp.pad(side[:, -rim:], fill)], axis=0)]
    ppermute x1, starting transfers between devices: 5.27 us -> 3.4 us  [body(): up = lax.ppermute(to_down, 'rows', shift_pairs('rows', 1))]
    pallas_call x1, Pallas kernels: 7.42 us -> 5.55 us  [outer(): pl.pallas_call(functools.partial(outer_kernel, channels, height, breadth)...]
    all_to_all x1, starting transfers between devices: 6.69 us -> 8.48 us  [body(): lax.all_to_all(packed, AXES, split_axis=0, concat_axis=0, tiled=True)]
  transfers between devices with their start and end apart: 11 -> 11, of which waited for: 7 -> 7; matrix products, arithmetic and copies ran while one was open for 4% -> 3% of each run, Pallas kernels for 30% -> 29%
where the time goes in v4:
time: 117 us; the launch traced here: 116 us
  Pallas kernels  47.8 us (41%)
  waiting for transfers between devices  35.2 us (30%)
  starting transfers between devices  26.5 us (23%)
  local copies, waits for them, and re-layouts  3.5 us (3%)
  other arithmetic  2.43 us (2%)
    ppermute x6, waiting for transfers between devices, total_over_devices(): lax.ppermute(value, AXES, [(i, i ^ step) for i in range(devices)])  22.2 us
    pallas_call x1, Pallas kernels, inner(): pl.pallas_call(functools.partial(inner_kernel, channels, height, breadth)...  15.1 us
    pallas_call x1, Pallas kernels, correlate(): pl.pallas_call(functools.partial(correlate_kernel, channels, height, brea...  12.2 us
    all_to_all x1, waiting for transfers between devices, body(): lax.all_to_all(packed, AXES, split_axis=0, concat_axis=0, tiled=True)  10.7 us
    ppermute x6, starting transfers between devices, total_over_devices(): lax.ppermute(value, AXES, [(i, i ^ step) for i in range(devices)])  9.63 us
    all_to_all x1, starting transfers between devices, body(): lax.all_to_all(packed, AXES, split_axis=0, concat_axis=0, tiled=True)  8.48 us
    pallas_call x1, Pallas kernels, reorder(): pl.pallas_call(reorder_kernel, grid=(breadth // lanes, height // step), i...  6.51 us
    pallas_call x1, Pallas kernels, unpack(): pl.pallas_call(functools.partial(unpack_kernel, channels), grid=(BLOCK //...  6.5 us
  transfers between devices with their start and end apart: 11, of which 7 were waited for; matrix products, arithmetic and copies ran while one was open for 3% of the time, Pallas kernels for 29%

profile of v4, /device:TPU:0, one launch (start us, length us, event | category | flops | bytes accessed | tf_op | source)
XLA Modules:
  0.0 116.3 jit_solution(15984423324478919177)
XLA Ops:
  0.7 6.5 %reorder.1 = (bf16[2048,512]{1,0:T(8,128)(2,1)}, bf16[2048,512]{1,0:T(8,128)(2,1)}, bf16[16,2048]{1,0:T(8,128)(2,1)}, bf16[16,2048]{1,0:T(8,128)(2,1)}, bf16[272...) custom-call(bf16[64,32,512]{2,1,0:T(8,128)(2,1)} %w_ref.1, ...), custom_call_target="tpu_custom_call" | custom-call | tf_op jit(solution)/shard_map/reorder/pallas_call | solution.py:135
  7.2 2.4 %collective-permute-start = (bf16[16,2048]{1,0:T(8,128)(2,1)}, bf16[16,2048]{1,0:T(8,128)(2,1)S(1)}, u32[]{:S(2)}, u32[]{:S(2)}) collective-permute-start(bf16[16,2048]{1,0:T(8,128)(2,1)} %get-tuple-element.33), channel_id=1, source_target_pairs={{0,1},{1,2},{2,3},{4,5},{5,6},{6,7},{8,9},{9,10},{10,11},{12,13},{... | collective-permute-start | bytes 196616 | tf_op jit(solution)/shard_map/ppermute | solution.py:794
  9.5 1.3 %collective-permute-start.1 = (bf16[16,2048]{1,0:T(8,128)(2,1)}, bf16[16,2048]{1,0:T(8,128)(2,1)S(1)}, u32[]{:S(2)}, u32[]{:S(2)}) collective-permute-start(bf16[16,2048]{1,0:T(8,128)(2,1)} %get-tuple-element.34), channel_id=1, source_target_pairs={{1,0},{2,1},{3,2},{5,4},{6,5},{7,6},{9,8},{10,9},{11,10},{13,12},{... | collective-permute-start | bytes 196616 | tf_op jit(solution)/shard_map/ppermute | solution.py:794
  10.9 0.1 eq.13
  10.9 0.2 convert_reduce_fusion
  11.1 0.1 reduce_sum.21
  11.2 0.1 add.80
  11.3 0.1 add.81
  11.4 0.1 add.83
  11.5 0.0 copy-done.6
  11.5 0.1 add.89
  11.6 0.6 broadcast_add_fusion.target_ref.target_hbm
  12.2 0.1 select_reduce_fusion
  12.3 0.5 broadcast_add_fusion.2.label_ref
  12.8 0.0 collective-permute-done
  12.8 2.2 %collective-permute-done.1 = bf16[16,2048]{1,0:T(8,128)(2,1)S(1)} collective-permute-done((bf16[16,2048]{1,0:T(8,128)(2,1)}, bf16[16,2048]{1,0:T(8,128)(2,1)S(1)}, u32[]{:S(2)}, u32[]{:S(2)}) %collective-permute-start.1) | collective-permute-done | bytes 65568 | tf_op jit(solution)/shard_map/ppermute | solution.py:794
  15.1 0.6 slice_dynamic-update-slice_fusion
  15.7 3.4 %collective-permute-start.2 = (bf16[272,512]{1,0:T(8,128)(2,1)}, bf16[272,512]{1,0:T(8,128)(2,1)S(1)}, u32[]{:S(2)}, u32[]{:S(2)}) collective-permute-start(bf16[272,512]{1,0:T(8,128)(2,1)} %get-tuple-element.56), channel_id=1, source_target_pairs={{0,4},{4,8},{8,12},{12,16},{16,20},{20,24},{24,28},{1,5},{5,9},{9,... | collective-permute-start | bytes 835592 | tf_op jit(solution)/shard_map/ppermute | solution.py:799
  19.1 1.3 %collective-permute-start.3 = (bf16[272,512]{1,0:T(8,128)(2,1)}, bf16[272,512]{1,0:T(8,128)(2,1)S(1)}, u32[]{:S(2)}, u32[]{:S(2)}) collective-permute-start(bf16[272,512]{1,0:T(8,128)(2,1)} %get-tuple-element.55), channel_id=1, source_target_pairs={{4,0},{8,4},{12,8},{16,12},{20,16},{24,20},{28,24},{5,1},{9,5},{13... | collective-permute-start | bytes 835592 | tf_op jit(solution)/shard_map/ppermute | solution.py:800
  20.4 15.1 %inner.1 = (bf16[32,272,128]{2,1,0:T(8,128)(2,1)}, bf16[2176,640]{1,0:T(8,128)(2,1)}, bf16[2176,640]{1,0:T(8,128)(2,1)}, bf16[2048,640]{1,0:T(8,128)(2,1)}, bf16[256,512]{1,0:T(8,128)(2,1)}) custom-call(bf16[2048,512]{1,0:T(8,128)(2,1)} %get-tuple-element.30.xw_ref, bf16[2048,512]{1,0:T(8,128)(2,1)} %get-tuple-element.31.xc_ref, bf16[16,2048]{1,0:T(8,128)(2,1)} %copy-done.1, ...), custom_call_target="tpu_custom_call" | custom-call | flops 6039797760 | bytes 20000000 | tf_op jit(solution)/shard_map/inner/pallas_call | solution.py:339
  35.5 0.0 collective-permute-done.2.up_ref
  35.5 0.0 copy-start.2
  35.5 0.0 collective-permute-done.3.down_ref
  35.6 0.0 copy-start.3
  35.6 0.7 copy-done.2
  36.2 0.1 copy-done.3
  36.3 5.6 %outer.1 = (bf16[32,272,128]{2,1,0:T(8,128)(2,1)}, bf16[2176,640]{1,0:T(8,128)(2,1)}, bf16[2176,640]{1,0:T(8,128)(2,1)}, bf16[2048,640]{1,0:T(8,128)(2,1)}) custom-call(bf16[2048,512]{1,0:T(8,128)(2,1)} %get-tuple-element.30.xw_ref, ...), custom_call_target="tpu_custom_call", output_to_operand_aliasing={{0}: (11, {}), {1}: (12, {}), {2}: (13, {}), {3}: (14, {})} | custom-call | tf_op jit(solution)/shard_map/outer/pallas_call | solution.py:527
  41.9 8.5 %all-to-all-start = ((bf16[32,272,128]{2,1,0:T(8,128)(2,1)}), bf16[32,272,128]{2,1,0:T(8,128)(2,1)}, u32[]{:S(2)}, u32[]{:S(2)}) async-start(bf16[32,272,128]{2,1,0:T(8,128)(2,1)} %get-tuple-element.48), calls=%async_computation | async-start | bytes 4456448 | tf_op jit(solution)/shard_map/all_to_all | solution.py:814
  50.4 12.2 %correlate.1 = f32[584,128]{1,0:T(8,128)} custom-call(bf16[2176,640]{1,0:T(8,128)(2,1)} %get-tuple-element.45.act_in_ref, bf16[2176,640]{1,0:T(8,128)(2,1)} %get-tuple-element.46.act_mid_ref, bf16[2048,640]{1,0:T(8,128)(2,1)} %get-tuple-element.47.g_ref, bf16[2048,512]{1,0:T(8,128)(2,1)} %get-tuple-element.31.xc_ref), custom_call_target="tpu_custom_call" | custom-call | flops 3221225472 | bytes 10000000 | tf_op jit(solution)/shard_map/correlate/pallas_call | solution.py:628
  62.6 0.9 pad_dynamic-slice_fusion
  63.5 0.3 collective-permute-start.4
  63.8 1.2 %collective-permute-done.4 = f32[296,128]{1,0:T(8,128)S(1)} collective-permute-done((f32[296,128]{1,0:T(8,128)S(1)}, f32[296,128]{1,0:T(8,128)S(1)}, u32[]{:S(2)}, u32[]{:S(2)}) %collective-permute-start.4) | collective-permute-done | bytes 151584 | tf_op jit(solution)/shard_map/ppermute | solution.py:751
  65.0 0.9 fusion
  65.9 1.8 %collective-permute-start.5 = (f32[296,128]{1,0:T(8,128)S(1)}, f32[296,128]{1,0:T(8,128)S(1)}, u32[]{:S(2)}, u32[]{:S(2)}) collective-permute-start(f32[296,128]{1,0:T(8,128)S(1)} %fusion), channel_id=1, source_target_pairs={{0,2},{1,3},{2,0},{3,1},{4,6},{5,7},{6,4},{7,5},{8,10},{9,11},{10,... | collective-permute-start | bytes 454664 | tf_op jit(solution)/shard_map/ppermute | solution.py:751
  67.7 5.7 %collective-permute-done.5 = f32[296,128]{1,0:T(8,128)S(1)} collective-permute-done((f32[296,128]{1,0:T(8,128)S(1)}, f32[296,128]{1,0:T(8,128)S(1)}, u32[]{:S(2)}, u32[]{:S(2)}) %collective-permute-start.5) | collective-permute-done | bytes 151584 | tf_op jit(solution)/shard_map/ppermute | solution.py:751
  73.5 5.0 %collective-permute-start.6 = (f32[296,128]{1,0:T(8,128)S(1)}, f32[296,128]{1,0:T(8,128)S(1)}, u32[]{:S(2)}, u32[]{:S(2)}) collective-permute-start(f32[296,128]{1,0:T(8,128)S(1)} %add.95), channel_id=1, source_target_pairs={{0,4},{1,5},{2,6},{3,7},{4,0},{5,1},{6,2},{7,3},{8,12},{9,13},{10,... | collective-permute-start | bytes 454664 | tf_op jit(solution)/shard_map/ppermute | solution.py:751
  78.4 6.3 %collective-permute-done.6 = f32[296,128]{1,0:T(8,128)S(1)} collective-permute-done((f32[296,128]{1,0:T(8,128)S(1)}, f32[296,128]{1,0:T(8,128)S(1)}, u32[]{:S(2)}, u32[]{:S(2)}) %collective-permute-start.6) | collective-permute-done | bytes 151584 | tf_op jit(solution)/shard_map/ppermute | solution.py:751
  84.7 0.1 collective-permute-start.7
  84.8 7.7 %collective-permute-done.7 = f32[296,128]{1,0:T(8,128)S(1)} collective-permute-done((f32[296,128]{1,0:T(8,128)S(1)}, f32[296,128]{1,0:T(8,128)S(1)}, u32[]{:S(2)}, u32[]{:S(2)}) %collective-permute-start.7) | collective-permute-done | bytes 151584 | tf_op jit(solution)/shard_map/ppermute | solution.py:751
  92.5 2.5 %collective-permute-start.8 = (f32[296,128]{1,0:T(8,128)S(1)}, f32[296,128]{1,0:T(8,128)S(1)}, u32[]{:S(2)}, u32[]{:S(2)}) collective-permute-start(f32[296,128]{1,0:T(8,128)S(1)} %add.97), channel_id=1, source_target_pairs={{0,16},{1,17},{2,18},{3,19},{4,20},{5,21},{6,22},{7,23},{8,24},{9,... | collective-permute-start | bytes 454664 | tf_op jit(solution)/shard_map/ppermute | solution.py:751
  95.0 10.7 %all-to-all-done.arrived_ref.label_ref = bf16[32,272,128]{2,1,0:T(8,128)(2,1)} async-done(((bf16[32,272,128]{2,1,0:T(8,128)(2,1)}), bf16[32,272,128]{2,1,0:T(8,128)(2,1)}, u32[]{:S(2)}, u32[]{:S(2)}) %all-to-all-start) | async-done | bytes 2228256 | tf_op jit(solution)/shard_map/all_to_all | solution.py:814
  105.7 6.5 %unpack.1 = f32[64,2,2,8,512]{4,3,2,1,0:T(8,128)} custom-call(bf16[32,272,128]{2,1,0:T(8,128)(2,1)} %all-to-all-done.arrived_ref.label_ref, bf16[32,272,128]{2,1,0:T(8,128)(2,1)} %all-to-all-done.arrived_ref.label_ref), custom_call_target="tpu_custom_call" | custom-call | tf_op jit(solution)/shard_map/unpack/pallas_call | solution.py:692
  112.2 0.0 collective-permute-done.8
  112.2 0.0 copy-start
  112.2 0.1 collective-permute-start.9
  112.3 1.4 %collective-permute-done.9.other_ref = f32[296,128]{1,0:T(8,128)S(1)} collective-permute-done((f32[296,128]{1,0:T(8,128)S(1)}, f32[296,128]{1,0:T(8,128)S(1)}, u32[]{:S(2)}, u32[]{:S(2)}) %collective-permute-start.9) | collective-permute-done | bytes 151584 | tf_op jit(solution)/shard_map/ppermute | solution.py:751
  113.7 0.7 copy-done.4
  114.4 1.9 %finish.1 = (f32[3,3,64,64]{3,2,1,0:T(8,128)}, f32[3,3,64,64]{3,2,1,0:T(8,128)}, f32[1,64]{1,0:T(1,128)}, f32[1,64]{1,0:T(1,128)}) custom-call(f32[296,128]{1,0:T(8,128)} %copy-done, f32[296,128]{1,0:T(8,128)} %copy-done.4), custom_call_target="tpu_custom_call" | custom-call | tf_op jit(solution)/shard_map/finish/pallas_call | solution.py:736
  (16 shorter events, 0.1 us)
Async XLA Ops:
  0.6 10.2 %copy-start.5 = (s32[2,32]{1,0:T(2,128)S(1)}, s32[2,32]{1,0:T(2,128)}, u32[]{:S(2)}) copy-start(s32[2,32]{1,0:T(2,128)} %param.12) | copy-start | bytes 772
  0.6 10.8 %copy-start.6 = (s32[2,32]{1,0:T(2,128)S(1)}, s32[2,32]{1,0:T(2,128)}, u32[]{:S(2)}) copy-start(s32[2,32]{1,0:T(2,128)} %param.13) | copy-start | bytes 772
  7.2 5.6 %collective-permute-start = (bf16[16,2048]{1,0:T(8,128)(2,1)}, bf16[16,2048]{1,0:T(8,128)(2,1)S(1)}, u32[]{:S(2)}, u32[]{:S(2)}) collective-permute-start(bf16[16,2048]{1,0:T(8,128)(2,1)} %get-tuple-element.33), channel_id=1, source_target_pairs={{0,1},{1,2},{2,3},{4,5},{5,6},{6,7},{8,9},{9,10},{10,11},{12,13},{... | collective-permute-start | bytes 196616 | tf_op jit(solution)/shard_map/ppermute | solution.py:794
  9.5 5.5 %collective-permute-start.1 = (bf16[16,2048]{1,0:T(8,128)(2,1)}, bf16[16,2048]{1,0:T(8,128)(2,1)S(1)}, u32[]{:S(2)}, u32[]{:S(2)}) collective-permute-start(bf16[16,2048]{1,0:T(8,128)(2,1)} %get-tuple-element.34), channel_id=1, source_target_pairs={{1,0},{2,1},{3,2},{5,4},{6,5},{7,6},{9,8},{10,9},{11,10},{13,12},{... | collective-permute-start | bytes 196616 | tf_op jit(solution)/shard_map/ppermute | solution.py:794
  15.1 5.3 %copy-start.1 = (bf16[16,2048]{1,0:T(8,128)(2,1)}, bf16[16,2048]{1,0:T(8,128)(2,1)S(1)}, u32[]{:S(2)}) copy-start(bf16[16,2048]{1,0:T(8,128)(2,1)S(1)} %add.78.side_ref.side_hbm) | copy-start | bytes 196612
  15.7 19.9 %collective-permute-start.2 = (bf16[272,512]{1,0:T(8,128)(2,1)}, bf16[272,512]{1,0:T(8,128)(2,1)S(1)}, u32[]{:S(2)}, u32[]{:S(2)}) collective-permute-start(bf16[272,512]{1,0:T(8,128)(2,1)} %get-tuple-element.56), channel_id=1, source_target_pairs={{0,4},{4,8},{8,12},{12,16},{16,20},{20,24},{24,28},{1,5},{5,9},{9,... | collective-permute-start | bytes 835592 | tf_op jit(solution)/shard_map/ppermute | solution.py:799
  19.1 16.5 %collective-permute-start.3 = (bf16[272,512]{1,0:T(8,128)(2,1)}, bf16[272,512]{1,0:T(8,128)(2,1)S(1)}, u32[]{:S(2)}, u32[]{:S(2)}) collective-permute-start(bf16[272,512]{1,0:T(8,128)(2,1)} %get-tuple-element.55), channel_id=1, source_target_pairs={{4,0},{8,4},{12,8},{16,12},{20,16},{24,20},{28,24},{5,1},{9,5},{13... | collective-permute-start | bytes 835592 | tf_op jit(solution)/shard_map/ppermute | solution.py:800
  35.5 0.7 copy-start.2
  35.6 0.8 copy-start.3
  41.9 63.8 %all-to-all-start = ((bf16[32,272,128]{2,1,0:T(8,128)(2,1)}), bf16[32,272,128]{2,1,0:T(8,128)(2,1)}, u32[]{:S(2)}, u32[]{:S(2)}) async-start(bf16[32,272,128]{2,1,0:T(8,128)(2,1)} %get-tuple-element.48), calls=%async_computation | async-start | bytes 4456448 | tf_op jit(solution)/shard_map/all_to_all | solution.py:814
  63.5 1.4 %collective-permute-start.4 = (f32[296,128]{1,0:T(8,128)S(1)}, f32[296,128]{1,0:T(8,128)S(1)}, u32[]{:S(2)}, u32[]{:S(2)}) collective-permute-start(f32[296,128]{1,0:T(8,128)S(1)} %pad_dynamic-slice_fusion), channel_id=1, source_target_pairs={{0,1},{1,0},{2,3},{3,2},{4,5},{5,4},{6,7},{7,6},{8,9},{9,8},{10,11... | collective-permute-start | bytes 454664 | tf_op jit(solution)/shard_map/ppermute | solution.py:751
  65.9 7.5 %collective-permute-start.5 = (f32[296,128]{1,0:T(8,128)S(1)}, f32[296,128]{1,0:T(8,128)S(1)}, u32[]{:S(2)}, u32[]{:S(2)}) collective-permute-start(f32[296,128]{1,0:T(8,128)S(1)} %fusion), channel_id=1, source_target_pairs={{0,2},{1,3},{2,0},{3,1},{4,6},{5,7},{6,4},{7,5},{8,10},{9,11},{10,... | collective-permute-start | bytes 454664 | tf_op jit(solution)/shard_map/ppermute | solution.py:751
  73.5 11.2 %collective-permute-start.6 = (f32[296,128]{1,0:T(8,128)S(1)}, f32[296,128]{1,0:T(8,128)S(1)}, u32[]{:S(2)}, u32[]{:S(2)}) collective-permute-start(f32[296,128]{1,0:T(8,128)S(1)} %add.95), channel_id=1, source_target_pairs={{0,4},{1,5},{2,6},{3,7},{4,0},{5,1},{6,2},{7,3},{8,12},{9,13},{10,... | collective-permute-start | bytes 454664 | tf_op jit(solution)/shard_map/ppermute | solution.py:751
  84.7 7.7 %collective-permute-start.7 = (f32[296,128]{1,0:T(8,128)S(1)}, f32[296,128]{1,0:T(8,128)S(1)}, u32[]{:S(2)}, u32[]{:S(2)}) collective-permute-start(f32[296,128]{1,0:T(8,128)S(1)} %add.96), channel_id=1, source_target_pairs={{0,8},{1,9},{2,10},{3,11},{4,12},{5,13},{6,14},{7,15},{8,0},{9,1},... | collective-permute-start | bytes 454664 | tf_op jit(solution)/shard_map/ppermute | solution.py:751
  92.5 19.8 %collective-permute-start.8 = (f32[296,128]{1,0:T(8,128)S(1)}, f32[296,128]{1,0:T(8,128)S(1)}, u32[]{:S(2)}, u32[]{:S(2)}) collective-permute-start(f32[296,128]{1,0:T(8,128)S(1)} %add.97), channel_id=1, source_target_pairs={{0,16},{1,17},{2,18},{3,19},{4,20},{5,21},{6,22},{7,23},{8,24},{9,... | collective-permute-start | bytes 454664 | tf_op jit(solution)/shard_map/ppermute | solution.py:751
  112.2 1.5 %copy-start = (f32[296,128]{1,0:T(8,128)}, f32[296,128]{1,0:T(8,128)S(1)}, u32[]{:S(2)}) copy-start(f32[296,128]{1,0:T(8,128)S(1)} %add.98.total_ref) | copy-start | bytes 454660
  112.2 1.4 %collective-permute-start.9 = (f32[296,128]{1,0:T(8,128)S(1)}, f32[296,128]{1,0:T(8,128)S(1)}, u32[]{:S(2)}, u32[]{:S(2)}) collective-permute-start(f32[296,128]{1,0:T(8,128)S(1)} %add.98.total_ref), channel_id=1, source_target_pairs={{0,1},{1,0},{2,3},{3,2},{4,5},{5,4},{6,7},{7,6},{8,9},{9,8},{10,11... | collective-permute-start | bytes 454664 | tf_op jit(solution)/shard_map/ppermute | solution.py:751
  113.7 0.7 copy-start.4

commit v5 on v4

--- a/solution.py
+++ b/solution.py
@@ -649,37 +649,60 @@
     )(act_in, act_mid, g_mid, xc)
 
 
-def unpack_kernel(channels, arrived_ref, label_ref, out_ref, chosen, flat):
-    devices = arrived_ref.shape[0]
-    block_rows, part, breadth = out_ref.shape[1], out_ref.shape[3], out_ref.shape[4]
+def unpack_kernel(
+    channels, breadth, arrived_ref, out_ref, arrived, label_rows, chosen, flat, frame, sem_in, sem_out
+):
+    devices = arrived.shape[0]
+    halves, block_rows, part = out_ref.shape[2], out_ref.shape[1], out_ref.shape[3]
     rows_to = CAP * BLOCK
-
-    @pl.when(pl.program_id(0) == 0)
-    def _():
-        shape = (BLOCK, block_rows * breadth)
-        place = lax.broadcasted_iota(jnp.int32, shape, 1) - lax.broadcasted_iota(jnp.int32, shape, 0)
-        place = place.astype(F32)
-
-        def select(source, _):
-            label = label_ref[source].astype(F32) * BLOCK
-            for rank in range(CAP):
-                at = rank * (128 // CAP)
-                hit = (place == label[:, at : at + 1]).astype(F32).astype(BF16)
-                row = pl.multiple_of(source * rows_to + rank * BLOCK, BLOCK)
-                chosen[pl.ds(row, BLOCK), :] = hit
-            return 0
-
-        lax.fori_loop(0, devices, select, 0, unroll=4)
-
-    for at in range(arrived_ref.shape[1] // rows_to):
-        tile = arrived_ref[:, at * rows_to : (at + 1) * rows_to, :]
-        flat[at * 128 : (at + 1) * 128, :] = tile.reshape(devices * rows_to, 128).T
-    for band in range(block_rows):
-        summed = jnp.dot(
-            flat[...], chosen[:, band * breadth : (band + 1) * breadth], preferred_element_type=F32
+    depth = DEPTH * rows_to
+    strip = depth // halves
+    labels = pltpu.make_async_copy(arrived_ref.at[:, depth : depth + 16, :], label_rows, sem_in.at[0])
+    labels.start()
+    loads = [
+        pltpu.make_async_copy(
+            arrived_ref.at[:, at * strip : (at + 1) * strip, :],
+            arrived.at[:, at * strip : (at + 1) * strip, :],
+            sem_in.at[1 + at],
         )
-        cube = summed.reshape(part, channels, breadth)
-        out_ref[:, band, 0, :, :] = jnp.swapaxes(cube, 0, 1)
+        for at in range(halves)
+    ]
+    for load in loads:
+        load.start()
+    shape = (BLOCK, block_rows * breadth)
+    place = lax.broadcasted_iota(jnp.int32, shape, 1) - lax.broadcasted_iota(jnp.int32, shape, 0)
+    place = place.astype(F32)
+    labels.wait()
+
+    def select(source, _):
+        label = label_rows[source].astype(F32) * BLOCK
+        for rank in range(CAP):
+            at = rank * (128 // CAP)
+            hit = (place == label[:, at : at + 1]).astype(F32).astype(BF16)
+            row = pl.multiple_of(source * rows_to + rank * BLOCK, BLOCK)
+            chosen[pl.ds(row, BLOCK), :] = hit
+        return 0
+
+    lax.fori_loop(0, devices, select, 0, unroll=4)
+    stores = []
+    for half in range(halves):
+        loads[half].wait()
+        for at in range(strip // rows_to):
+            row = half * strip + at * rows_to
+            tile = arrived[:, row : row + rows_to, :]
+            flat[at * 128 : (at + 1) * 128, :] = tile.reshape(devices * rows_to, 128).T
+        for band in range(block_rows):
+            summed = jnp.dot(
+                flat[...], chosen[:, band * breadth : (band + 1) * breadth], preferred_element_type=F32
+            )
+            slot = half * block_rows + band
+            frame[slot] = jnp.swapaxes(summed.reshape(part, channels, breadth), 0, 1)
+            stores.append(
+                pltpu.make_async_copy(frame.at[slot], out_ref.at[:, band, half], sem_out.at[slot])
+            )
+            stores[-1].start()
+    for store in stores:
+        store.wait()
 
 
 def unpack(sizes, arrived):
@@ -688,23 +711,25 @@
     devices = arrived.shape[0]
     rows_to = CAP * BLOCK
     part = 8
-    tiles = DEPTH * part // BLOCK
+    halves = BLOCK // part
+    hbm = pl.BlockSpec(memory_space=pl.ANY)
     return pl.pallas_call(
-        functools.partial(unpack_kernel, channels),
-        grid=(BLOCK // part,),
-        in_specs=[
-            pl.BlockSpec((devices, tiles * rows_to, 128), lambda h: (0, h, 0)),
-            pl.BlockSpec((devices, 16, 128), lambda h: (0, DEPTH * rows_to // 16, 0)),
-        ],
-        out_specs=pl.BlockSpec((channels, block_rows, 1, part, breadth), lambda h: (0, 0, h, 0, 0)),
-        out_shape=jax.ShapeDtypeStruct((channels, block_rows, BLOCK // part, part, breadth), F32),
+        functools.partial(unpack_kernel, channels, breadth),
+        in_specs=[hbm],
+        out_specs=hbm,
+        out_shape=jax.ShapeDtypeStruct((channels, block_rows, halves, part, breadth), F32),
         scratch_shapes=[
+            pltpu.VMEM((devices, DEPTH * rows_to, 128), BF16),
+            pltpu.VMEM((devices, 16, 128), BF16),
             pltpu.VMEM((devices * rows_to, block_rows * breadth), BF16),
             pltpu.VMEM((part * channels, devices * rows_to), BF16),
+            pltpu.VMEM((halves * block_rows, channels, part, breadth), F32),
+            pltpu.SemaphoreType.DMA((1 + halves,)),
+            pltpu.SemaphoreType.DMA((halves * block_rows,)),
         ],
         compiler_params=params(),
         name="unpack",
-    )(arrived, arrived)
+    )(arrived)
 
 
 def shift_pairs(axis, step):
@@ -746,7 +771,7 @@
     return jnp.transpose(w1, order), b1[0], jnp.transpose(w2, order), b2[0]
 
 
-def total_over_devices(terms, devices, frame_of):
+def total_over_devices(terms, devices, arrived, frame_of):
     me = lax.axis_index(AXES)
     swap = lambda value, step: lax.ppermute(value, AXES, [(i, i ^ step) for i in range(devices)])
     bit = me % 2
@@ -758,8 +783,9 @@
     while 2 * step < devices:
         total = total + swap(total, step)
         step *= 2
+    total, arrived = lax.optimization_barrier((total, arrived))
     other = swap(total, step)
-    frame = frame_of()
+    frame = frame_of(arrived)
     other, frame = lax.optimization_barrier((other, frame))
     total = total + other
     return total, swap(total, 1), frame
@@ -818,7 +844,8 @@
     total, other, frame = total_over_devices(
         jnp.concatenate([terms, fill], axis=0),
         devices,
-        lambda: unpack(sizes, arrived),
+        arrived,
+        functools.partial(unpack, sizes),
     )
     return (frame.reshape(sizes), *finish(channels, factor, total, other))
 

time: 117 us -> 116 us (level)
  starting transfers between devices: 26.5 us -> 24 us
  waiting for transfers between devices: 35.2 us -> 37.7 us
    ppermute x6, waiting for transfers between devices: 22.2 us -> 25.9 us  [total_over_devices(): lax.ppermute(value, AXES, [(i, i ^ step) for i in range(devices)])]
    ppermute x6, starting transfers between devices: 9.63 us -> 7.13 us  [total_over_devices(): lax.ppermute(value, AXES, [(i, i ^ step) for i in range(devices)])]
    all_to_all x1, waiting for transfers between devices: 10.7 us -> 9.53 us  [body(): lax.all_to_all(packed, AXES, split_axis=0, concat_axis=0, tiled=True)]
  transfers between devices with their start and end apart: 11 -> 11, of which waited for: 7 -> 8; matrix products, arithmetic and copies ran while one was open for 3% -> 3% of each run, Pallas kernels for 29% -> 29%
where the time goes in v5:
time: 116 us
  Pallas kernels  47.2 us (41%)
  waiting for transfers between devices  37.7 us (33%)
  starting transfers between devices  24 us (21%)
  local copies, waits for them, and re-layouts  3.5 us (3%)
  other arithmetic  2.43 us (2%)
    ppermute x6, waiting for transfers between devices, total_over_devices(): lax.ppermute(value, AXES, [(i, i ^ step) for i in range(devices)])  25.9 us
    pallas_call x1, Pallas kernels, inner(): pl.pallas_call(functools.partial(inner_kernel, channels, height, breadth)...  15.1 us
    pallas_call x1, Pallas kernels, correlate(): pl.pallas_call(functools.partial(correlate_kernel, channels, height, brea...  12.2 us
    all_to_all x1, waiting for transfers between devices, body(): lax.all_to_all(packed, AXES, split_axis=0, concat_axis=0, tiled=True)  9.53 us
    all_to_all x1, starting transfers between devices, body(): lax.all_to_all(packed, AXES, split_axis=0, concat_axis=0, tiled=True)  8.48 us
    ppermute x6, starting transfers between devices, total_over_devices(): lax.ppermute(value, AXES, [(i, i ^ step) for i in range(devices)])  7.13 us
    pallas_call x1, Pallas kernels, reorder(): pl.pallas_call(reorder_kernel, grid=(breadth // lanes, height // step), i...  6.51 us
    pallas_call x1, Pallas kernels, unpack(): pl.pallas_call(functools.partial(unpack_kernel, channels, breadth), in_sp...  5.85 us
  transfers between devices with their start and end apart: 11, of which 8 were waited for; matrix products, arithmetic and copies ran while one was open for 3% of the time, Pallas kernels for 29%

profile of v5, /device:TPU:0, one launch (start us, length us, event | category | flops | bytes accessed | tf_op | source)
XLA Modules:
  0.0 115.7 jit_solution(15149249304640145691)
XLA Ops:
  0.7 6.5 %reorder.1 = (bf16[2048,512]{1,0:T(8,128)(2,1)}, bf16[2048,512]{1,0:T(8,128)(2,1)}, bf16[16,2048]{1,0:T(8,128)(2,1)}, bf16[16,2048]{1,0:T(8,128)(2,1)}, bf16[272...) custom-call(bf16[64,32,512]{2,1,0:T(8,128)(2,1)} %w_ref.1, ...), custom_call_target="tpu_custom_call" | custom-call | tf_op jit(solution)/shard_map/reorder/pallas_call | solution.py:135
  7.2 2.4 %collective-permute-start = (bf16[16,2048]{1,0:T(8,128)(2,1)}, bf16[16,2048]{1,0:T(8,128)(2,1)S(1)}, u32[]{:S(2)}, u32[]{:S(2)}) collective-permute-start(bf16[16,2048]{1,0:T(8,128)(2,1)} %get-tuple-element.35), channel_id=1, source_target_pairs={{0,1},{1,2},{2,3},{4,5},{5,6},{6,7},{8,9},{9,10},{10,11},{12,13},{... | collective-permute-start | bytes 196616 | tf_op jit(solution)/shard_map/ppermute | solution.py:820
  9.5 1.3 %collective-permute-start.1 = (bf16[16,2048]{1,0:T(8,128)(2,1)}, bf16[16,2048]{1,0:T(8,128)(2,1)S(1)}, u32[]{:S(2)}, u32[]{:S(2)}) collective-permute-start(bf16[16,2048]{1,0:T(8,128)(2,1)} %get-tuple-element.36), channel_id=1, source_target_pairs={{1,0},{2,1},{3,2},{5,4},{6,5},{7,6},{9,8},{10,9},{11,10},{13,12},{... | collective-permute-start | bytes 196616 | tf_op jit(solution)/shard_map/ppermute | solution.py:820
  10.8 0.0 copy-done.5
  10.9 0.1 eq.13
  10.9 0.2 convert_reduce_fusion
  11.1 0.1 reduce_sum.21
  11.2 0.1 add.80
  11.3 0.1 add.81
  11.4 0.1 add.83
  11.5 0.0 copy-done.6
  11.5 0.1 add.89
  11.6 0.6 broadcast_add_fusion.target_ref.target_hbm
  12.2 0.1 select_reduce_fusion
  12.3 0.5 broadcast_add_fusion.2.label_ref
  12.8 0.0 collective-permute-done
  12.8 2.2 %collective-permute-done.1 = bf16[16,2048]{1,0:T(8,128)(2,1)S(1)} collective-permute-done((bf16[16,2048]{1,0:T(8,128)(2,1)}, bf16[16,2048]{1,0:T(8,128)(2,1)S(1)}, u32[]{:S(2)}, u32[]{:S(2)}) %collective-permute-start.1) | collective-permute-done | bytes 65568 | tf_op jit(solution)/shard_map/ppermute | solution.py:820
  15.1 0.6 slice_dynamic-update-slice_fusion
  15.7 3.4 %collective-permute-start.2 = (bf16[272,512]{1,0:T(8,128)(2,1)}, bf16[272,512]{1,0:T(8,128)(2,1)S(1)}, u32[]{:S(2)}, u32[]{:S(2)}) collective-permute-start(bf16[272,512]{1,0:T(8,128)(2,1)} %get-tuple-element.60), channel_id=1, source_target_pairs={{0,4},{4,8},{8,12},{12,16},{16,20},{20,24},{24,28},{1,5},{5,9},{9,... | collective-permute-start | bytes 835592 | tf_op jit(solution)/shard_map/ppermute | solution.py:825
  19.1 1.3 %collective-permute-start.3 = (bf16[272,512]{1,0:T(8,128)(2,1)}, bf16[272,512]{1,0:T(8,128)(2,1)S(1)}, u32[]{:S(2)}, u32[]{:S(2)}) collective-permute-start(bf16[272,512]{1,0:T(8,128)(2,1)} %get-tuple-element.59), channel_id=1, source_target_pairs={{4,0},{8,4},{12,8},{16,12},{20,16},{24,20},{28,24},{5,1},{9,5},{13... | collective-permute-start | bytes 835592 | tf_op jit(solution)/shard_map/ppermute | solution.py:826
  20.4 15.1 %inner.1 = (bf16[32,272,128]{2,1,0:T(8,128)(2,1)}, bf16[2176,640]{1,0:T(8,128)(2,1)}, bf16[2176,640]{1,0:T(8,128)(2,1)}, bf16[2048,640]{1,0:T(8,128)(2,1)}, bf16[256,512]{1,0:T(8,128)(2,1)}) custom-call(bf16[2048,512]{1,0:T(8,128)(2,1)} %get-tuple-element.32.xw_ref, bf16[2048,512]{1,0:T(8,128)(2,1)} %get-tuple-element.33.xc_ref, bf16[16,2048]{1,0:T(8,128)(2,1)} %copy-done.1, ...), custom_call_target="tpu_custom_call" | custom-call | flops 6039797760 | bytes 20000000 | tf_op jit(solution)/shard_map/inner/pallas_call | solution.py:339
  35.5 0.0 collective-permute-done.2.up_ref
  35.5 0.0 copy-start.2
  35.5 0.0 collective-permute-done.3.down_ref
  35.6 0.0 copy-start.3
  35.6 0.7 copy-done.2
  36.2 0.1 copy-done.3
  36.3 5.6 %outer.1 = (bf16[32,272,128]{2,1,0:T(8,128)(2,1)}, bf16[2176,640]{1,0:T(8,128)(2,1)}, bf16[2176,640]{1,0:T(8,128)(2,1)}, bf16[2048,640]{1,0:T(8,128)(2,1)}) custom-call(bf16[2048,512]{1,0:T(8,128)(2,1)} %get-tuple-element.32.xw_ref, ...), custom_call_target="tpu_custom_call", output_to_operand_aliasing={{0}: (11, {}), {1}: (12, {}), {2}: (13, {}), {3}: (14, {})} | custom-call | tf_op jit(solution)/shard_map/outer/pallas_call | solution.py:527
  41.9 8.5 %all-to-all-start = ((bf16[32,272,128]{2,1,0:T(8,128)(2,1)}), bf16[32,272,128]{2,1,0:T(8,128)(2,1)}, u32[]{:S(2)}, u32[]{:S(2)}) async-start(bf16[32,272,128]{2,1,0:T(8,128)(2,1)} %get-tuple-element.50), calls=%async_computation | async-start | bytes 4456448 | tf_op jit(solution)/shard_map/all_to_all | solution.py:840
  50.4 12.2 %correlate.1 = f32[584,128]{1,0:T(8,128)} custom-call(bf16[2176,640]{1,0:T(8,128)(2,1)} %get-tuple-element.47.act_in_ref, bf16[2176,640]{1,0:T(8,128)(2,1)} %get-tuple-element.48.act_mid_ref, bf16[2048,640]{1,0:T(8,128)(2,1)} %get-tuple-element.49.g_ref, bf16[2048,512]{1,0:T(8,128)(2,1)} %get-tuple-element.33.xc_ref), custom_call_target="tpu_custom_call" | custom-call | flops 3221225472 | bytes 10000000 | tf_op jit(solution)/shard_map/correlate/pallas_call | solution.py:628
  62.6 0.9 pad_dynamic-slice_fusion
  63.5 0.3 collective-permute-start.4
  63.8 1.2 %collective-permute-done.4 = f32[296,128]{1,0:T(8,128)S(1)} collective-permute-done((f32[296,128]{1,0:T(8,128)S(1)}, f32[296,128]{1,0:T(8,128)S(1)}, u32[]{:S(2)}, u32[]{:S(2)}) %collective-permute-start.4) | collective-permute-done | bytes 151584 | tf_op jit(solution)/shard_map/ppermute | solution.py:776
  65.0 0.9 fusion
  65.9 1.8 %collective-permute-start.5 = (f32[296,128]{1,0:T(8,128)S(1)}, f32[296,128]{1,0:T(8,128)S(1)}, u32[]{:S(2)}, u32[]{:S(2)}) collective-permute-start(f32[296,128]{1,0:T(8,128)S(1)} %fusion), channel_id=1, source_target_pairs={{0,2},{1,3},{2,0},{3,1},{4,6},{5,7},{6,4},{7,5},{8,10},{9,11},{10,... | collective-permute-start | bytes 454664 | tf_op jit(solution)/shard_map/ppermute | solution.py:776
  67.7 5.7 %collective-permute-done.5 = f32[296,128]{1,0:T(8,128)S(1)} collective-permute-done((f32[296,128]{1,0:T(8,128)S(1)}, f32[296,128]{1,0:T(8,128)S(1)}, u32[]{:S(2)}, u32[]{:S(2)}) %collective-permute-start.5) | collective-permute-done | bytes 151584 | tf_op jit(solution)/shard_map/ppermute | solution.py:776
  73.5 5.0 %collective-permute-start.6 = (f32[296,128]{1,0:T(8,128)S(1)}, f32[296,128]{1,0:T(8,128)S(1)}, u32[]{:S(2)}, u32[]{:S(2)}) collective-permute-start(f32[296,128]{1,0:T(8,128)S(1)} %add.95), channel_id=1, source_target_pairs={{0,4},{1,5},{2,6},{3,7},{4,0},{5,1},{6,2},{7,3},{8,12},{9,13},{10,... | collective-permute-start | bytes 454664 | tf_op jit(solution)/shard_map/ppermute | solution.py:776
  78.4 6.3 %collective-permute-done.6 = f32[296,128]{1,0:T(8,128)S(1)} collective-permute-done((f32[296,128]{1,0:T(8,128)S(1)}, f32[296,128]{1,0:T(8,128)S(1)}, u32[]{:S(2)}, u32[]{:S(2)}) %collective-permute-start.6) | collective-permute-done | bytes 151584 | tf_op jit(solution)/shard_map/ppermute | solution.py:776
  84.7 0.1 collective-permute-start.7
  84.8 7.7 %collective-permute-done.7 = f32[296,128]{1,0:T(8,128)S(1)} collective-permute-done((f32[296,128]{1,0:T(8,128)S(1)}, f32[296,128]{1,0:T(8,128)S(1)}, u32[]{:S(2)}, u32[]{:S(2)}) %collective-permute-start.7) | collective-permute-done | bytes 151584 | tf_op jit(solution)/shard_map/ppermute | solution.py:776
  92.5 9.5 %all-to-all-done.arrived_ref = bf16[32,272,128]{2,1,0:T(8,128)(2,1)} async-done(((bf16[32,272,128]{2,1,0:T(8,128)(2,1)}), bf16[32,272,128]{2,1,0:T(8,128)(2,1)}, u32[]{:S(2)}, u32[]{:S(2)}) %all-to-all-start) | async-done | bytes 2228256 | tf_op jit(solution)/shard_map/all_to_all | solution.py:840
  102.0 0.0 collective-permute-start.8
  102.0 5.8 %unpack.1 = f32[64,2,2,8,512]{4,3,2,1,0:T(8,128)} custom-call(bf16[32,272,128]{2,1,0:T(8,128)(2,1)} %all-to-all-done.arrived_ref), custom_call_target="tpu_custom_call" | custom-call | tf_op jit(solution)/shard_map/unpack/pallas_call | solution.py:716
  107.8 3.7 %collective-permute-done.8 = f32[296,128]{1,0:T(8,128)S(1)} collective-permute-done((f32[296,128]{1,0:T(8,128)S(1)}, f32[296,128]{1,0:T(8,128)S(1)}, u32[]{:S(2)}, u32[]{:S(2)}) %collective-permute-start.8) | collective-permute-done | bytes 151584 | tf_op jit(solution)/shard_map/ppermute | solution.py:776
  111.6 0.1 collective-permute-start.9
  111.7 1.4 %collective-permute-done.9.other_ref = f32[296,128]{1,0:T(8,128)S(1)} collective-permute-done((f32[296,128]{1,0:T(8,128)S(1)}, f32[296,128]{1,0:T(8,128)S(1)}, u32[]{:S(2)}, u32[]{:S(2)}) %collective-permute-start.9) | collective-permute-done | bytes 151584 | tf_op jit(solution)/shard_map/ppermute | solution.py:776
  113.1 0.7 copy-done.4
  113.7 1.9 %finish.1 = (f32[3,3,64,64]{3,2,1,0:T(8,128)}, f32[3,3,64,64]{3,2,1,0:T(8,128)}, f32[1,64]{1,0:T(1,128)}, f32[1,64]{1,0:T(1,128)}) custom-call(f32[296,128]{1,0:T(8,128)} %copy-done, f32[296,128]{1,0:T(8,128)} %copy-done.4), custom_call_target="tpu_custom_call" | custom-call | tf_op jit(solution)/shard_map/finish/pallas_call | solution.py:761
  (16 shorter events, 0.1 us)
Async XLA Ops:
  0.6 10.2 %copy-start.5 = (s32[2,32]{1,0:T(2,128)S(1)}, s32[2,32]{1,0:T(2,128)}, u32[]{:S(2)}) copy-start(s32[2,32]{1,0:T(2,128)} %param.12) | copy-start | bytes 772
  0.6 10.8 %copy-start.6 = (s32[2,32]{1,0:T(2,128)S(1)}, s32[2,32]{1,0:T(2,128)}, u32[]{:S(2)}) copy-start(s32[2,32]{1,0:T(2,128)} %param.13) | copy-start | bytes 772
  7.2 5.6 %collective-permute-start = (bf16[16,2048]{1,0:T(8,128)(2,1)}, bf16[16,2048]{1,0:T(8,128)(2,1)S(1)}, u32[]{:S(2)}, u32[]{:S(2)}) collective-permute-start(bf16[16,2048]{1,0:T(8,128)(2,1)} %get-tuple-element.35), channel_id=1, source_target_pairs={{0,1},{1,2},{2,3},{4,5},{5,6},{6,7},{8,9},{9,10},{10,11},{12,13},{... | collective-permute-start | bytes 196616 | tf_op jit(solution)/shard_map/ppermute | solution.py:820
  9.5 5.5 %collective-permute-start.1 = (bf16[16,2048]{1,0:T(8,128)(2,1)}, bf16[16,2048]{1,0:T(8,128)(2,1)S(1)}, u32[]{:S(2)}, u32[]{:S(2)}) collective-permute-start(bf16[16,2048]{1,0:T(8,128)(2,1)} %get-tuple-element.36), channel_id=1, source_target_pairs={{1,0},{2,1},{3,2},{5,4},{6,5},{7,6},{9,8},{10,9},{11,10},{13,12},{... | collective-permute-start | bytes 196616 | tf_op jit(solution)/shard_map/ppermute | solution.py:820
  15.1 5.3 %copy-start.1 = (bf16[16,2048]{1,0:T(8,128)(2,1)}, bf16[16,2048]{1,0:T(8,128)(2,1)S(1)}, u32[]{:S(2)}) copy-start(bf16[16,2048]{1,0:T(8,128)(2,1)S(1)} %add.78.side_ref.side_hbm) | copy-start | bytes 196612
  15.7 19.9 %collective-permute-start.2 = (bf16[272,512]{1,0:T(8,128)(2,1)}, bf16[272,512]{1,0:T(8,128)(2,1)S(1)}, u32[]{:S(2)}, u32[]{:S(2)}) collective-permute-start(bf16[272,512]{1,0:T(8,128)(2,1)} %get-tuple-element.60), channel_id=1, source_target_pairs={{0,4},{4,8},{8,12},{12,16},{16,20},{20,24},{24,28},{1,5},{5,9},{9,... | collective-permute-start | bytes 835592 | tf_op jit(solution)/shard_map/ppermute | solution.py:825
  19.1 16.5 %collective-permute-start.3 = (bf16[272,512]{1,0:T(8,128)(2,1)}, bf16[272,512]{1,0:T(8,128)(2,1)S(1)}, u32[]{:S(2)}, u32[]{:S(2)}) collective-permute-start(bf16[272,512]{1,0:T(8,128)(2,1)} %get-tuple-element.59), channel_id=1, source_target_pairs={{4,0},{8,4},{12,8},{16,12},{20,16},{24,20},{28,24},{5,1},{9,5},{13... | collective-permute-start | bytes 835592 | tf_op jit(solution)/shard_map/ppermute | solution.py:826
  35.5 0.7 copy-start.2
  35.6 0.8 copy-start.3
  41.9 60.1 %all-to-all-start = ((bf16[32,272,128]{2,1,0:T(8,128)(2,1)}), bf16[32,272,128]{2,1,0:T(8,128)(2,1)}, u32[]{:S(2)}, u32[]{:S(2)}) async-start(bf16[32,272,128]{2,1,0:T(8,128)(2,1)} %get-tuple-element.50), calls=%async_computation | async-start | bytes 4456448 | tf_op jit(solution)/shard_map/all_to_all | solution.py:840
  63.5 1.4 %collective-permute-start.4 = (f32[296,128]{1,0:T(8,128)S(1)}, f32[296,128]{1,0:T(8,128)S(1)}, u32[]{:S(2)}, u32[]{:S(2)}) collective-permute-start(f32[296,128]{1,0:T(8,128)S(1)} %pad_dynamic-slice_fusion), channel_id=1, source_target_pairs={{0,1},{1,0},{2,3},{3,2},{4,5},{5,4},{6,7},{7,6},{8,9},{9,8},{10,11... | collective-permute-start | bytes 454664 | tf_op jit(solution)/shard_map/ppermute | solution.py:776
  65.9 7.5 %collective-permute-start.5 = (f32[296,128]{1,0:T(8,128)S(1)}, f32[296,128]{1,0:T(8,128)S(1)}, u32[]{:S(2)}, u32[]{:S(2)}) collective-permute-start(f32[296,128]{1,0:T(8,128)S(1)} %fusion), channel_id=1, source_target_pairs={{0,2},{1,3},{2,0},{3,1},{4,6},{5,7},{6,4},{7,5},{8,10},{9,11},{10,... | collective-permute-start | bytes 454664 | tf_op jit(solution)/shard_map/ppermute | solution.py:776
  73.5 11.2 %collective-permute-start.6 = (f32[296,128]{1,0:T(8,128)S(1)}, f32[296,128]{1,0:T(8,128)S(1)}, u32[]{:S(2)}, u32[]{:S(2)}) collective-permute-start(f32[296,128]{1,0:T(8,128)S(1)} %add.95), channel_id=1, source_target_pairs={{0,4},{1,5},{2,6},{3,7},{4,0},{5,1},{6,2},{7,3},{8,12},{9,13},{10,... | collective-permute-start | bytes 454664 | tf_op jit(solution)/shard_map/ppermute | solution.py:776
  84.7 7.7 %collective-permute-start.7 = (f32[296,128]{1,0:T(8,128)S(1)}, f32[296,128]{1,0:T(8,128)S(1)}, u32[]{:S(2)}, u32[]{:S(2)}) collective-permute-start(f32[296,128]{1,0:T(8,128)S(1)} %add.96), channel_id=1, source_target_pairs={{0,8},{1,9},{2,10},{3,11},{4,12},{5,13},{6,14},{7,15},{8,0},{9,1},... | collective-permute-start | bytes 454664 | tf_op jit(solution)/shard_map/ppermute | solution.py:776
  102.0 9.6 %collective-permute-start.8 = (f32[296,128]{1,0:T(8,128)S(1)}, f32[296,128]{1,0:T(8,128)S(1)}, u32[]{:S(2)}, u32[]{:S(2)}) collective-permute-start(f32[296,128]{1,0:T(8,128)S(1)} %add.97), channel_id=1, source_target_pairs={{0,16},{1,17},{2,18},{3,19},{4,20},{5,21},{6,22},{7,23},{8,24},{9,... | collective-permute-start | bytes 454664 | tf_op jit(solution)/shard_map/ppermute | solution.py:776
  111.6 1.5 %copy-start = (f32[296,128]{1,0:T(8,128)}, f32[296,128]{1,0:T(8,128)S(1)}, u32[]{:S(2)}) copy-start(f32[296,128]{1,0:T(8,128)S(1)} %add.98.total_ref) | copy-start | bytes 454660
  111.6 1.4 %collective-permute-start.9 = (f32[296,128]{1,0:T(8,128)S(1)}, f32[296,128]{1,0:T(8,128)S(1)}, u32[]{:S(2)}, u32[]{:S(2)}) collective-permute-start(f32[296,128]{1,0:T(8,128)S(1)} %add.98.total_ref), channel_id=1, source_target_pairs={{0,1},{1,0},{2,3},{3,2},{4,5},{5,4},{6,7},{7,6},{8,9},{9,8},{10,11... | collective-permute-start | bytes 454664 | tf_op jit(solution)/shard_map/ppermute | solution.py:776
  113.1 0.7 copy-start.4

commit v6 on v5

--- a/solution.py
+++ b/solution.py
@@ -479,17 +479,12 @@
         (act_mid.at[rows2 : 2 * rows2, :], act_mid_ref.at[body : body + 2 * ch, :]),
         (grads.at[0:ch, :], g_ref.at[0:ch, :]),
         (grads.at[ch : 2 * ch, :], g_ref.at[body - ch : body, :]),
-        (packed.at[:, :, 0:rows2], packed_ref.at[:, 0:rows_to, :]),
-        (
-            packed.at[:, :, rows2 : 2 * rows2],
-            packed_ref.at[:, (DEPTH - 1) * rows_to : DEPTH * rows_to, :],
-        ),
     ]
     stores = [
         pltpu.make_async_copy(source, target, sem_out.at[at])
         for at, (source, target) in enumerate(stores)
     ]
-    for store in stores[:6]:
+    for store in stores:
         store.start()
     both = (
         jnp.concatenate([gw[0:rows2, :], gw_mid_ref[0:rows2, :]], axis=0),
@@ -497,7 +492,7 @@
     )
 
     def pack(part, _):
-        rows = pl.ds(pl.multiple_of(part * size, size), size)
+        rows = slice(part * size, (part + 1) * size)
         total = sum(
             lax.dot_general(
                 chosen[rows, band * breadth : (band + 1) * breadth],
@@ -512,9 +507,19 @@
         )
         return 0
 
-    lax.fori_loop(0, chosen.shape[0] // size, pack, 0, unroll=4)
-    for store in stores[6:]:
-        store.start()
+    group = size // rows_to
+    for part in range(packed.shape[0] // group):
+        pack(part, 0)
+        devices = slice(part * group, (part + 1) * group)
+        for at, tile in enumerate((0, DEPTH - 1)):
+            stores.append(
+                pltpu.make_async_copy(
+                    packed.at[devices, :, at * rows2 : (at + 1) * rows2],
+                    packed_ref.at[devices, tile * rows_to : (tile + 1) * rows_to, :],
+                    sem_out.at[len(stores)],
+                )
+            )
+            stores[-1].start()
     for store in stores:
         store.wait()
 
@@ -546,7 +551,7 @@
             pltpu.VMEM((2, 16, 2 * channels), BF16),
             *[pltpu.VMEM(item.shape, item.dtype) for item in operands[4:]],
             pltpu.SemaphoreType.DMA((19,)),
-            pltpu.SemaphoreType.DMA((8,)),
+            pltpu.SemaphoreType.DMA((6 + 2 * slots * BLOCK // 256,)),
         ],
         compiler_params=params(),
         name="outer",
@@ -783,7 +788,6 @@
     while 2 * step < devices:
         total = total + swap(total, step)
         step *= 2
-    total, arrived = lax.optimization_barrier((total, arrived))
     other = swap(total, step)
     frame = frame_of(arrived)
     other, frame = lax.optimization_barrier((other, frame))

time: 116 us -> 116 us (level)
  starting transfers between devices: 24 us -> 26.5 us
  waiting for transfers between devices: 37.7 us -> 35.2 us
    ppermute x6, waiting for transfers between devices: 25.9 us -> 22.2 us  [total_over_devices(): lax.ppermute(value, AXES, [(i, i ^ step) for i in range(devices)])]
    ppermute x6, starting transfers between devices: 7.13 us -> 9.63 us  [total_over_devices(): lax.ppermute(value, AXES, [(i, i ^ step) for i in range(devices)])]
    all_to_all x1, waiting for transfers between devices: 9.53 us -> 10.7 us  [body(): lax.all_to_all(packed, AXES, split_axis=0, concat_axis=0, tiled=True)]
  transfers between devices with their start and end apart: 11 -> 11, of which waited for: 8 -> 7; matrix products, arithmetic and copies ran while one was open for 3% -> 3% of each run, Pallas kernels for 29% -> 29%
where the time goes in v6:
time: 116 us
  Pallas kernels  47.1 us (41%)
  waiting for transfers between devices  35.2 us (30%)
  starting transfers between devices  26.5 us (23%)
  local copies, waits for them, and re-layouts  3.5 us (3%)
  other arithmetic  2.44 us (2%)
    ppermute x6, waiting for transfers between devices, total_over_devices(): lax.ppermute(value, AXES, [(i, i ^ step) for i in range(devices)])  22.2 us
    pallas_call x1, Pallas kernels, inner(): pl.pallas_call(functools.partial(inner_kernel, channels, height, breadth)...  15.1 us
    pallas_call x1, Pallas kernels, correlate(): pl.pallas_call(functools.partial(correlate_kernel, channels, height, brea...  12.2 us
    all_to_all x1, waiting for transfers between devices, body(): lax.all_to_all(packed, AXES, split_axis=0, concat_axis=0, tiled=True)  10.7 us
    ppermute x6, starting transfers between devices, total_over_devices(): lax.ppermute(value, AXES, [(i, i ^ step) for i in range(devices)])  9.63 us
    all_to_all x1, starting transfers between devices, body(): lax.all_to_all(packed, AXES, split_axis=0, concat_axis=0, tiled=True)  8.48 us
    pallas_call x1, Pallas kernels, reorder(): pl.pallas_call(reorder_kernel, grid=(breadth // lanes, height // step), i...  6.51 us
    pallas_call x1, Pallas kernels, unpack(): pl.pallas_call(functools.partial(unpack_kernel, channels, breadth), in_sp...  5.85 us
  transfers between devices with their start and end apart: 11, of which 7 were waited for; matrix products, arithmetic and copies ran while one was open for 3% of the time, Pallas kernels for 29%

profile of v6, /device:TPU:0, one launch (start us, length us, event | category | flops | bytes accessed | tf_op | source)
XLA Modules:
  0.0 115.6 jit_solution(3030968917412924891)
XLA Ops:
  0.6 0.0 copy-start.5
  0.6 0.0 copy-start.6
  0.7 6.5 %reorder.1 = (bf16[2048,512]{1,0:T(8,128)(2,1)}, bf16[2048,512]{1,0:T(8,128)(2,1)}, bf16[16,2048]{1,0:T(8,128)(2,1)}, bf16[16,2048]{1,0:T(8,128)(2,1)}, bf16[272...) custom-call(bf16[64,32,512]{2,1,0:T(8,128)(2,1)} %w_ref.1, ...), custom_call_target="tpu_custom_call" | custom-call | tf_op jit(solution)/shard_map/reorder/pallas_call | solution.py:135
  7.2 2.4 %collective-permute-start = (bf16[16,2048]{1,0:T(8,128)(2,1)}, bf16[16,2048]{1,0:T(8,128)(2,1)S(1)}, u32[]{:S(2)}, u32[]{:S(2)}) collective-permute-start(bf16[16,2048]{1,0:T(8,128)(2,1)} %get-tuple-element.33), channel_id=1, source_target_pairs={{0,1},{1,2},{2,3},{4,5},{5,6},{6,7},{8,9},{9,10},{10,11},{12,13},{... | collective-permute-start | bytes 196616 | tf_op jit(solution)/shard_map/ppermute | solution.py:824
  9.5 1.3 %collective-permute-start.1 = (bf16[16,2048]{1,0:T(8,128)(2,1)}, bf16[16,2048]{1,0:T(8,128)(2,1)S(1)}, u32[]{:S(2)}, u32[]{:S(2)}) collective-permute-start(bf16[16,2048]{1,0:T(8,128)(2,1)} %get-tuple-element.34), channel_id=1, source_target_pairs={{1,0},{2,1},{3,2},{5,4},{6,5},{7,6},{9,8},{10,9},{11,10},{13,12},{... | collective-permute-start | bytes 196616 | tf_op jit(solution)/shard_map/ppermute | solution.py:824
  10.9 0.1 eq.13
  10.9 0.2 convert_reduce_fusion
  11.1 0.1 reduce_sum.21
  11.2 0.1 add.80
  11.3 0.1 add.81
  11.4 0.1 add.83
  11.5 0.1 add.89
  11.6 0.6 broadcast_add_fusion.target_ref.target_hbm
  12.2 0.1 select_reduce_fusion
  12.3 0.5 broadcast_add_fusion.2.label_ref
  12.8 0.0 collective-permute-done
  12.8 2.2 %collective-permute-done.1 = bf16[16,2048]{1,0:T(8,128)(2,1)S(1)} collective-permute-done((bf16[16,2048]{1,0:T(8,128)(2,1)}, bf16[16,2048]{1,0:T(8,128)(2,1)S(1)}, u32[]{:S(2)}, u32[]{:S(2)}) %collective-permute-start.1) | collective-permute-done | bytes 65568 | tf_op jit(solution)/shard_map/ppermute | solution.py:824
  15.1 0.6 slice_dynamic-update-slice_fusion
  15.7 3.4 %collective-permute-start.2 = (bf16[272,512]{1,0:T(8,128)(2,1)}, bf16[272,512]{1,0:T(8,128)(2,1)S(1)}, u32[]{:S(2)}, u32[]{:S(2)}) collective-permute-start(bf16[272,512]{1,0:T(8,128)(2,1)} %get-tuple-element.56), channel_id=1, source_target_pairs={{0,4},{4,8},{8,12},{12,16},{16,20},{20,24},{24,28},{1,5},{5,9},{9,... | collective-permute-start | bytes 835592 | tf_op jit(solution)/shard_map/ppermute | solution.py:829
  19.1 1.3 %collective-permute-start.3 = (bf16[272,512]{1,0:T(8,128)(2,1)}, bf16[272,512]{1,0:T(8,128)(2,1)S(1)}, u32[]{:S(2)}, u32[]{:S(2)}) collective-permute-start(bf16[272,512]{1,0:T(8,128)(2,1)} %get-tuple-element.55), channel_id=1, source_target_pairs={{4,0},{8,4},{12,8},{16,12},{20,16},{24,20},{28,24},{5,1},{9,5},{13... | collective-permute-start | bytes 835592 | tf_op jit(solution)/shard_map/ppermute | solution.py:830
  20.4 15.1 %inner.1 = (bf16[32,272,128]{2,1,0:T(8,128)(2,1)}, bf16[2176,640]{1,0:T(8,128)(2,1)}, bf16[2176,640]{1,0:T(8,128)(2,1)}, bf16[2048,640]{1,0:T(8,128)(2,1)}, bf16[256,512]{1,0:T(8,128)(2,1)}) custom-call(bf16[2048,512]{1,0:T(8,128)(2,1)} %get-tuple-element.30.xw_ref, bf16[2048,512]{1,0:T(8,128)(2,1)} %get-tuple-element.31.xc_ref, bf16[16,2048]{1,0:T(8,128)(2,1)} %copy-done.1, ...), custom_call_target="tpu_custom_call" | custom-call | flops 6039797760 | bytes 20000000 | tf_op jit(solution)/shard_map/inner/pallas_call | solution.py:339
  35.5 0.0 collective-permute-done.2.up_ref
  35.5 0.0 copy-start.2
  35.5 0.0 collective-permute-done.3.down_ref
  35.6 0.0 copy-start.3
  35.6 0.7 copy-done.2
  36.2 0.1 copy-done.3
  36.3 5.5 %outer.1 = (bf16[32,272,128]{2,1,0:T(8,128)(2,1)}, bf16[2176,640]{1,0:T(8,128)(2,1)}, bf16[2176,640]{1,0:T(8,128)(2,1)}, bf16[2048,640]{1,0:T(8,128)(2,1)}) custom-call(bf16[2048,512]{1,0:T(8,128)(2,1)} %get-tuple-element.30.xw_ref, ...), custom_call_target="tpu_custom_call", output_to_operand_aliasing={{0}: (11, {}), {1}: (12, {}), {2}: (13, {}), {3}: (14, {})} | custom-call | tf_op jit(solution)/shard_map/outer/pallas_call | solution.py:532
  41.8 8.5 %all-to-all-start = ((bf16[32,272,128]{2,1,0:T(8,128)(2,1)}), bf16[32,272,128]{2,1,0:T(8,128)(2,1)}, u32[]{:S(2)}, u32[]{:S(2)}) async-start(bf16[32,272,128]{2,1,0:T(8,128)(2,1)} %get-tuple-element.48), calls=%async_computation | async-start | bytes 4456448 | tf_op jit(solution)/shard_map/all_to_all | solution.py:844
  50.4 12.2 %correlate.1 = f32[584,128]{1,0:T(8,128)} custom-call(bf16[2176,640]{1,0:T(8,128)(2,1)} %get-tuple-element.45.act_in_ref, bf16[2176,640]{1,0:T(8,128)(2,1)} %get-tuple-element.46.act_mid_ref, bf16[2048,640]{1,0:T(8,128)(2,1)} %get-tuple-element.47.g_ref, bf16[2048,512]{1,0:T(8,128)(2,1)} %get-tuple-element.31.xc_ref), custom_call_target="tpu_custom_call" | custom-call | flops 3221225472 | bytes 10000000 | tf_op jit(solution)/shard_map/correlate/pallas_call | solution.py:633
  62.6 0.9 pad_dynamic-slice_fusion
  63.5 0.3 collective-permute-start.4
  63.7 1.2 %collective-permute-done.4 = f32[296,128]{1,0:T(8,128)S(1)} collective-permute-done((f32[296,128]{1,0:T(8,128)S(1)}, f32[296,128]{1,0:T(8,128)S(1)}, u32[]{:S(2)}, u32[]{:S(2)}) %collective-permute-start.4) | collective-permute-done | bytes 151584 | tf_op jit(solution)/shard_map/ppermute | solution.py:781
  64.9 0.9 fusion
  65.9 1.8 %collective-permute-start.5 = (f32[296,128]{1,0:T(8,128)S(1)}, f32[296,128]{1,0:T(8,128)S(1)}, u32[]{:S(2)}, u32[]{:S(2)}) collective-permute-start(f32[296,128]{1,0:T(8,128)S(1)} %fusion), channel_id=1, source_target_pairs={{0,2},{1,3},{2,0},{3,1},{4,6},{5,7},{6,4},{7,5},{8,10},{9,11},{10,... | collective-permute-start | bytes 454664 | tf_op jit(solution)/shard_map/ppermute | solution.py:781
  67.6 5.7 %collective-permute-done.5 = f32[296,128]{1,0:T(8,128)S(1)} collective-permute-done((f32[296,128]{1,0:T(8,128)S(1)}, f32[296,128]{1,0:T(8,128)S(1)}, u32[]{:S(2)}, u32[]{:S(2)}) %collective-permute-start.5) | collective-permute-done | bytes 151584 | tf_op jit(solution)/shard_map/ppermute | solution.py:781
  73.4 5.0 %collective-permute-start.6 = (f32[296,128]{1,0:T(8,128)S(1)}, f32[296,128]{1,0:T(8,128)S(1)}, u32[]{:S(2)}, u32[]{:S(2)}) collective-permute-start(f32[296,128]{1,0:T(8,128)S(1)} %add.95), channel_id=1, source_target_pairs={{0,4},{1,5},{2,6},{3,7},{4,0},{5,1},{6,2},{7,3},{8,12},{9,13},{10,... | collective-permute-start | bytes 454664 | tf_op jit(solution)/shard_map/ppermute | solution.py:781
  78.4 6.3 %collective-permute-done.6 = f32[296,128]{1,0:T(8,128)S(1)} collective-permute-done((f32[296,128]{1,0:T(8,128)S(1)}, f32[296,128]{1,0:T(8,128)S(1)}, u32[]{:S(2)}, u32[]{:S(2)}) %collective-permute-start.6) | collective-permute-done | bytes 151584 | tf_op jit(solution)/shard_map/ppermute | solution.py:781
  84.6 0.1 collective-permute-start.7
  84.7 7.7 %collective-permute-done.7 = f32[296,128]{1,0:T(8,128)S(1)} collective-permute-done((f32[296,128]{1,0:T(8,128)S(1)}, f32[296,128]{1,0:T(8,128)S(1)}, u32[]{:S(2)}, u32[]{:S(2)}) %collective-permute-start.7) | collective-permute-done | bytes 151584 | tf_op jit(solution)/shard_map/ppermute | solution.py:781
  92.4 2.5 %collective-permute-start.8 = (f32[296,128]{1,0:T(8,128)S(1)}, f32[296,128]{1,0:T(8,128)S(1)}, u32[]{:S(2)}, u32[]{:S(2)}) collective-permute-start(f32[296,128]{1,0:T(8,128)S(1)} %add.97), channel_id=1, source_target_pairs={{0,16},{1,17},{2,18},{3,19},{4,20},{5,21},{6,22},{7,23},{8,24},{9,... | collective-permute-start | bytes 454664 | tf_op jit(solution)/shard_map/ppermute | solution.py:781
  94.9 10.7 %all-to-all-done.arrived_ref = bf16[32,272,128]{2,1,0:T(8,128)(2,1)} async-done(((bf16[32,272,128]{2,1,0:T(8,128)(2,1)}), bf16[32,272,128]{2,1,0:T(8,128)(2,1)}, u32[]{:S(2)}, u32[]{:S(2)}) %all-to-all-start) | async-done | bytes 2228256 | tf_op jit(solution)/shard_map/all_to_all | solution.py:844
  105.7 5.8 %unpack.1 = f32[64,2,2,8,512]{4,3,2,1,0:T(8,128)} custom-call(bf16[32,272,128]{2,1,0:T(8,128)(2,1)} %all-to-all-done.arrived_ref), custom_call_target="tpu_custom_call" | custom-call | tf_op jit(solution)/shard_map/unpack/pallas_call | solution.py:721
  111.5 0.0 collective-permute-done.8
  111.6 0.1 collective-permute-start.9
  111.6 1.4 %collective-permute-done.9.other_ref = f32[296,128]{1,0:T(8,128)S(1)} collective-permute-done((f32[296,128]{1,0:T(8,128)S(1)}, f32[296,128]{1,0:T(8,128)S(1)}, u32[]{:S(2)}, u32[]{:S(2)}) %collective-permute-start.9) | collective-permute-done | bytes 151584 | tf_op jit(solution)/shard_map/ppermute | solution.py:781
  113.0 0.7 copy-done.4
  113.7 1.9 %finish.1 = (f32[3,3,64,64]{3,2,1,0:T(8,128)}, f32[3,3,64,64]{3,2,1,0:T(8,128)}, f32[1,64]{1,0:T(1,128)}, f32[1,64]{1,0:T(1,128)}) custom-call(f32[296,128]{1,0:T(8,128)} %copy-done, f32[296,128]{1,0:T(8,128)} %copy-done.4), custom_call_target="tpu_custom_call" | custom-call | tf_op jit(solution)/shard_map/finish/pallas_call | solution.py:766
  (16 shorter events, 0.1 us)
Async XLA Ops:
  0.6 10.2 %copy-start.5 = (s32[2,32]{1,0:T(2,128)S(1)}, s32[2,32]{1,0:T(2,128)}, u32[]{:S(2)}) copy-start(s32[2,32]{1,0:T(2,128)} %param.12) | copy-start | bytes 772
  0.6 10.8 %copy-start.6 = (s32[2,32]{1,0:T(2,128)S(1)}, s32[2,32]{1,0:T(2,128)}, u32[]{:S(2)}) copy-start(s32[2,32]{1,0:T(2,128)} %param.13) | copy-start | bytes 772
  7.2 5.6 %collective-permute-start = (bf16[16,2048]{1,0:T(8,128)(2,1)}, bf16[16,2048]{1,0:T(8,128)(2,1)S(1)}, u32[]{:S(2)}, u32[]{:S(2)}) collective-permute-start(bf16[16,2048]{1,0:T(8,128)(2,1)} %get-tuple-element.33), channel_id=1, source_target_pairs={{0,1},{1,2},{2,3},{4,5},{5,6},{6,7},{8,9},{9,10},{10,11},{12,13},{... | collective-permute-start | bytes 196616 | tf_op jit(solution)/shard_map/ppermute | solution.py:824
  9.5 5.5 %collective-permute-start.1 = (bf16[16,2048]{1,0:T(8,128)(2,1)}, bf16[16,2048]{1,0:T(8,128)(2,1)S(1)}, u32[]{:S(2)}, u32[]{:S(2)}) collective-permute-start(bf16[16,2048]{1,0:T(8,128)(2,1)} %get-tuple-element.34), channel_id=1, source_target_pairs={{1,0},{2,1},{3,2},{5,4},{6,5},{7,6},{9,8},{10,9},{11,10},{13,12},{... | collective-permute-start | bytes 196616 | tf_op jit(solution)/shard_map/ppermute | solution.py:824
  15.1 5.3 %copy-start.1 = (bf16[16,2048]{1,0:T(8,128)(2,1)}, bf16[16,2048]{1,0:T(8,128)(2,1)S(1)}, u32[]{:S(2)}) copy-start(bf16[16,2048]{1,0:T(8,128)(2,1)S(1)} %add.78.side_ref.side_hbm) | copy-start | bytes 196612
  15.7 19.9 %collective-permute-start.2 = (bf16[272,512]{1,0:T(8,128)(2,1)}, bf16[272,512]{1,0:T(8,128)(2,1)S(1)}, u32[]{:S(2)}, u32[]{:S(2)}) collective-permute-start(bf16[272,512]{1,0:T(8,128)(2,1)} %get-tuple-element.56), channel_id=1, source_target_pairs={{0,4},{4,8},{8,12},{12,16},{16,20},{20,24},{24,28},{1,5},{5,9},{9,... | collective-permute-start | bytes 835592 | tf_op jit(solution)/shard_map/ppermute | solution.py:829
  19.1 16.5 %collective-permute-start.3 = (bf16[272,512]{1,0:T(8,128)(2,1)}, bf16[272,512]{1,0:T(8,128)(2,1)S(1)}, u32[]{:S(2)}, u32[]{:S(2)}) collective-permute-start(bf16[272,512]{1,0:T(8,128)(2,1)} %get-tuple-element.55), channel_id=1, source_target_pairs={{4,0},{8,4},{12,8},{16,12},{20,16},{24,20},{28,24},{5,1},{9,5},{13... | collective-permute-start | bytes 835592 | tf_op jit(solution)/shard_map/ppermute | solution.py:830
  35.5 0.7 copy-start.2
  35.6 0.8 copy-start.3
  41.8 63.8 %all-to-all-start = ((bf16[32,272,128]{2,1,0:T(8,128)(2,1)}), bf16[32,272,128]{2,1,0:T(8,128)(2,1)}, u32[]{:S(2)}, u32[]{:S(2)}) async-start(bf16[32,272,128]{2,1,0:T(8,128)(2,1)} %get-tuple-element.48), calls=%async_computation | async-start | bytes 4456448 | tf_op jit(solution)/shard_map/all_to_all | solution.py:844
  63.5 1.4 %collective-permute-start.4 = (f32[296,128]{1,0:T(8,128)S(1)}, f32[296,128]{1,0:T(8,128)S(1)}, u32[]{:S(2)}, u32[]{:S(2)}) collective-permute-start(f32[296,128]{1,0:T(8,128)S(1)} %pad_dynamic-slice_fusion), channel_id=1, source_target_pairs={{0,1},{1,0},{2,3},{3,2},{4,5},{5,4},{6,7},{7,6},{8,9},{9,8},{10,11... | collective-permute-start | bytes 454664 | tf_op jit(solution)/shard_map/ppermute | solution.py:781
  65.9 7.5 %collective-permute-start.5 = (f32[296,128]{1,0:T(8,128)S(1)}, f32[296,128]{1,0:T(8,128)S(1)}, u32[]{:S(2)}, u32[]{:S(2)}) collective-permute-start(f32[296,128]{1,0:T(8,128)S(1)} %fusion), channel_id=1, source_target_pairs={{0,2},{1,3},{2,0},{3,1},{4,6},{5,7},{6,4},{7,5},{8,10},{9,11},{10,... | collective-permute-start | bytes 454664 | tf_op jit(solution)/shard_map/ppermute | solution.py:781
  73.4 11.2 %collective-permute-start.6 = (f32[296,128]{1,0:T(8,128)S(1)}, f32[296,128]{1,0:T(8,128)S(1)}, u32[]{:S(2)}, u32[]{:S(2)}) collective-permute-start(f32[296,128]{1,0:T(8,128)S(1)} %add.95), channel_id=1, source_target_pairs={{0,4},{1,5},{2,6},{3,7},{4,0},{5,1},{6,2},{7,3},{8,12},{9,13},{10,... | collective-permute-start | bytes 454664 | tf_op jit(solution)/shard_map/ppermute | solution.py:781
  84.6 7.7 %collective-permute-start.7 = (f32[296,128]{1,0:T(8,128)S(1)}, f32[296,128]{1,0:T(8,128)S(1)}, u32[]{:S(2)}, u32[]{:S(2)}) collective-permute-start(f32[296,128]{1,0:T(8,128)S(1)} %add.96), channel_id=1, source_target_pairs={{0,8},{1,9},{2,10},{3,11},{4,12},{5,13},{6,14},{7,15},{8,0},{9,1},... | collective-permute-start | bytes 454664 | tf_op jit(solution)/shard_map/ppermute | solution.py:781
  92.4 19.1 %collective-permute-start.8 = (f32[296,128]{1,0:T(8,128)S(1)}, f32[296,128]{1,0:T(8,128)S(1)}, u32[]{:S(2)}, u32[]{:S(2)}) collective-permute-start(f32[296,128]{1,0:T(8,128)S(1)} %add.97), channel_id=1, source_target_pairs={{0,16},{1,17},{2,18},{3,19},{4,20},{5,21},{6,22},{7,23},{8,24},{9,... | collective-permute-start | bytes 454664 | tf_op jit(solution)/shard_map/ppermute | solution.py:781
  111.5 1.5 %copy-start = (f32[296,128]{1,0:T(8,128)}, f32[296,128]{1,0:T(8,128)S(1)}, u32[]{:S(2)}) copy-start(f32[296,128]{1,0:T(8,128)S(1)} %add.98.total_ref) | copy-start | bytes 454660
  111.6 1.4 %collective-permute-start.9 = (f32[296,128]{1,0:T(8,128)S(1)}, f32[296,128]{1,0:T(8,128)S(1)}, u32[]{:S(2)}, u32[]{:S(2)}) collective-permute-start(f32[296,128]{1,0:T(8,128)S(1)} %add.98.total_ref), channel_id=1, source_target_pairs={{0,1},{1,0},{2,3},{3,2},{4,5},{5,4},{6,7},{7,6},{8,9},{9,8},{10,11... | collective-permute-start | bytes 454664 | tf_op jit(solution)/shard_map/ppermute | solution.py:781
  113.0 0.7 copy-start.4
